TPU v7x, 32 devices: a whole 2x2x4 slice. The times are simulated.
32 devices in a mesh: parts: 2 (over y), node: 4 (over z), local: 4 (over x, core).
Axes of the slice: x: 2, y: 2, z: 4, core: 2. Of those that a mesh axis runs over, the one named last changes fastest.
Arguments:
- tokens: bfloat16 [2048, 3584], P(('parts', 'node', 'local')), parts along dimension 0, may hold values from -6 to 6
- expert_ids: int32 [2048, 8], P(('parts', 'node', 'local')), parts along dimension 0, may hold values from 0 to 7, as said below
- gate_scores: bfloat16 [2048, 8], P(('parts', 'node', 'local')), parts along dimension 0, may hold values from 0.19921875 to 1
- gate_weight: bfloat16 [16, 3584, 512], P(('node', 'local')), may hold values from -0.09375 to 0.09375
- up_weight: bfloat16 [16, 3584, 512], P(('node', 'local')), may hold values from -0.09375 to 0.09375
- down_weight: bfloat16 [16, 512, 3584], P(('node', 'local')), may hold values from -0.1875 to 0.1875
Outputs:
- combined: bfloat16 [2048, 3584], P(('parts', 'node', 'local')), parts along dimension 0
There are 2 independent parts, one for each index of `parts`. A program takes and returns all parts, laid end to end along the dimension named above; an argument that names none is the same for every part. Nothing has to cross between parts.
Inputs may be any that keep to these rules, and one draw needn't show every extreme that they name: `expert_ids`: each token names 8 different experts, two from each of exactly 4 groups, in any order. Among the 64 tokens of one device each group is named by exactly 64 tokens and no expert by more than 64. In every group one expert, the same on every device of a part, is named by exactly 64 tokens of every device.
All inputs are finite; a program needn't handle non-finite values.
Results may differ from a plain program's by a relative error of at most 0.0072.
Values may be sent and summed in bfloat16 or wider, within the bound.
No kernel may reach another device: no remote copies, remote signals or barrier semaphores. Data moves between devices by JAX's collectives and lax.ppermute only.
A program may use at most 128 MiB of HBM per device.

v0:
```python
import jax
import jax.numpy as jnp
from jax import lax
from jax.sharding import PartitionSpec as P

TOPG = 4


def partner(value, axis, bit):
    mask = 2**bit
    pairs = [(source, source ^ mask) for source in range(lax.axis_size(axis))]
    return lax.ppermute(value, axis, pairs)


def expert_apply(arrived, gate_weight, up_weight, down_weight):
    layout = arrived.shape
    flat_rows = arrived.reshape(-1, layout[-1])
    gate_act = jnp.dot(flat_rows, gate_weight[0], preferred_element_type=jnp.float32)
    up_act = jnp.dot(flat_rows, up_weight[0], preferred_element_type=jnp.float32)
    hidden = (jax.nn.silu(gate_act) * up_act).astype(jnp.bfloat16)
    result = jnp.dot(hidden, down_weight[0], preferred_element_type=jnp.float32).astype(
        jnp.bfloat16
    )
    return result.reshape(layout)


def body(tokens, expert_ids, gate_scores, gate_weight, up_weight, down_weight):
    rows_dev, model_width = tokens.shape
    node_count = lax.axis_size("node")
    local_count = lax.axis_size("local")
    per_group = local_count // 2
    chooser_cap = rows_dev * TOPG // node_count
    bound_most = min(chooser_cap, 3 * chooser_cap // per_group)
    group_ids = jnp.arange(node_count)
    owner_group = expert_ids // per_group
    chosen = jnp.any(owner_group[:, :, None] == group_ids[None, None, :], axis=1)
    chosen_int = chosen.astype(jnp.int32)
    before = jnp.cumsum(chosen_int, axis=0) - chosen_int
    select_one = chosen.T[:, None, :] & (
        before.T[:, None, :] == jnp.arange(chooser_cap)[None, :, None]
    )
    one_hot = select_one.astype(jnp.bfloat16)
    send_rows = jnp.einsum(
        "gsb,bd->gsd", one_hot, tokens, preferred_element_type=jnp.float32
    ).astype(jnp.bfloat16)
    token_at = jnp.sum(jnp.where(select_one, jnp.arange(rows_dev)[None, None, :], 0), axis=-1)
    occupied = jnp.any(select_one, axis=-1)
    inside = (owner_group[token_at] == group_ids[:, None, None]) & occupied[:, :, None]
    send_ids = jnp.where(inside, expert_ids[token_at] % per_group, -1)
    send_scores = jnp.where(inside, gate_scores[token_at], 0)
    arrived_rows, arrived_ids, arrived_scores = (
        lax.all_to_all(send_rows, "node", split_axis=0, concat_axis=0, tiled=True),
        lax.all_to_all(send_ids, "node", split_axis=0, concat_axis=0, tiled=True),
        lax.all_to_all(send_scores, "node", split_axis=0, concat_axis=0, tiled=True),
    )
    relayed = node_count * chooser_cap
    relay_rows = arrived_rows.reshape(relayed, model_width)
    relay_ids = arrived_ids.reshape(relayed, -1)
    relay_scores = arrived_scores.reshape(relayed, -1).astype(jnp.float32)
    member_ids = jnp.arange(per_group)
    matches = relay_ids[:, :, None] == member_ids[None, None, :]
    naming = jnp.any(matches, axis=1)
    naming_int = naming.astype(jnp.int32)
    ahead_count = jnp.cumsum(naming_int, axis=0) - naming_int
    group_cap = node_count * bound_most
    half_cap = group_cap // 2
    select_two = naming.T[:, None, :] & (
        ahead_count.T[:, None, :] == jnp.arange(group_cap)[None, :, None]
    )
    expert_rows = jnp.einsum(
        "jsr,rd->jsd",
        select_two.astype(jnp.bfloat16),
        relay_rows,
        preferred_element_type=jnp.float32,
    ).astype(jnp.bfloat16)
    outbound = expert_rows.reshape(local_count, half_cap, model_width)
    arrived = lax.all_to_all(outbound, "local", split_axis=0, concat_axis=0, tiled=True)
    partner_rows = partner(arrived, "local", 0)
    stacked = jnp.concatenate([arrived, partner_rows], axis=0)
    outputs = expert_apply(stacked, gate_weight, up_weight, down_weight)
    count = arrived.shape[0]
    mine = outputs[:count]
    theirs = outputs[count:]
    back = partner(theirs, "local", 0)
    partials = (mine.astype(jnp.float32) + back.astype(jnp.float32)).astype(jnp.bfloat16)
    returned = lax.all_to_all(partials, "local", split_axis=0, concat_axis=0, tiled=True)
    relay_weight = jnp.sum(jnp.where(matches, relay_scores[:, :, None], 0.0), axis=1)
    weighted = (jnp.transpose(select_two, (2, 0, 1)) * relay_weight[:, :, None]).astype(
        jnp.bfloat16
    )
    expert_output = returned.reshape(per_group, group_cap, model_width)
    group_sum = jnp.einsum(
        "rjs,jsd->rd", weighted, expert_output, preferred_element_type=jnp.float32
    ).astype(jnp.bfloat16)
    gathered_back = lax.all_to_all(
        group_sum.reshape(node_count, chooser_cap, model_width),
        "node",
        split_axis=0,
        concat_axis=0,
        tiled=True,
    )
    combined = jnp.einsum("gsb,gsd->bd", one_hot, gathered_back, preferred_element_type=jnp.float32)
    return combined.astype(jnp.bfloat16)


def solution(mesh):
    in_specs = (
        P(("parts", "node", "local"), None),
        P(("parts", "node", "local"), None),
        P(("parts", "node", "local"), None),
        P(("node", "local"), None, None),
        P(("node", "local"), None, None),
        P(("node", "local"), None, None),
    )
    out_specs = P(("parts", "node", "local"), None)
    return jax.shard_map(body, mesh=mesh, in_specs=in_specs, out_specs=out_specs, check_vma=False)
```

profile of v0, /device:TPU:0, one launch (start us, length us, event | category | flops | bytes accessed | tf_op | source)
XLA Modules:
  0.0 261.5 jit_solution(5087318036236903690)
XLA Ops:
  0.0 0.8 copy.76
  0.9 0.1 copy.80
  1.0 0.1 copy.81
  1.1 0.1 reduce_window_sum.28
  1.1 0.1 copy.82
  1.2 0.2 fusion.26
  1.4 0.2 select_reduce_fusion
  1.6 0.1 reshape.70
  1.7 0.7 gather_fusion.1
  2.4 0.7 gather_fusion
  3.1 0.8 copy.89
  3.9 0.9 gather_fusion.2
  4.7 0.1 copy.90
  4.8 0.1 copy.85
  4.9 0.1 copy.83
  5.0 0.7 reshape.102
  5.7 6.3 %all-to-all-start = ((s32[4,1,512]{2,1,0:T(1,128)}), s32[4,1,512]{2,1,0:T(1,128)S(1)}, u32[]{:S(2)}, u32[]{:S(2)}) async-start(s32[4,1,512]{2,1,0:T(1,128)} %reshape.102), calls=%async_computation | async-start | bytes 16384 | tf_op jit(solution)/shard_map/all_to_all | solution.py:53
  12.0 2.0 convolution_convert_fusion.2
  14.1 3.6 %all-to-all-done = s32[4,1,512]{2,1,0:T(1,128)S(1)} async-done(((s32[4,1,512]{2,1,0:T(1,128)}), s32[4,1,512]{2,1,0:T(1,128)S(1)}, u32[]{:S(2)}, u32[]{:S(2)}) %all-to-all-start) | async-done | bytes 8224 | tf_op jit(solution)/shard_map/all_to_all | solution.py:53
  17.6 3.6 %all-to-all-start.2 = ((bf16[4,64,3584]{2,1,0:T(8,128)(2,1)}), bf16[4,64,3584]{2,1,0:T(8,128)(2,1)S(1)}, u32[]{:S(2)}, u32[]{:S(2)}) async-start(bf16[4,64,3584]{2,1,0:T(8,128)(2,1)} %convolution_convert_fusion.2), calls=%async_computation.2 | async-start | bytes 3670016 | tf_op jit(solution)/shard_map/all_to_all | solution.py:52
  21.2 0.5 broadcast.76
  21.7 0.7 reduce.2
  22.4 0.1 reshape.103
  22.5 0.1 eq.81
  22.6 0.6 reduce-window.6
  23.2 0.2 slice_reduce_fusion
  23.5 0.2 reduce-window.9
  23.6 0.1 add_bitcast_fusion
  23.7 38.9 %all-to-all-done.2 = bf16[4,64,3584]{2,1,0:T(8,128)(2,1)S(1)} async-done(((bf16[4,64,3584]{2,1,0:T(8,128)(2,1)}), bf16[4,64,3584]{2,1,0:T(8,128)(2,1)S(1)}, u32[]{:S(2)}, u32[]{:S(2)}) %all-to-all-start.2) | async-done | bytes 1835040 | tf_op jit(solution)/shard_map/all_to_all | solution.py:52
  62.6 1.1 convolution_convert_fusion.1
  63.7 45.1 %all_to_all.30 = bf16[4,128,3584]{2,1,0:T(8,128)(2,1)S(1)} all-to-all(bf16[4,128,3584]{2,1,0:T(8,128)(2,1)S(1)} %bitcast.68), channel_id=1, replica_groups=mesh['parts'=2,'node'=4,'local'=4] {'local'}, dimensions={0} | all-to-all | bytes 7340032 | tf_op jit(solution)/shard_map/all_to_all | solution.py:77
  108.8 6.5 %collective-permute-done = bf16[4,128,3584]{2,1,0:T(8,128)(2,1)} collective-permute-done((bf16[4,128,3584]{2,1,0:T(8,128)(2,1)S(1)}, bf16[4,128,3584]{2,1,0:T(8,128)(2,1)}, u32[]{:S(2)}, u32[]{:S(2)}) %collective-permute-start) | collective-permute-done | bytes 3670048 | tf_op jit(solution)/shard_map/ppermute | solution.py:12
  115.4 5.7 %pad_maximum_fusion = bf16[8,128,3584]{2,1,0:T(8,128)(2,1)} fusion(bf16[4,128,3584]{2,1,0:T(8,128)(2,1)} %collective-permute-done, bf16[4,128,3584]{2,1,0:T(8,128)(2,1)S(1)} %all_to_all.30), kind=kLoop, calls=%fused_computation.4 | loop fusion | flops 3670016 | bytes 14680064 | tf_op jit(solution)/shard_map/concatenate | solution.py:79
  121.1 9.4 %fusion.4 = f32[1024,512]{1,0:T(8,128)} fusion(bf16[1024,3584]{1,0:T(8,128)(2,1)} %bitcast.70, bf16[1,3584,512]{2,1,0:T(8,128)(2,1)} %param.10), kind=kOutput, calls=%fused_computation.14 | convolution fusion | flops 3758096384 | bytes 13107200 | tf_op jit(solution)/shard_map/dot_general | solution.py:19
  130.5 14.6 %convolution_convert_fusion = bf16[1024,3584]{1,0:T(8,128)(2,1)} fusion(bf16[1,512,3584]{2,1,0:T(8,128)(2,1)} %param.11, f32[1024,512]{1,0:T(8,128)} %fusion.4, bf16[1024,3584]{1,0:T(8,128)(2,1)} %bitcast.71, bf16[1,3584,512]{2,1,0:T(8,128)(2,1)} %param.9), kind=kOutput, calls=%fused_computation.3 | convolution fusion | flops 7523008512 | bytes 24117248 | tf_op jit(solution)/shard_map/dot_general | solution.py:21
  145.1 6.6 %fusion.41 = (bf16[512,3584]{1,0:T(8,128)(2,1)}, bf16[512,3584]{1,0:T(8,128)(2,1)}) fusion(bf16[1024,3584]{1,0:T(8,128)(2,1)} %convolution_convert_fusion), kind=kLoop, calls=%fused_computation.69 | loop fusion | bytes 14680064 | tf_op jit(solution)/shard_map/slice | solution.py:83
  151.7 0.1 collective-permute-start.1
  151.8 0.7 reshape.100
  152.5 3.2 %all-to-all-start.1 = ((bf16[4,2,256]{2,1,0:T(2,128)(2,1)}), bf16[4,2,256]{2,1,0:T(2,128)(2,1)S(1)}, u32[]{:S(2)}, u32[]{:S(2)}) async-start(bf16[4,2,256]{2,1,0:T(2,128)(2,1)} %reshape.100), calls=%async_computation.1 | async-start | bytes 8192 | tf_op jit(solution)/shard_map/all_to_all | solution.py:54
  155.8 2.7 %collective-permute-done.1 = bf16[4,128,3584]{2,1,0:T(8,128)(2,1)} collective-permute-done((bf16[4,128,3584]{2,1,0:T(8,128)(2,1)}, bf16[4,128,3584]{2,1,0:T(8,128)(2,1)}, u32[]{:S(2)}, u32[]{:S(2)}) %collective-permute-start.1) | collective-permute-done | bytes 3670048 | tf_op jit(solution)/shard_map/ppermute | solution.py:12
  158.5 5.9 %fusion = bf16[4,128,3584]{2,1,0:T(8,128)(2,1)} fusion(bf16[4,128,3584]{2,1,0:T(8,128)(2,1)} %bitcast.69, bf16[4,128,3584]{2,1,0:T(8,128)(2,1)} %collective-permute-done.1), kind=kLoop, calls=%fused_computation.6 | loop fusion | flops 7340032 | bytes 11010048 | tf_op jit(solution)/shard_map/convert_element_type | solution.py:85
  164.3 4.7 %all-to-all-start.4 = ((bf16[4,128,3584]{2,1,0:T(8,128)(2,1)}), bf16[4,128,3584]{2,1,0:T(8,128)(2,1)}, u32[]{:S(2)}, u32[]{:S(2)}) async-start(bf16[4,128,3584]{2,1,0:T(8,128)(2,1)} %fusion), calls=%async_computation.4 | async-start | bytes 7340032 | tf_op jit(solution)/shard_map/all_to_all | solution.py:86
  169.1 0.1 reshape.101
  169.2 0.1 reshape.66
  169.3 42.4 %all-to-all-done.4 = bf16[4,128,3584]{2,1,0:T(8,128)(2,1)} async-done(((bf16[4,128,3584]{2,1,0:T(8,128)(2,1)}), bf16[4,128,3584]{2,1,0:T(8,128)(2,1)}, u32[]{:S(2)}, u32[]{:S(2)}) %all-to-all-start.4) | async-done | bytes 3670048 | tf_op jit(solution)/shard_map/all_to_all | solution.py:86
  211.7 3.3 %fusion.1 = bf16[256,3584]{1,0:T(8,128)(2,1)S(1)} fusion(bf16[2,256,3584]{2,1,0:T(8,128)(2,1)} %bitcast.18, bf16[256,2]{0,1:T(2,128)(2,1)S(1)} %select_reduce_fusion.1, s32[256,2]{0,1:T(2,128)S(1)} %bitcast.85, pred[256,2]{0,1:T(4,128)(4,1)S(1)} %fusion.35), kind=kOutput, calls=%fused_computation.9 | convolution fusion | flops 940834816 | bytes 5508608 | tf_op jit(solution)/shard_map/rjs,jsd->rd/dot_general | solution.py:92
  215.0 45.2 %all_to_all.31 = bf16[4,64,3584]{2,1,0:T(8,128)(2,1)S(1)} all-to-all(bf16[4,64,3584]{2,1,0:T(8,128)(2,1)S(1)} %bitcast.73), channel_id=1, replica_groups=mesh['parts'=2,'node'=4,'local'=4] {'node'}, dimensions={0} | all-to-all | bytes 3670016 | tf_op jit(solution)/shard_map/all_to_all | solution.py:95
  260.2 1.3 fusion.2
  (19 shorter events, 0.2 us)
Async XLA Ops:
  0.0 12.0 %copy-start = (bf16[64,3584]{1,0:T(8,128)(2,1)S(1)}, bf16[64,3584]{1,0:T(8,128)(2,1)}, u32[]{:S(2)}) copy-start(bf16[64,3584]{1,0:T(8,128)(2,1)} %param.6) | copy-start | bytes 1376260
  5.7 11.9 %all-to-all-start = ((s32[4,1,512]{2,1,0:T(1,128)}), s32[4,1,512]{2,1,0:T(1,128)S(1)}, u32[]{:S(2)}, u32[]{:S(2)}) async-start(s32[4,1,512]{2,1,0:T(1,128)} %reshape.102), calls=%async_computation | async-start | bytes 16384 | tf_op jit(solution)/shard_map/all_to_all | solution.py:53
  17.6 45.0 %all-to-all-start.2 = ((bf16[4,64,3584]{2,1,0:T(8,128)(2,1)}), bf16[4,64,3584]{2,1,0:T(8,128)(2,1)S(1)}, u32[]{:S(2)}, u32[]{:S(2)}) async-start(bf16[4,64,3584]{2,1,0:T(8,128)(2,1)} %convolution_convert_fusion.2), calls=%async_computation.2 | async-start | bytes 3670016 | tf_op jit(solution)/shard_map/all_to_all | solution.py:52
  108.8 6.5 %collective-permute-start = (bf16[4,128,3584]{2,1,0:T(8,128)(2,1)S(1)}, bf16[4,128,3584]{2,1,0:T(8,128)(2,1)}, u32[]{:S(2)}, u32[]{:S(2)}) collective-permute-start(bf16[4,128,3584]{2,1,0:T(8,128)(2,1)S(1)} %all_to_all.30), channel_id=1, source_target_pairs={{0,1},{1,0},{2,3},{3,2},{4,5},{5,4},{6,7},{7,6},{8,9},{9,8},{10,11... | collective-permute-start | bytes 11010056 | tf_op jit(solution)/shard_map/ppermute | solution.py:12
  151.7 6.8 %collective-permute-start.1 = (bf16[4,128,3584]{2,1,0:T(8,128)(2,1)}, bf16[4,128,3584]{2,1,0:T(8,128)(2,1)}, u32[]{:S(2)}, u32[]{:S(2)}) collective-permute-start(bf16[4,128,3584]{2,1,0:T(8,128)(2,1)} %bitcast.17), channel_id=1, source_target_pairs={{0,1},{1,0},{2,3},{3,2},{4,5},{5,4},{6,7},{7,6},{8,9},{9,8},{10,11... | collective-permute-start | bytes 11010056 | tf_op jit(solution)/shard_map/ppermute | solution.py:12
  152.5 11.8 %all-to-all-start.1 = ((bf16[4,2,256]{2,1,0:T(2,128)(2,1)}), bf16[4,2,256]{2,1,0:T(2,128)(2,1)S(1)}, u32[]{:S(2)}, u32[]{:S(2)}) async-start(bf16[4,2,256]{2,1,0:T(2,128)(2,1)} %reshape.100), calls=%async_computation.1 | async-start | bytes 8192 | tf_op jit(solution)/shard_map/all_to_all | solution.py:54
  164.3 47.4 %all-to-all-start.4 = ((bf16[4,128,3584]{2,1,0:T(8,128)(2,1)}), bf16[4,128,3584]{2,1,0:T(8,128)(2,1)}, u32[]{:S(2)}, u32[]{:S(2)}) async-start(bf16[4,128,3584]{2,1,0:T(8,128)(2,1)} %fusion), calls=%async_computation.4 | async-start | bytes 7340032 | tf_op jit(solution)/shard_map/all_to_all | solution.py:86
where the time goes:
time: 262 us; the launch traced here: 261 us
  waiting for transfers between devices  94.1 us (36%)
  blocking collectives  90.3 us (34%)
  matrix products  31.7 us (12%)
  starting transfers between devices  18 us (7%)
  other arithmetic  13.7 us (5%)
  local copies, waits for them, and re-layouts  13.5 us (5%)
    all_to_all x1, blocking collectives, body(): lax.all_to_all(group_sum.reshape(node_count, chooser_cap, model_width), '...  45.2 us
    all_to_all x1, blocking collectives, body(): lax.all_to_all(outbound, 'local', split_axis=0, concat_axis=0, tiled=True)  45.1 us
    all_to_all x1, waiting for transfers between devices, body(): lax.all_to_all(partials, 'local', split_axis=0, concat_axis=0, tiled=True)  42.4 us
    all_to_all x1, waiting for transfers between devices, body(): lax.all_to_all(send_rows, 'node', split_axis=0, concat_axis=0, tiled=True)  38.9 us
    dot_general x1, matrix products, expert_apply(): jnp.dot(hidden, down_weight[0], preferred_element_type=jnp.float32)  14.6 us
    dot_general x1, matrix products, expert_apply(): jnp.dot(flat_rows, up_weight[0], preferred_element_type=jnp.float32)  9.4 us
    ppermute x2, waiting for transfers between devices, partner(): return lax.ppermute(value, axis, pairs)  9.23 us
    slice x1, local copies, waits for them, and re-layouts, body(): theirs = outputs[count:]  6.63 us
  transfers between devices with their start and end apart: 6, of which 5 were waited for; matrix products, arithmetic and copies ran while one was open for 4% of the time, Pallas kernels for 0%

commit v1 on v0

--- a/solution.py
+++ b/solution.py
@@ -1,6 +1,10 @@
+import functools
+
 import jax
 import jax.numpy as jnp
 from jax import lax
+from jax.experimental import pallas as pl
+from jax.experimental.pallas import tpu as pltpu
 from jax.sharding import PartitionSpec as P
 
 TOPG = 4
@@ -24,7 +28,7 @@
     return result.reshape(layout)
 
 
-def body(tokens, expert_ids, gate_scores, gate_weight, up_weight, down_weight):
+def routed(tokens, expert_ids, gate_scores, gate_weight, up_weight, down_weight):
     rows_dev, model_width = tokens.shape
     node_count = lax.axis_size("node")
     local_count = lax.axis_size("local")
@@ -102,6 +106,152 @@
     combined = jnp.einsum("gsb,gsd->bd", one_hot, gathered_back, preferred_element_type=jnp.float32)
     return combined.astype(jnp.bfloat16)
 
+def expert_kernel(count, down_tiles, hidden_tile, *refs):
+    blocks, scores, weights = refs[:count], refs[count], refs[count + 1 : count + 7]
+    outs = refs[count + 7 : 2 * count + 7]
+    rows_all, gate, up, down, hidden, sems = refs[2 * count + 7 :]
+    rows, width = blocks[0].shape
+    half = gate.shape[-1]
+    started = []
+
+    def fetch(source, target):
+        copy = pltpu.make_async_copy(source, target, sems.at[len(started)])
+        copy.start()
+        started.append(copy)
+        return copy
+
+    first, second = [], []
+    for side in range(2):
+        gate_hbm, up_hbm, _ = weights[3 * side : 3 * side + 3]
+        for start in range(0, half, hidden_tile):
+            cols = pl.ds(start, hidden_tile)
+            pair = (
+                fetch(gate_hbm.at[0, :, cols], gate.at[side, :, cols]),
+                fetch(up_hbm.at[0, :, cols], up.at[side, :, cols]),
+            )
+            first.append((side, cols, pair))
+    step = width // down_tiles
+    for start in range(0, width, step):
+        cols = pl.ds(start, step)
+        pair = tuple(
+            fetch(weights[3 * side + 2].at[0, :, cols], down.at[side, :, cols]) for side in range(2)
+        )
+        second.append((cols, pair))
+    for i in range(count):
+        rows_all[pl.ds(i * rows, rows), :] = blocks[i][...]
+    for side, cols, pair in first:
+        for copy in pair:
+            copy.wait()
+        gate_act = jnp.dot(rows_all[...], gate[side, :, cols], preferred_element_type=jnp.float32)
+        up_act = jnp.dot(rows_all[...], up[side, :, cols], preferred_element_type=jnp.float32)
+        hidden[side, :, cols] = (jax.nn.silu(gate_act) * up_act).astype(jnp.bfloat16)
+    for cols, pair in second:
+        for copy in pair:
+            copy.wait()
+        result = jnp.dot(hidden[0], down[0, :, cols], preferred_element_type=jnp.float32)
+        result += jnp.dot(hidden[1], down[1, :, cols], preferred_element_type=jnp.float32)
+        result = (result * scores[...]).astype(jnp.bfloat16)
+        for i in range(count):
+            outs[i][:, cols] = result[i * rows : (i + 1) * rows]
+
+
+def expert_rows(blocks, scores, own, other):
+    count = len(blocks)
+    rows, width = blocks[0].shape
+    half = own[0].shape[-1]
+    total = count * rows
+    down_tiles = 4
+    hidden_tile = half // 2
+    vmem = pl.BlockSpec(memory_space=pltpu.VMEM)
+    anywhere = pl.BlockSpec(memory_space=pl.ANY)
+    return pl.pallas_call(
+        functools.partial(expert_kernel, count, down_tiles, hidden_tile),
+        out_shape=[jax.ShapeDtypeStruct((rows, width), jnp.bfloat16)] * count,
+        in_specs=[vmem] * (count + 1) + [anywhere] * 6,
+        out_specs=[vmem] * count,
+        scratch_shapes=[
+            pltpu.VMEM((total, width), jnp.bfloat16),
+            pltpu.VMEM((2, width, half), jnp.bfloat16),
+            pltpu.VMEM((2, width, half), jnp.bfloat16),
+            pltpu.VMEM((2, half, width), jnp.bfloat16),
+            pltpu.VMEM((2, total, half), jnp.bfloat16),
+            pltpu.SemaphoreType.DMA((4 * (half // hidden_tile) + 2 * down_tiles,)),
+        ],
+        compiler_params=pltpu.CompilerParams(vmem_limit_bytes=48 * 2**20),
+        cost_estimate=pl.CostEstimate(
+            flops=12 * total * width * half,
+            bytes_accessed=12 * width * half + 4 * total * width,
+            transcendentals=2 * total * half,
+        ),
+    )(*blocks, jnp.concatenate(scores, axis=0), *own, *other)
+
+
+def added(*terms):
+    return sum(term.astype(jnp.float32) for term in terms).astype(jnp.bfloat16)
+
+
+def dense(tokens, expert_ids, gate_scores, gate_weight, up_weight, down_weight):
+    node_count = lax.axis_size("node")
+    local_count = lax.axis_size("local")
+    node, local = lax.axis_index("node"), lax.axis_index("local")
+
+    def next_node(value):
+        pairs = [(source, (source + 1) % node_count) for source in range(node_count)]
+        return lax.ppermute(value, "node", pairs)
+
+    own = (gate_weight, up_weight, down_weight)
+    other = tuple(partner(weight, "local", 0) for weight in own)
+
+    experts = jnp.arange(node_count * (local_count // 2))
+    named = expert_ids[:, :, None] == experts[None, None, :]
+    factors = jnp.sum(jnp.where(named, gate_scores[:, :, None], 0), axis=1).astype(jnp.bfloat16)
+    factors = lax.all_gather(factors, ("node", "local"))
+    mine = node * (local_count // 2) + local // 2
+    factors = lax.dynamic_index_in_dim(factors, mine, 2, keepdims=True).astype(jnp.float32)
+
+    def factor_of(slot, here):
+        source = lax.rem(node - slot + node_count, node_count) * local_count
+        source += local if here else local ^ 2
+        return lax.dynamic_index_in_dim(factors, source, 0, keepdims=False)
+
+    along, across = [tokens], []
+    for slot in range(node_count):
+        across.append(partner(along[slot], "local", 1))
+        if slot < node_count - 1:
+            along.append(next_node(along[slot]))
+
+    order = [("a", 0)]
+    for slot in range(1, node_count):
+        order += [("a", slot), ("x", slot - 1)]
+    order.append(("x", node_count - 1))
+    sizes = [3] + [2] * (node_count - 2) + [1]
+    done = {}
+    at = 0
+    for size in sizes:
+        keys = order[at : at + size]
+        at += size
+        blocks = [(along if kind == "a" else across)[slot] for kind, slot in keys]
+        scores = [factor_of(slot, kind == "a") for kind, slot in keys]
+        results = expert_rows(blocks, scores, own, other)
+        done.update(zip(keys, results))
+
+    running = None
+    for slot in list(range(1, node_count)) + [0]:
+        terms = [done["a", slot], partner(done["x", slot], "local", 1)]
+        if running is not None:
+            terms.append(running)
+        running = added(*terms)
+        if slot:
+            running = next_node(running)
+    return running
+
+
+def body(tokens, expert_ids, gate_scores, gate_weight, up_weight, down_weight):
+    per_group = lax.axis_size("local") // 2
+    names_all = expert_ids.shape[1] == lax.axis_size("node") * per_group
+    layer = dense if names_all and per_group == 2 else routed
+    return layer(tokens, expert_ids, gate_scores, gate_weight, up_weight, down_weight)
+
 
 def solution(mesh):
     in_specs = (

time: 262 us -> 128 us (0.49)
  blocking collectives: 90.3 us -> 24.8 us
  waiting for transfers between devices: 94.1 us -> 52.9 us
  matrix products: 31.7 us -> 0 us
  Pallas kernels: 0 us -> 30.7 us
  other arithmetic: 13.7 us -> 4.24 us
  local copies, waits for them, and re-layouts: 13.5 us -> 4.55 us
  starting transfers between devices: 18 us -> 10.3 us
    all_to_all x2 -> x0, blocking collectives: 90.3 us -> none  [the longest x1 45.2 us: body(): lax.all_to_all(group_sum.reshape(node_count, chooser_cap, model_width), '...]
    all_to_all x4 -> x0, waiting for transfers between devices: 84.9 us -> none  [the longest x1 42.4 us: body(): lax.all_to_all(partials, 'local', split_axis=0, concat_axis=0, tiled=True)]
    ppermute x0 -> x6, waiting for transfers between devices: none -> 35.1 us  [next_node(): return lax.ppermute(value, 'node', pairs)]
    dot_general x6 -> x0, matrix products: 31.7 us -> none  [the longest x1 14.6 us: expert_apply(): jnp.dot(hidden, down_weight[0], preferred_element_type=jnp.float32)]
    pallas_call x0 -> x4, Pallas kernels: none -> 30.7 us  [expert_rows(): pl.pallas_call(functools.partial(expert_kernel, count, down_tiles, hidden...]
    all_gather x0 -> x1, blocking collectives: none -> 24.8 us  [dense(): factors = lax.all_gather(factors, ('node', 'local'))]
    all_to_all x4 -> x0, starting transfers between devices: 17.9 us -> none  [the longest x1 6.32 us: body(): lax.all_to_all(send_ids, 'node', split_axis=0, concat_axis=0, tiled=True)]
    ppermute x2 -> x11, waiting for transfers between devices: 9.23 us -> 17.8 us  [partner(): return lax.ppermute(value, axis, pairs)]
  transfers between devices with their start and end apart: 6 -> 17, of which waited for: 5 -> 8; matrix products, arithmetic and copies ran while one was open for 4% -> 3% of each run, Pallas kernels for 0% -> 24%
where the time goes in v1:
time: 128 us
  waiting for transfers between devices  52.9 us (41%)
  Pallas kernels  30.7 us (24%)
  blocking collectives  24.8 us (19%)
  starting transfers between devices  10.3 us (8%)
  local copies, waits for them, and re-layouts  4.55 us (4%)
  other arithmetic  4.24 us (3%)
    ppermute x6, waiting for transfers between devices, next_node(): return lax.ppermute(value, 'node', pairs)  35.1 us
    pallas_call x4, Pallas kernels, expert_rows(): pl.pallas_call(functools.partial(expert_kernel, count, down_tiles, hidden...  30.7 us
    all_gather x1, blocking collectives, dense(): factors = lax.all_gather(factors, ('node', 'local'))  24.8 us
    ppermute x11, waiting for transfers between devices, partner(): return lax.ppermute(value, axis, pairs)  17.8 us
    ppermute x11, starting transfers between devices, partner(): return lax.ppermute(value, axis, pairs)  7.63 us
    unnamed x8, local copies, waits for them, and re-layouts  4.08 us
    convert_element_type x4, other arithmetic, added(): sum((term.astype(jnp.float32) for term in terms)).astype(jnp.bfloat16)  3.3 us
    ppermute x6, starting transfers between devices, next_node(): return lax.ppermute(value, 'node', pairs)  2.7 us
  transfers between devices with their start and end apart: 17, of which 8 were waited for; matrix products, arithmetic and copies ran while one was open for 3% of the time, Pallas kernels for 24%

profile of v1, /device:TPU:0, one launch (start us, length us, event | category | flops | bytes accessed | tf_op | source)
XLA Modules:
  0.0 127.7 jit_solution(17659379383447454733)
XLA Ops:
  0.0 0.5 collective-permute-start.2
  0.5 0.1 collective-permute-start.3
  0.5 0.5 collective-permute-start.4
  1.0 2.6 %collective-permute-start = (bf16[64,3584]{1,0:T(8,128)(2,1)}, bf16[64,3584]{1,0:T(8,128)(2,1)S(1)}, u32[]{:S(2)}, u32[]{:S(2)}) collective-permute-start(bf16[64,3584]{1,0:T(8,128)(2,1)} %refs_0_.1), channel_id=1, source_target_pairs={{0,4},{4,8},{8,12},{12,0},{1,5},{5,9},{9,13},{13,1},{2,6},{6,10},{... | collective-permute-start | bytes 1376264 | tf_op jit(solution)/shard_map/ppermute | solution.py:200
  3.5 13.4 %collective-permute-done.refs_1_ = bf16[64,3584]{1,0:T(8,128)(2,1)S(1)} collective-permute-done((bf16[64,3584]{1,0:T(8,128)(2,1)}, bf16[64,3584]{1,0:T(8,128)(2,1)S(1)}, u32[]{:S(2)}, u32[]{:S(2)}) %collective-permute-start) | collective-permute-done | bytes 458784 | tf_op jit(solution)/shard_map/ppermute | solution.py:200
  17.0 1.5 %collective-permute-start.11 = (bf16[64,3584]{1,0:T(8,128)(2,1)S(1)}, bf16[64,3584]{1,0:T(8,128)(2,1)S(1)}, u32[]{:S(2)}, u32[]{:S(2)}) collective-permute-start(bf16[64,3584]{1,0:T(8,128)(2,1)S(1)} %collective-permute-done.refs_1_), channel_id=1, source_target_pairs={{0,2},{1,3},{2,0},{3,1},{4,6},{5,7},{6,4},{7,5},{8,10},{9,11},{10,... | collective-permute-start | bytes 1376264 | tf_op jit(solution)/shard_map/ppermute | solution.py:16
  18.5 0.7 fusion.1
  19.2 24.8 %all-gather.1 = bf16[16,64,8]{1,2,0:T(8,128)(2,1)S(1)} all-gather(bf16[1,64,8]{1,2,0:T(8,128)(2,1)S(1)} %bitcast.17), channel_id=2, replica_groups=mesh['parts'=2,'node'=4,'local'=4] {'node','local'}, dimensions={0}, use_global_device_ids=true | all-gather | bytes 17408 | tf_op jit(solution)/shard_map/all_gather | solution.py:208
  44.0 0.0 collective-permute-done.6.refs_0_
  44.0 0.0 collective-permute-start.7
  44.1 0.1 pad_maximum_fusion.2
  44.2 0.1 copy.26.refs_2_
  44.3 0.3 collective-permute-start.8
  44.6 0.1 pad_maximum_fusion
  44.7 0.1 copy.23.refs_3_
  44.8 0.1 pad_maximum_fusion.1
  44.9 0.1 copy.24.refs_2_
  45.0 13.6 %collective-permute-done.7.refs_0_ = bf16[64,3584]{1,0:T(8,128)(2,1)S(1)} collective-permute-done((bf16[64,3584]{1,0:T(8,128)(2,1)S(1)}, bf16[64,3584]{1,0:T(8,128)(2,1)S(1)}, u32[]{:S(2)}, u32[]{:S(2)}) %collective-permute-start.7) | collective-permute-done | bytes 458784 | tf_op jit(solution)/shard_map/ppermute | solution.py:200
  58.5 0.2 collective-permute-start.1
  58.8 1.8 %collective-permute-start.9 = (bf16[64,3584]{1,0:T(8,128)(2,1)S(1)}, bf16[64,3584]{1,0:T(8,128)(2,1)S(1)}, u32[]{:S(2)}, u32[]{:S(2)}) collective-permute-start(bf16[64,3584]{1,0:T(8,128)(2,1)S(1)} %collective-permute-done.7.refs_0_), channel_id=1, source_target_pairs={{0,2},{1,3},{2,0},{3,1},{4,6},{5,7},{6,4},{7,5},{8,10},{9,11},{10,... | collective-permute-start | bytes 1376264 | tf_op jit(solution)/shard_map/ppermute | solution.py:16
  60.6 0.0 collective-permute-done.3.refs_8_.refs_7_.refs_6_
  60.6 0.0 collective-permute-done.4.refs_9_.refs_8_.refs_7_
  60.6 2.0 %copy-done = bf16[1,3584,512]{2,1,0:T(8,128)(2,1)S(1)} copy-done((bf16[1,3584,512]{2,1,0:T(8,128)(2,1)S(1)}, bf16[1,3584,512]{2,1,0:T(8,128)(2,1)}, u32[]{:S(2)}) %copy-start) | copy-done | bytes 3670040
  62.6 7.1 %shard_map.67 = (bf16[64,3584]{1,0:T(8,128)(2,1)S(1)}, bf16[64,3584]{1,0:T(8,128)(2,1)S(1)}) custom-call(bf16[64,3584]{1,0:T(8,128)(2,1)S(1)} %collective-permute-done.6.refs_0_, bf16[64,3584]{1,0:T(8,128)(2,1)S(1)} %collective-permute-done.11.refs_1_, f32[128,1]{1,0:T(8,128)S(1)} %copy.26.refs_2_, bf16[1,3584,512]{2,1,0:T(8,128)(2,1)S(1)} %copy-done, ...), custom_call_target="tpu_custom_call" | custom-call | flops 2818572288 | bytes 23855104 | tf_op jit(solution)/shard_map/pallas_call | solution.py:167
  69.7 0.0 copy-start.3
  69.7 0.3 collective-permute-start.13
  70.0 0.0 collective-permute-done.8.refs_1_
  70.1 7.8 %shard_map.65 = (bf16[64,3584]{1,0:T(8,128)(2,1)S(1)}, bf16[64,3584]{1,0:T(8,128)(2,1)}) custom-call(bf16[64,3584]{1,0:T(8,128)(2,1)S(1)} %collective-permute-done.7.refs_0_, bf16[64,3584]{1,0:T(8,128)(2,1)S(1)} %collective-permute-done.8.refs_1_, f32[128,1]{1,0:T(8,128)S(1)} %copy.24.refs_2_, bf16[1,3584,512]{2,1,0:T(8,128)(2,1)S(1)} %copy-done.1, ...), custom_call_target="tpu_custom_call" | custom-call | flops 2818572288 | bytes 23855104 | tf_op jit(solution)/shard_map/pallas_call | solution.py:167
  77.9 1.9 %collective-permute-start.12 = (bf16[64,3584]{1,0:T(8,128)(2,1)}, bf16[64,3584]{1,0:T(8,128)(2,1)}, u32[]{:S(2)}, u32[]{:S(2)}) collective-permute-start(bf16[64,3584]{1,0:T(8,128)(2,1)} %get-tuple-element.16), channel_id=1, source_target_pairs={{0,2},{1,3},{2,0},{3,1},{4,6},{5,7},{6,4},{7,5},{8,10},{9,11},{10,... | collective-permute-start | bytes 1376264 | tf_op jit(solution)/shard_map/ppermute | solution.py:16
  79.7 0.0 collective-permute-done.1.refs_2_
  79.7 8.6 %shard_map.64 = (bf16[64,3584]{1,0:T(8,128)(2,1)S(1)}, bf16[64,3584]{1,0:T(8,128)(2,1)S(1)}, bf16[64,3584]{1,0:T(8,128)(2,1)S(1)}) custom-call(bf16[64,3584]{1,0:T(8,128)(2,1)S(1)} %copy-done.3, bf16[64,3584]{1,0:T(8,128)(2,1)S(1)} %collective-permute-done.refs_1_, bf16[64,3584]{1,0:T(8,128)(2,1)S(1)} %collective-permute-done.1.refs_2_, ...), custom_call_target="tpu_custom_call" | custom-call | flops 4227858432 | bytes 24772608 | tf_op jit(solution)/shard_map/pallas_call | solution.py:167
  88.4 3.5 %collective-permute-done.13 = bf16[64,3584]{1,0:T(8,128)(2,1)S(1)} collective-permute-done((bf16[64,3584]{1,0:T(8,128)(2,1)S(1)}, bf16[64,3584]{1,0:T(8,128)(2,1)S(1)}, u32[]{:S(2)}, u32[]{:S(2)}) %collective-permute-start.13) | collective-permute-done | bytes 458784 | tf_op jit(solution)/shard_map/ppermute | solution.py:16
  91.9 0.9 add_convert_fusion.3
  92.7 0.1 copy.25.refs_1_
  92.8 2.0 %copy-done.2 = bf16[1,3584,512]{2,1,0:T(8,128)(2,1)S(1)} copy-done((bf16[1,3584,512]{2,1,0:T(8,128)(2,1)S(1)}, bf16[1,3584,512]{2,1,0:T(8,128)(2,1)}, u32[]{:S(2)}) %copy-start.2) | copy-done | bytes 3670040
  94.9 7.1 %shard_map.66 = bf16[64,3584]{1,0:T(8,128)(2,1)S(1)} custom-call(bf16[64,3584]{1,0:T(8,128)(2,1)S(1)} %collective-permute-done.9.refs_0_, f32[64,1]{1,0:T(8,128)S(1)} %copy.25.refs_1_, bf16[1,3584,512]{2,1,0:T(8,128)(2,1)S(1)} %copy-done.2, bf16[1,3584,512]{2,1,0:T(8,128)(2,1)} %refs_4_.7, bf16[1,512,3584]{2,1,0:T(8,128)(2,1)} %refs_5_.5, ...), custom_call_target="tpu_custom_call" | custom-call | flops 1409286144 | bytes 22937600 | tf_op jit(solution)/shard_map/pallas_call | solution.py:167
  102.0 0.3 collective-permute-start.10
  102.3 2.1 %collective-permute-done.14 = bf16[64,3584]{1,0:T(8,128)(2,1)} collective-permute-done((bf16[64,3584]{1,0:T(8,128)(2,1)}, bf16[64,3584]{1,0:T(8,128)(2,1)}, u32[]{:S(2)}, u32[]{:S(2)}) %collective-permute-start.14) | collective-permute-done | bytes 458784 | tf_op jit(solution)/shard_map/ppermute | solution.py:200
  104.4 1.3 %add_convert_fusion.2 = bf16[64,3584]{1,0:T(8,128)(2,1)S(1)} fusion(bf16[64,3584]{1,0:T(8,128)(2,1)} %collective-permute-done.14, bf16[64,3584]{1,0:T(8,128)(2,1)} %collective-permute-done.12, bf16[64,3584]{1,0:T(8,128)(2,1)S(1)} %get-tuple-element.15), kind=kLoop, calls=%fused_computation.2 | loop fusion | flops 1376256 | bytes 1835008 | tf_op jit(solution)/shard_map/convert_element_type | solution.py:190
  105.7 0.1 collective-permute-start.15
  105.8 0.4 collective-permute-start.5
  106.2 9.3 %collective-permute-done.10 = bf16[64,3584]{1,0:T(8,128)(2,1)S(1)} collective-permute-done((bf16[64,3584]{1,0:T(8,128)(2,1)S(1)}, bf16[64,3584]{1,0:T(8,128)(2,1)S(1)}, u32[]{:S(2)}, u32[]{:S(2)}) %collective-permute-start.10) | collective-permute-done | bytes 458784 | tf_op jit(solution)/shard_map/ppermute | solution.py:16
  115.5 0.7 collective-permute-done.15
  116.2 0.2 add_convert_fusion.1
  116.4 0.1 collective-permute-start.16
  116.5 5.0 %collective-permute-done.5 = bf16[64,3584]{1,0:T(8,128)(2,1)S(1)} collective-permute-done((bf16[64,3584]{1,0:T(8,128)(2,1)S(1)}, bf16[64,3584]{1,0:T(8,128)(2,1)S(1)}, u32[]{:S(2)}, u32[]{:S(2)}) %collective-permute-start.5) | collective-permute-done | bytes 458784 | tf_op jit(solution)/shard_map/ppermute | solution.py:16
  121.4 5.3 %collective-permute-done.16 = bf16[64,3584]{1,0:T(8,128)(2,1)S(1)} collective-permute-done((bf16[64,3584]{1,0:T(8,128)(2,1)S(1)}, bf16[64,3584]{1,0:T(8,128)(2,1)S(1)}, u32[]{:S(2)}, u32[]{:S(2)}) %collective-permute-start.16) | collective-permute-done | bytes 458784 | tf_op jit(solution)/shard_map/ppermute | solution.py:200
  126.7 0.9 add_convert_fusion
  (13 shorter events, 0.1 us)
Async XLA Ops:
  0.0 58.8 %collective-permute-start.2 = (bf16[1,3584,512]{2,1,0:T(8,128)(2,1)}, bf16[1,3584,512]{2,1,0:T(8,128)(2,1)}, u32[]{:S(2)}, u32[]{:S(2)}) collective-permute-start(bf16[1,3584,512]{2,1,0:T(8,128)(2,1)} %refs_3_.5), channel_id=1, source_target_pairs={{0,1},{1,0},{2,3},{3,2},{4,5},{5,4},{6,7},{7,6},{8,9},{9,8},{10,11... | collective-permute-start | bytes 11010056 | tf_op jit(solution)/shard_map/ppermute | solution.py:16
  0.5 60.1 %collective-permute-start.3 = (bf16[1,3584,512]{2,1,0:T(8,128)(2,1)}, bf16[1,3584,512]{2,1,0:T(8,128)(2,1)}, u32[]{:S(2)}, u32[]{:S(2)}) collective-permute-start(bf16[1,3584,512]{2,1,0:T(8,128)(2,1)} %refs_4_.7), channel_id=1, source_target_pairs={{0,1},{1,0},{2,3},{3,2},{4,5},{5,4},{6,7},{7,6},{8,9},{9,8},{10,11... | collective-permute-start | bytes 11010056 | tf_op jit(solution)/shard_map/ppermute | solution.py:16
  0.5 60.1 %collective-permute-start.4 = (bf16[1,512,3584]{2,1,0:T(8,128)(2,1)}, bf16[1,512,3584]{2,1,0:T(8,128)(2,1)}, u32[]{:S(2)}, u32[]{:S(2)}) collective-permute-start(bf16[1,512,3584]{2,1,0:T(8,128)(2,1)} %refs_5_.5), channel_id=1, source_target_pairs={{0,1},{1,0},{2,3},{3,2},{4,5},{5,4},{6,7},{7,6},{8,9},{9,8},{10,11... | collective-permute-start | bytes 11010056 | tf_op jit(solution)/shard_map/ppermute | solution.py:16
  1.0 16.0 %collective-permute-start = (bf16[64,3584]{1,0:T(8,128)(2,1)}, bf16[64,3584]{1,0:T(8,128)(2,1)S(1)}, u32[]{:S(2)}, u32[]{:S(2)}) collective-permute-start(bf16[64,3584]{1,0:T(8,128)(2,1)} %refs_0_.1), channel_id=1, source_target_pairs={{0,4},{4,8},{8,12},{12,0},{1,5},{5,9},{9,13},{13,1},{2,6},{6,10},{... | collective-permute-start | bytes 1376264 | tf_op jit(solution)/shard_map/ppermute | solution.py:200
  17.0 27.0 %collective-permute-start.6 = (bf16[64,3584]{1,0:T(8,128)(2,1)S(1)}, bf16[64,3584]{1,0:T(8,128)(2,1)S(1)}, u32[]{:S(2)}, u32[]{:S(2)}) collective-permute-start(bf16[64,3584]{1,0:T(8,128)(2,1)S(1)} %collective-permute-done.refs_1_), channel_id=1, source_target_pairs={{0,4},{4,8},{8,12},{12,0},{1,5},{5,9},{9,13},{13,1},{2,6},{6,10},{... | collective-permute-start | bytes 1376264 | tf_op jit(solution)/shard_map/ppermute | solution.py:200
  17.0 27.3 %collective-permute-start.11 = (bf16[64,3584]{1,0:T(8,128)(2,1)S(1)}, bf16[64,3584]{1,0:T(8,128)(2,1)S(1)}, u32[]{:S(2)}, u32[]{:S(2)}) collective-permute-start(bf16[64,3584]{1,0:T(8,128)(2,1)S(1)} %collective-permute-done.refs_1_), channel_id=1, source_target_pairs={{0,2},{1,3},{2,0},{3,1},{4,6},{5,7},{6,4},{7,5},{8,10},{9,11},{10,... | collective-permute-start | bytes 1376264 | tf_op jit(solution)/shard_map/ppermute | solution.py:16
  44.0 14.6 %collective-permute-start.7 = (bf16[64,3584]{1,0:T(8,128)(2,1)S(1)}, bf16[64,3584]{1,0:T(8,128)(2,1)S(1)}, u32[]{:S(2)}, u32[]{:S(2)}) collective-permute-start(bf16[64,3584]{1,0:T(8,128)(2,1)S(1)} %collective-permute-done.6.refs_0_), channel_id=1, source_target_pairs={{0,4},{4,8},{8,12},{12,0},{1,5},{5,9},{9,13},{13,1},{2,6},{6,10},{... | collective-permute-start | bytes 1376264 | tf_op jit(solution)/shard_map/ppermute | solution.py:200
  44.3 25.8 %collective-permute-start.8 = (bf16[64,3584]{1,0:T(8,128)(2,1)S(1)}, bf16[64,3584]{1,0:T(8,128)(2,1)S(1)}, u32[]{:S(2)}, u32[]{:S(2)}) collective-permute-start(bf16[64,3584]{1,0:T(8,128)(2,1)S(1)} %collective-permute-done.6.refs_0_), channel_id=1, source_target_pairs={{0,2},{1,3},{2,0},{3,1},{4,6},{5,7},{6,4},{7,5},{8,10},{9,11},{10,... | collective-permute-start | bytes 1376264 | tf_op jit(solution)/shard_map/ppermute | solution.py:16
  58.5 21.2 %collective-permute-start.1 = (bf16[64,3584]{1,0:T(8,128)(2,1)}, bf16[64,3584]{1,0:T(8,128)(2,1)S(1)}, u32[]{:S(2)}, u32[]{:S(2)}) collective-permute-start(bf16[64,3584]{1,0:T(8,128)(2,1)} %refs_0_.1), channel_id=1, source_target_pairs={{0,2},{1,3},{2,0},{3,1},{4,6},{5,7},{6,4},{7,5},{8,10},{9,11},{10,... | collective-permute-start | bytes 1376264 | tf_op jit(solution)/shard_map/ppermute | solution.py:16
  58.8 34.1 %collective-permute-start.9 = (bf16[64,3584]{1,0:T(8,128)(2,1)S(1)}, bf16[64,3584]{1,0:T(8,128)(2,1)S(1)}, u32[]{:S(2)}, u32[]{:S(2)}) collective-permute-start(bf16[64,3584]{1,0:T(8,128)(2,1)S(1)} %collective-permute-done.7.refs_0_), channel_id=1, source_target_pairs={{0,2},{1,3},{2,0},{3,1},{4,6},{5,7},{6,4},{7,5},{8,10},{9,11},{10,... | collective-permute-start | bytes 1376264 | tf_op jit(solution)/shard_map/ppermute | solution.py:16
  60.6 2.0 %copy-start = (bf16[1,3584,512]{2,1,0:T(8,128)(2,1)S(1)}, bf16[1,3584,512]{2,1,0:T(8,128)(2,1)}, u32[]{:S(2)}) copy-start(bf16[1,3584,512]{2,1,0:T(8,128)(2,1)} %refs_3_.5) | copy-start | bytes 11010052
  62.6 7.4 %copy-start.1 = (bf16[1,3584,512]{2,1,0:T(8,128)(2,1)S(1)}, bf16[1,3584,512]{2,1,0:T(8,128)(2,1)}, u32[]{:S(2)}) copy-start(bf16[1,3584,512]{2,1,0:T(8,128)(2,1)} %refs_3_.5) | copy-start | bytes 11010052
  69.7 10.0 %copy-start.3 = (bf16[64,3584]{1,0:T(8,128)(2,1)S(1)}, bf16[64,3584]{1,0:T(8,128)(2,1)}, u32[]{:S(2)}) copy-start(bf16[64,3584]{1,0:T(8,128)(2,1)} %refs_0_.1) | copy-start | bytes 1376260
  69.7 22.1 %collective-permute-start.13 = (bf16[64,3584]{1,0:T(8,128)(2,1)S(1)}, bf16[64,3584]{1,0:T(8,128)(2,1)S(1)}, u32[]{:S(2)}, u32[]{:S(2)}) collective-permute-start(bf16[64,3584]{1,0:T(8,128)(2,1)S(1)} %get-tuple-element.18), channel_id=1, source_target_pairs={{0,2},{1,3},{2,0},{3,1},{4,6},{5,7},{6,4},{7,5},{8,10},{9,11},{10,... | collective-permute-start | bytes 1376264 | tf_op jit(solution)/shard_map/ppermute | solution.py:16
  77.9 24.4 %collective-permute-start.12 = (bf16[64,3584]{1,0:T(8,128)(2,1)}, bf16[64,3584]{1,0:T(8,128)(2,1)}, u32[]{:S(2)}, u32[]{:S(2)}) collective-permute-start(bf16[64,3584]{1,0:T(8,128)(2,1)} %get-tuple-element.16), channel_id=1, source_target_pairs={{0,2},{1,3},{2,0},{3,1},{4,6},{5,7},{6,4},{7,5},{8,10},{9,11},{10,... | collective-permute-start | bytes 1376264 | tf_op jit(solution)/shard_map/ppermute | solution.py:16
  92.7 11.7 %collective-permute-start.14 = (bf16[64,3584]{1,0:T(8,128)(2,1)}, bf16[64,3584]{1,0:T(8,128)(2,1)}, u32[]{:S(2)}, u32[]{:S(2)}) collective-permute-start(bf16[64,3584]{1,0:T(8,128)(2,1)} %add_convert_fusion.3), channel_id=1, source_target_pairs={{0,4},{4,8},{8,12},{12,0},{1,5},{5,9},{9,13},{13,1},{2,6},{6,10},{... | collective-permute-start | bytes 1376264 | tf_op jit(solution)/shard_map/ppermute | solution.py:200
  92.8 2.0 %copy-start.2 = (bf16[1,3584,512]{2,1,0:T(8,128)(2,1)S(1)}, bf16[1,3584,512]{2,1,0:T(8,128)(2,1)}, u32[]{:S(2)}) copy-start(bf16[1,3584,512]{2,1,0:T(8,128)(2,1)} %refs_3_.5) | copy-start | bytes 11010052
  102.0 13.5 %collective-permute-start.10 = (bf16[64,3584]{1,0:T(8,128)(2,1)S(1)}, bf16[64,3584]{1,0:T(8,128)(2,1)S(1)}, u32[]{:S(2)}, u32[]{:S(2)}) collective-permute-start(bf16[64,3584]{1,0:T(8,128)(2,1)S(1)} %shard_map.66), channel_id=1, source_target_pairs={{0,2},{1,3},{2,0},{3,1},{4,6},{5,7},{6,4},{7,5},{8,10},{9,11},{10,... | collective-permute-start | bytes 1376264 | tf_op jit(solution)/shard_map/ppermute | solution.py:16
  105.7 10.5 %collective-permute-start.15 = (bf16[64,3584]{1,0:T(8,128)(2,1)S(1)}, bf16[64,3584]{1,0:T(8,128)(2,1)S(1)}, u32[]{:S(2)}, u32[]{:S(2)}) collective-permute-start(bf16[64,3584]{1,0:T(8,128)(2,1)S(1)} %add_convert_fusion.2), channel_id=1, source_target_pairs={{0,4},{4,8},{8,12},{12,0},{1,5},{5,9},{9,13},{13,1},{2,6},{6,10},{... | collective-permute-start | bytes 1376264 | tf_op jit(solution)/shard_map/ppermute | solution.py:200
  105.8 15.6 %collective-permute-start.5 = (bf16[64,3584]{1,0:T(8,128)(2,1)S(1)}, bf16[64,3584]{1,0:T(8,128)(2,1)S(1)}, u32[]{:S(2)}, u32[]{:S(2)}) collective-permute-start(bf16[64,3584]{1,0:T(8,128)(2,1)S(1)} %get-tuple-element.13), channel_id=1, source_target_pairs={{0,2},{1,3},{2,0},{3,1},{4,6},{5,7},{6,4},{7,5},{8,10},{9,11},{10,... | collective-permute-start | bytes 1376264 | tf_op jit(solution)/shard_map/ppermute | solution.py:16
  116.4 10.3 %collective-permute-start.16 = (bf16[64,3584]{1,0:T(8,128)(2,1)S(1)}, bf16[64,3584]{1,0:T(8,128)(2,1)S(1)}, u32[]{:S(2)}, u32[]{:S(2)}) collective-permute-start(bf16[64,3584]{1,0:T(8,128)(2,1)S(1)} %add_convert_fusion.1), channel_id=1, source_target_pairs={{0,4},{4,8},{8,12},{12,0},{1,5},{5,9},{9,13},{13,1},{2,6},{6,10},{... | collective-permute-start | bytes 1376264 | tf_op jit(solution)/shard_map/ppermute | solution.py:200

commit v2 on v1

--- a/solution.py
+++ b/solution.py
@@ -106,11 +106,12 @@
     combined = jnp.einsum("gsb,gsd->bd", one_hot, gathered_back, preferred_element_type=jnp.float32)
     return combined.astype(jnp.bfloat16)
 
-def expert_kernel(count, down_tiles, hidden_tile, *refs):
-    blocks, scores, weights = refs[:count], refs[count], refs[count + 1 : count + 7]
-    outs = refs[count + 7 : 2 * count + 7]
-    rows_all, gate, up, down, hidden, sems = refs[2 * count + 7 :]
-    rows, width = blocks[0].shape
+def expert_kernel(counts, down_tiles, hidden_tile, *refs):
+    taken, given = counts
+    blocks, scores, weights = refs[:taken], refs[taken], refs[taken + 1 : taken + 7]
+    outs = refs[taken + 7 : taken + 7 + given]
+    rows_all, gate, up, down, hidden, sems = refs[taken + 7 + given :]
+    width = rows_all.shape[1]
     half = gate.shape[-1]
     started = []
 
@@ -137,8 +138,10 @@
             fetch(weights[3 * side + 2].at[0, :, cols], down.at[side, :, cols]) for side in range(2)
         )
         second.append((cols, pair))
-    for i in range(count):
-        rows_all[pl.ds(i * rows, rows), :] = blocks[i][...]
+    at = 0
+    for block in blocks:
+        rows_all[pl.ds(at, block.shape[0]), :] = block[...]
+        at += block.shape[0]
     for side, cols, pair in first:
         for copy in pair:
             copy.wait()
@@ -151,24 +154,26 @@
         result = jnp.dot(hidden[0], down[0, :, cols], preferred_element_type=jnp.float32)
         result += jnp.dot(hidden[1], down[1, :, cols], preferred_element_type=jnp.float32)
         result = (result * scores[...]).astype(jnp.bfloat16)
-        for i in range(count):
-            outs[i][:, cols] = result[i * rows : (i + 1) * rows]
-
-
-def expert_rows(blocks, scores, own, other):
-    count = len(blocks)
-    rows, width = blocks[0].shape
+        at = 0
+        for out in outs:
+            out[:, cols] = result[at : at + out.shape[0]]
+            at += out.shape[0]
+
+
+def expert_rows(blocks, scores, own, other, out_rows):
+    width = blocks[0].shape[1]
     half = own[0].shape[-1]
-    total = count * rows
+    total = sum(block.shape[0] for block in blocks)
+    given = total // out_rows
     down_tiles = 4
     hidden_tile = half // 2
     vmem = pl.BlockSpec(memory_space=pltpu.VMEM)
     anywhere = pl.BlockSpec(memory_space=pl.ANY)
     return pl.pallas_call(
-        functools.partial(expert_kernel, count, down_tiles, hidden_tile),
-        out_shape=[jax.ShapeDtypeStruct((rows, width), jnp.bfloat16)] * count,
-        in_specs=[vmem] * (count + 1) + [anywhere] * 6,
-        out_specs=[vmem] * count,
+        functools.partial(expert_kernel, (len(blocks), given), down_tiles, hidden_tile),
+        out_shape=[jax.ShapeDtypeStruct((out_rows, width), jnp.bfloat16)] * given,
+        in_specs=[vmem] * (len(blocks) + 1) + [anywhere] * 6,
+        out_specs=[vmem] * given,
         scratch_shapes=[
             pltpu.VMEM((total, width), jnp.bfloat16),
             pltpu.VMEM((2, width, half), jnp.bfloat16),
@@ -183,66 +188,98 @@
             bytes_accessed=12 * width * half + 4 * total * width,
             transcendentals=2 * total * half,
         ),
-    )(*blocks, jnp.concatenate(scores, axis=0), *own, *other)
+    )(*blocks, scores, *own, *other)
 
 
 def added(*terms):
     return sum(term.astype(jnp.float32) for term in terms).astype(jnp.bfloat16)
+
+
+def together(*values):
+    return lax.optimization_barrier(values)
 
 
 def dense(tokens, expert_ids, gate_scores, gate_weight, up_weight, down_weight):
     node_count = lax.axis_size("node")
     local_count = lax.axis_size("local")
     node, local = lax.axis_index("node"), lax.axis_index("local")
+    rows = tokens.shape[0]
+    split = rows // 2
+    last = node_count - 1
 
     def next_node(value):
         pairs = [(source, (source + 1) % node_count) for source in range(node_count)]
         return lax.ppermute(value, "node", pairs)
 
+    def other_x(value):
+        return partner(value, "local", 1)
+
     own = (gate_weight, up_weight, down_weight)
     other = tuple(partner(weight, "local", 0) for weight in own)
 
     experts = jnp.arange(node_count * (local_count // 2))
     named = expert_ids[:, :, None] == experts[None, None, :]
     factors = jnp.sum(jnp.where(named, gate_scores[:, :, None], 0), axis=1).astype(jnp.bfloat16)
-    factors = lax.all_gather(factors, ("node", "local"))
+    factors = jnp.stack([factors, other_x(factors)])
+    bit = 0
+    while 2**bit < node_count:
+        factors = jnp.concatenate([factors, partner(factors, "node", bit)])
+        bit += 1
     mine = node * (local_count // 2) + local // 2
     factors = lax.dynamic_index_in_dim(factors, mine, 2, keepdims=True).astype(jnp.float32)
 
-    def factor_of(slot, here):
-        source = lax.rem(node - slot + node_count, node_count) * local_count
-        source += local if here else local ^ 2
-        return lax.dynamic_index_in_dim(factors, source, 0, keepdims=False)
+    def factor_of(kind, slot):
+        source = lax.rem(node - slot + node_count, node_count)
+        at = 2 * (source ^ node) + (0 if kind == "a" else 1)
+        return lax.dynamic_index_in_dim(factors, at, 0, keepdims=False)
+
+    done = {}
+
+    def work(keys, parts=None):
+        blocks = parts or [(along if kind == "a" else across)[slot] for kind, slot in keys]
+        scores = jnp.concatenate([factor_of(*key) for key in keys])
+        results = expert_rows(blocks, scores, own, other, rows)
+        done.update(zip(keys, results))
+        return results
+
+    def hold(keys, *values):
+        held = together(*values, *[done[key] for key in keys])
+        done.update(zip(keys, held[len(values) :]))
+        return held[: len(values)]
 
     along, across = [tokens], []
-    for slot in range(node_count):
-        across.append(partner(along[slot], "local", 1))
-        if slot < node_count - 1:
-            along.append(next_node(along[slot]))
-
-    order = [("a", 0)]
-    for slot in range(1, node_count):
-        order += [("a", slot), ("x", slot - 1)]
-    order.append(("x", node_count - 1))
-    sizes = [3] + [2] * (node_count - 2) + [1]
-    done = {}
-    at = 0
-    for size in sizes:
-        keys = order[at : at + size]
-        at += size
-        blocks = [(along if kind == "a" else across)[slot] for kind, slot in keys]
-        scores = [factor_of(slot, kind == "a") for kind, slot in keys]
-        results = expert_rows(blocks, scores, own, other)
-        done.update(zip(keys, results))
-
-    running = None
-    for slot in list(range(1, node_count)) + [0]:
-        terms = [done["a", slot], partner(done["x", slot], "local", 1)]
-        if running is not None:
-            terms.append(running)
-        running = added(*terms)
-        if slot:
-            running = next_node(running)
+    early = [("a", 0)] + [(kind, slot) for slot in range(1, last) for kind in "ax"]
+    early = [("a", 0)]
+    for slot in range(1, last):
+        early += [("a", slot), ("x", slot - 1)]
+    for slot in range(last):
+        moved, crossed = next_node(along[slot]), other_x(along[slot])
+        if slot < last - 1:
+            moved, crossed = together(moved, crossed)
+        else:
+            work(early)
+            moved, crossed = hold(early, moved, crossed)
+        along.append(moved)
+        across.append(crossed)
+    upper, lower = other_x(along[last][:split]), next_node(across[last - 1][split:])
+    middle = [("a", last), ("x", last - 1)]
+    work(middle)
+    upper, lower = hold(middle, upper, lower)
+
+    crossed, passed = together(other_x(done["x", 1][:split]), next_node(done["x", 1][split:]))
+    second = done["x", 2]
+    done["x", 2] = jnp.concatenate([second[:split], added(second[split:], passed)])
+    first = done["a", 1]
+    running = jnp.concatenate([added(first[:split], crossed), first[split:]])
+    for slot in list(range(2, node_count)) + [0]:
+        crossed, moved = other_x(done["x", slot]), next_node(running)
+        if slot == 2:
+            late = [("x", last)]
+            work(late, [upper, lower])
+            crossed, moved = hold(late, crossed, moved)
+        elif slot:
+            crossed, moved = together(crossed, moved)
+        running = added(done["a", slot], crossed, moved)
     return running
 
 

time: 128 us -> 106 us (0.83)
  blocking collectives: 24.8 us -> 0 us
  starting transfers between devices: 10.3 us -> 24.9 us
  Pallas kernels: 30.7 us -> 25.3 us
  waiting for transfers between devices: 52.9 us -> 48.9 us
    all_gather x1 -> x0, blocking collectives: 24.8 us -> none  [dense(): factors = lax.all_gather(factors, ('node', 'local'))]
    ppermute x6 -> x8, starting transfers between devices: 2.7 us -> 10.8 us  [next_node(): return lax.ppermute(value, 'node', pairs)]
    ppermute x6 -> x8, waiting for transfers between devices: 35.1 us -> 27.1 us  [next_node(): return lax.ppermute(value, 'node', pairs)]
    ppermute x11 -> x14, starting transfers between devices: 7.63 us -> 14.1 us  [partner(): return lax.ppermute(value, axis, pairs)]
    pallas_call x4 -> x3, Pallas kernels: 30.7 us -> 25.3 us  [expert_rows(): pl.pallas_call(functools.partial(expert_kernel, (len(blocks), given), dow...]
    ppermute x11 -> x14, waiting for transfers between devices: 17.8 us -> 21.8 us  [partner(): return lax.ppermute(value, axis, pairs)]
    convert_element_type x4 -> x5, other arithmetic: 3.3 us -> 1.38 us  [added(): sum((term.astype(jnp.float32) for term in terms)).astype(jnp.bfloat16)]
    unnamed x8 -> x10, local copies, waits for them, and re-layouts: 4.08 us -> 3.06 us
  transfers between devices with their start and end apart: 17 -> 22, of which waited for: 8 -> 9; matrix products, arithmetic and copies ran while one was open for 3% -> 2% of each run, Pallas kernels for 24% -> 24%
where the time goes in v2:
time: 106 us
  waiting for transfers between devices  48.9 us (46%)
  Pallas kernels  25.3 us (24%)
  starting transfers between devices  24.9 us (23%)
  local copies, waits for them, and re-layouts  3.63 us (3%)
  other arithmetic  3.02 us (3%)
    ppermute x8, waiting for transfers between devices, next_node(): return lax.ppermute(value, 'node', pairs)  27.1 us
    pallas_call x3, Pallas kernels, expert_rows(): pl.pallas_call(functools.partial(expert_kernel, (len(blocks), given), dow...  25.3 us
    ppermute x14, waiting for transfers between devices, partner(): return lax.ppermute(value, axis, pairs)  21.8 us
    ppermute x14, starting transfers between devices, partner(): return lax.ppermute(value, axis, pairs)  14.1 us
    ppermute x8, starting transfers between devices, next_node(): return lax.ppermute(value, 'node', pairs)  10.8 us
    unnamed x10, local copies, waits for them, and re-layouts  3.06 us
  transfers between devices with their start and end apart: 22, of which 9 were waited for; matrix products, arithmetic and copies ran while one was open for 2% of the time, Pallas kernels for 24%

profile of v2, /device:TPU:0, one launch (start us, length us, event | category | flops | bytes accessed | tf_op | source)
XLA Modules:
  0.0 105.9 jit_solution(14239149379205718530)
XLA Ops:
  0.0 0.5 collective-permute-start.10
  0.5 0.1 collective-permute-start.11
  0.5 0.5 collective-permute-start.9
  1.0 0.7 fusion.1
  1.7 2.6 %collective-permute-start.6 = (bf16[64,8]{0,1:T(8,128)(2,1)S(1)}, bf16[64,8]{0,1:T(8,128)(2,1)S(1)}, u32[]{:S(2)}, u32[]{:S(2)}) collective-permute-start(bf16[64,8]{0,1:T(8,128)(2,1)S(1)} %fusion.1), channel_id=1, source_target_pairs={{0,2},{1,3},{2,0},{3,1},{4,6},{5,7},{6,4},{7,5},{8,10},{9,11},{10,... | collective-permute-start | bytes 3080 | tf_op jit(solution)/shard_map/ppermute | solution.py:16
  4.2 1.6 %collective-permute-start = (bf16[64,3584]{1,0:T(8,128)(2,1)}, bf16[64,3584]{1,0:T(8,128)(2,1)S(1)}, u32[]{:S(2)}, u32[]{:S(2)}) collective-permute-start(bf16[64,3584]{1,0:T(8,128)(2,1)} %refs_0_.1), channel_id=1, source_target_pairs={{0,4},{4,8},{8,12},{12,0},{1,5},{5,9},{9,13},{13,1},{2,6},{6,10},{... | collective-permute-start | bytes 1376264 | tf_op jit(solution)/shard_map/ppermute | solution.py:212
  5.8 2.1 %collective-permute-start.7 = (bf16[2,64,8]{1,2,0:T(8,128)(2,1)S(1)}, bf16[2,64,8]{1,2,0:T(8,128)(2,1)S(1)}, u32[]{:S(2)}, u32[]{:S(2)}) collective-permute-start(bf16[2,64,8]{1,2,0:T(8,128)(2,1)S(1)} %pad_maximum_fusion.3), channel_id=1, source_target_pairs={{0,4},{4,0},{8,12},{12,8},{1,5},{5,1},{9,13},{13,9},{2,6},{6,2},{1... | collective-permute-start | bytes 6152 | tf_op jit(solution)/shard_map/ppermute | solution.py:16
  7.9 8.4 %collective-permute-done.7 = bf16[2,64,8]{1,2,0:T(8,128)(2,1)S(1)} collective-permute-done((bf16[2,64,8]{1,2,0:T(8,128)(2,1)S(1)}, bf16[2,64,8]{1,2,0:T(8,128)(2,1)S(1)}, u32[]{:S(2)}, u32[]{:S(2)}) %collective-permute-start.7) | collective-permute-done | bytes 2080 | tf_op jit(solution)/shard_map/ppermute | solution.py:16
  16.3 0.5 collective-permute-start.1
  16.9 2.1 %collective-permute-done.refs_1_ = bf16[64,3584]{1,0:T(8,128)(2,1)S(1)} collective-permute-done((bf16[64,3584]{1,0:T(8,128)(2,1)}, bf16[64,3584]{1,0:T(8,128)(2,1)S(1)}, u32[]{:S(2)}, u32[]{:S(2)}) %collective-permute-start) | collective-permute-done | bytes 458784 | tf_op jit(solution)/shard_map/ppermute | solution.py:212
  19.0 1.2 %collective-permute-start.8 = (bf16[4,64,8]{1,2,0:T(8,128)(2,1)S(1)}, bf16[4,64,8]{1,2,0:T(8,128)(2,1)S(1)}, u32[]{:S(2)}, u32[]{:S(2)}) collective-permute-start(bf16[4,64,8]{1,2,0:T(8,128)(2,1)S(1)} %pad_maximum_fusion.2), channel_id=1, source_target_pairs={{0,8},{4,12},{8,0},{12,4},{1,9},{5,13},{9,1},{13,5},{2,10},{6,14},... | collective-permute-start | bytes 12296 | tf_op jit(solution)/shard_map/ppermute | solution.py:16
  20.2 8.1 %collective-permute-done.1.refs_2_ = bf16[64,3584]{1,0:T(8,128)(2,1)S(1)} collective-permute-done((bf16[64,3584]{1,0:T(8,128)(2,1)}, bf16[64,3584]{1,0:T(8,128)(2,1)S(1)}, u32[]{:S(2)}, u32[]{:S(2)}) %collective-permute-start.1) | collective-permute-done | bytes 458784 | tf_op jit(solution)/shard_map/ppermute | solution.py:16
  28.3 2.5 %collective-permute-start.2 = (bf16[64,3584]{1,0:T(8,128)(2,1)S(1)}, bf16[64,3584]{1,0:T(8,128)(2,1)S(1)}, u32[]{:S(2)}, u32[]{:S(2)}) collective-permute-start(bf16[64,3584]{1,0:T(8,128)(2,1)S(1)} %collective-permute-done.refs_1_), channel_id=1, source_target_pairs={{0,4},{4,8},{8,12},{12,0},{1,5},{5,9},{9,13},{13,1},{2,6},{6,10},{... | collective-permute-start | bytes 1376264 | tf_op jit(solution)/shard_map/ppermute | solution.py:212
  30.8 0.5 collective-permute-start.3
  31.4 0.1 concatenate.22
  31.5 0.1 copy.22.refs_5_
  31.6 0.1 pad_maximum_fusion.4
  31.7 0.1 copy.23.refs_2_
  31.8 10.2 %collective-permute-done.2.refs_3_ = bf16[64,3584]{1,0:T(8,128)(2,1)S(1)} collective-permute-done((bf16[64,3584]{1,0:T(8,128)(2,1)S(1)}, bf16[64,3584]{1,0:T(8,128)(2,1)S(1)}, u32[]{:S(2)}, u32[]{:S(2)}) %collective-permute-start.2) | collective-permute-done | bytes 458784 | tf_op jit(solution)/shard_map/ppermute | solution.py:212
  42.0 1.0 collective-permute-start.4
  43.0 1.1 %collective-permute-start.5 = (bf16[64,3584]{1,0:T(8,128)(2,1)S(1)}, bf16[64,3584]{1,0:T(8,128)(2,1)S(1)}, u32[]{:S(2)}, u32[]{:S(2)}) collective-permute-start(bf16[64,3584]{1,0:T(8,128)(2,1)S(1)} %collective-permute-done.2.refs_3_), channel_id=1, source_target_pairs={{0,2},{1,3},{2,0},{3,1},{4,6},{5,7},{6,4},{7,5},{8,10},{9,11},{10,... | collective-permute-start | bytes 1376264 | tf_op jit(solution)/shard_map/ppermute | solution.py:16
  44.1 1.0 copy-done.2
  45.1 11.2 %shard_map.64 = (bf16[64,3584]{1,0:T(8,128)(2,1)S(1)}, bf16[64,3584]{1,0:T(8,128)(2,1)S(1)}, bf16[64,3584]{1,0:T(8,128)(2,1)S(1)}, bf16[64,3584]{1,0:T(8,128)(2,1)S(1)}, bf16[64,3584]{1,0:T(8,128)(2,1)S(1)}) custom-call(bf16[64,3584]{1,0:T(8,128)(2,1)S(1)} %copy-done.2, bf16[64,3584]{1,0:T(8,128)(2,1)S(1)} %collective-permute-done.refs_1_, ...), custom_call_target="tpu_custom_call" | custom-call | flops 7046430720 | bytes 26607616 | tf_op jit(solution)/shard_map/pallas_call | solution.py:172
  56.3 1.0 collective-permute-start.13
  57.4 1.7 %collective-permute-start.14 = (bf16[32,3584]{1,0:T(8,128)(2,1)S(1)}, bf16[32,3584]{1,0:T(8,128)(2,1)S(1)}, u32[]{:S(2)}, u32[]{:S(2)}) collective-permute-start(bf16[32,3584]{1,0:T(8,128)(2,1)S(1)} %slice.25), channel_id=1, source_target_pairs={{0,4},{4,8},{8,12},{12,0},{1,5},{5,9},{9,13},{13,1},{2,6},{6,10},{... | collective-permute-start | bytes 688136 | tf_op jit(solution)/shard_map/ppermute | solution.py:212
  59.1 0.6 collective-permute-start.15
  59.7 0.3 collective-permute-start.16
  60.0 7.0 %shard_map.65 = (bf16[64,3584]{1,0:T(8,128)(2,1)S(1)}, bf16[64,3584]{1,0:T(8,128)(2,1)S(1)}) custom-call(bf16[64,3584]{1,0:T(8,128)(2,1)S(1)} %collective-permute-done.4.refs_0_, bf16[64,3584]{1,0:T(8,128)(2,1)S(1)} %collective-permute-done.5.refs_1_, f32[128,1]{1,0:T(8,128)S(1)} %copy.23.refs_2_, bf16[1,3584,512]{2,1,0:T(8,128)(2,1)S(1)} %copy-done, ...), custom_call_target="tpu_custom_call" | custom-call | flops 2818572288 | bytes 23855104 | tf_op jit(solution)/shard_map/pallas_call | solution.py:172
  67.0 1.1 %collective-permute-done.16 = bf16[32,3584]{1,0:T(8,128)(2,1)S(1)} collective-permute-done((bf16[32,3584]{1,0:T(8,128)(2,1)S(1)}, bf16[32,3584]{1,0:T(8,128)(2,1)S(1)}, u32[]{:S(2)}, u32[]{:S(2)}) %collective-permute-start.16) | collective-permute-done | bytes 229408 | tf_op jit(solution)/shard_map/ppermute | solution.py:212
  68.2 0.1 add_convert_fusion.3
  68.3 1.2 %collective-permute-start.18 = (bf16[64,3584]{1,0:T(8,128)(2,1)S(1)}, bf16[64,3584]{1,0:T(8,128)(2,1)S(1)}, u32[]{:S(2)}, u32[]{:S(2)}) collective-permute-start(bf16[64,3584]{1,0:T(8,128)(2,1)S(1)} %pad_maximum_fusion.1), channel_id=1, source_target_pairs={{0,4},{4,8},{8,12},{12,0},{1,5},{5,9},{9,13},{13,1},{2,6},{6,10},{... | collective-permute-start | bytes 1376264 | tf_op jit(solution)/shard_map/ppermute | solution.py:212
  69.4 0.1 add_convert_fusion.4
  69.5 0.8 pad_maximum_fusion
  70.3 1.5 %collective-permute-start.17 = (bf16[64,3584]{1,0:T(8,128)(2,1)}, bf16[64,3584]{1,0:T(8,128)(2,1)S(1)}, u32[]{:S(2)}, u32[]{:S(2)}) collective-permute-start(bf16[64,3584]{1,0:T(8,128)(2,1)} %pad_maximum_fusion), channel_id=1, source_target_pairs={{0,2},{1,3},{2,0},{3,1},{4,6},{5,7},{6,4},{7,5},{8,10},{9,11},{10,... | collective-permute-start | bytes 1376264 | tf_op jit(solution)/shard_map/ppermute | solution.py:16
  71.8 0.1 copy.24.refs_2_
  71.9 2.0 %copy-done.1 = bf16[1,3584,512]{2,1,0:T(8,128)(2,1)S(1)} copy-done((bf16[1,3584,512]{2,1,0:T(8,128)(2,1)S(1)}, bf16[1,3584,512]{2,1,0:T(8,128)(2,1)}, u32[]{:S(2)}) %copy-start.1) | copy-done | bytes 3670040
  73.9 7.1 %shard_map.66 = bf16[64,3584]{1,0:T(8,128)(2,1)S(1)} custom-call(bf16[32,3584]{1,0:T(8,128)(2,1)S(1)} %collective-permute-done.13.refs_0_, bf16[32,3584]{1,0:T(8,128)(2,1)S(1)} %collective-permute-done.14.refs_1_, f32[64,1]{1,0:T(8,128)S(1)} %copy.24.refs_2_, bf16[1,3584,512]{2,1,0:T(8,128)(2,1)S(1)} %copy-done.1, bf16[1,3584,512]{2,1,0:T(8,128)(2,1)} %refs_4_.3, ...), custom_call_target="tpu_custom_call" | custom-call | flops 1409286144 | bytes 22937600 | tf_op jit(solution)/shard_map/pallas_call | solution.py:172
  81.1 0.2 add_convert_fusion.2
  81.3 1.0 collective-permute-start.20
  82.3 1.1 collective-permute-start.19
  83.4 1.0 collective-permute-start.12
  84.3 8.1 %collective-permute-done.20 = bf16[64,3584]{1,0:T(8,128)(2,1)S(1)} collective-permute-done((bf16[64,3584]{1,0:T(8,128)(2,1)S(1)}, bf16[64,3584]{1,0:T(8,128)(2,1)S(1)}, u32[]{:S(2)}, u32[]{:S(2)}) %collective-permute-start.20) | collective-permute-done | bytes 458784 | tf_op jit(solution)/shard_map/ppermute | solution.py:212
  92.5 2.0 %collective-permute-done.19 = bf16[64,3584]{1,0:T(8,128)(2,1)S(1)} collective-permute-done((bf16[64,3584]{1,0:T(8,128)(2,1)S(1)}, bf16[64,3584]{1,0:T(8,128)(2,1)S(1)}, u32[]{:S(2)}, u32[]{:S(2)}) %collective-permute-start.19) | collective-permute-done | bytes 458784 | tf_op jit(solution)/shard_map/ppermute | solution.py:16
  94.5 0.2 add_convert_fusion.1
  94.7 1.6 %collective-permute-start.21 = (bf16[64,3584]{1,0:T(8,128)(2,1)S(1)}, bf16[64,3584]{1,0:T(8,128)(2,1)S(1)}, u32[]{:S(2)}, u32[]{:S(2)}) collective-permute-start(bf16[64,3584]{1,0:T(8,128)(2,1)S(1)} %add_convert_fusion.1), channel_id=1, source_target_pairs={{0,4},{4,8},{8,12},{12,0},{1,5},{5,9},{9,13},{13,1},{2,6},{6,10},{... | collective-permute-start | bytes 1376264 | tf_op jit(solution)/shard_map/ppermute | solution.py:212
  96.2 3.2 %collective-permute-done.12 = bf16[64,3584]{1,0:T(8,128)(2,1)S(1)} collective-permute-done((bf16[64,3584]{1,0:T(8,128)(2,1)S(1)}, bf16[64,3584]{1,0:T(8,128)(2,1)S(1)}, u32[]{:S(2)}, u32[]{:S(2)}) %collective-permute-start.12) | collective-permute-done | bytes 458784 | tf_op jit(solution)/shard_map/ppermute | solution.py:16
  99.4 5.6 %collective-permute-done.21 = bf16[64,3584]{1,0:T(8,128)(2,1)S(1)} collective-permute-done((bf16[64,3584]{1,0:T(8,128)(2,1)S(1)}, bf16[64,3584]{1,0:T(8,128)(2,1)S(1)}, u32[]{:S(2)}, u32[]{:S(2)}) %collective-permute-start.21) | collective-permute-done | bytes 458784 | tf_op jit(solution)/shard_map/ppermute | solution.py:212
  105.0 0.9 add_convert_fusion
  (31 shorter events, 0.2 us)
Async XLA Ops:
  0.0 44.1 %collective-permute-start.10 = (bf16[1,3584,512]{2,1,0:T(8,128)(2,1)}, bf16[1,3584,512]{2,1,0:T(8,128)(2,1)}, u32[]{:S(2)}, u32[]{:S(2)}) collective-permute-start(bf16[1,3584,512]{2,1,0:T(8,128)(2,1)} %refs_4_.3), channel_id=1, source_target_pairs={{0,1},{1,0},{2,3},{3,2},{4,5},{5,4},{6,7},{7,6},{8,9},{9,8},{10,11... | collective-permute-start | bytes 11010056 | tf_op jit(solution)/shard_map/ppermute | solution.py:16
  0.5 43.6 %collective-permute-start.11 = (bf16[1,512,3584]{2,1,0:T(8,128)(2,1)}, bf16[1,512,3584]{2,1,0:T(8,128)(2,1)}, u32[]{:S(2)}, u32[]{:S(2)}) collective-permute-start(bf16[1,512,3584]{2,1,0:T(8,128)(2,1)} %refs_5_.3), channel_id=1, source_target_pairs={{0,1},{1,0},{2,3},{3,2},{4,5},{5,4},{6,7},{7,6},{8,9},{9,8},{10,11... | collective-permute-start | bytes 11010056 | tf_op jit(solution)/shard_map/ppermute | solution.py:16
  0.5 43.5 %collective-permute-start.9 = (bf16[1,3584,512]{2,1,0:T(8,128)(2,1)}, bf16[1,3584,512]{2,1,0:T(8,128)(2,1)}, u32[]{:S(2)}, u32[]{:S(2)}) collective-permute-start(bf16[1,3584,512]{2,1,0:T(8,128)(2,1)} %refs_3_.3), channel_id=1, source_target_pairs={{0,1},{1,0},{2,3},{3,2},{4,5},{5,4},{6,7},{7,6},{8,9},{9,8},{10,11... | collective-permute-start | bytes 11010056 | tf_op jit(solution)/shard_map/ppermute | solution.py:16
  1.7 4.1 %collective-permute-start.6 = (bf16[64,8]{0,1:T(8,128)(2,1)S(1)}, bf16[64,8]{0,1:T(8,128)(2,1)S(1)}, u32[]{:S(2)}, u32[]{:S(2)}) collective-permute-start(bf16[64,8]{0,1:T(8,128)(2,1)S(1)} %fusion.1), channel_id=1, source_target_pairs={{0,2},{1,3},{2,0},{3,1},{4,6},{5,7},{6,4},{7,5},{8,10},{9,11},{10,... | collective-permute-start | bytes 3080 | tf_op jit(solution)/shard_map/ppermute | solution.py:16
  4.2 14.8 %collective-permute-start = (bf16[64,3584]{1,0:T(8,128)(2,1)}, bf16[64,3584]{1,0:T(8,128)(2,1)S(1)}, u32[]{:S(2)}, u32[]{:S(2)}) collective-permute-start(bf16[64,3584]{1,0:T(8,128)(2,1)} %refs_0_.1), channel_id=1, source_target_pairs={{0,4},{4,8},{8,12},{12,0},{1,5},{5,9},{9,13},{13,1},{2,6},{6,10},{... | collective-permute-start | bytes 1376264 | tf_op jit(solution)/shard_map/ppermute | solution.py:212
  5.8 10.5 %collective-permute-start.7 = (bf16[2,64,8]{1,2,0:T(8,128)(2,1)S(1)}, bf16[2,64,8]{1,2,0:T(8,128)(2,1)S(1)}, u32[]{:S(2)}, u32[]{:S(2)}) collective-permute-start(bf16[2,64,8]{1,2,0:T(8,128)(2,1)S(1)} %pad_maximum_fusion.3), channel_id=1, source_target_pairs={{0,4},{4,0},{8,12},{12,8},{1,5},{5,1},{9,13},{13,9},{2,6},{6,2},{1... | collective-permute-start | bytes 6152 | tf_op jit(solution)/shard_map/ppermute | solution.py:16
  16.3 12.0 %collective-permute-start.1 = (bf16[64,3584]{1,0:T(8,128)(2,1)}, bf16[64,3584]{1,0:T(8,128)(2,1)S(1)}, u32[]{:S(2)}, u32[]{:S(2)}) collective-permute-start(bf16[64,3584]{1,0:T(8,128)(2,1)} %refs_0_.1), channel_id=1, source_target_pairs={{0,2},{1,3},{2,0},{3,1},{4,6},{5,7},{6,4},{7,5},{8,10},{9,11},{10,... | collective-permute-start | bytes 1376264 | tf_op jit(solution)/shard_map/ppermute | solution.py:16
  19.0 11.8 %collective-permute-start.8 = (bf16[4,64,8]{1,2,0:T(8,128)(2,1)S(1)}, bf16[4,64,8]{1,2,0:T(8,128)(2,1)S(1)}, u32[]{:S(2)}, u32[]{:S(2)}) collective-permute-start(bf16[4,64,8]{1,2,0:T(8,128)(2,1)S(1)} %pad_maximum_fusion.2), channel_id=1, source_target_pairs={{0,8},{4,12},{8,0},{12,4},{1,9},{5,13},{9,1},{13,5},{2,10},{6,14},... | collective-permute-start | bytes 12296 | tf_op jit(solution)/shard_map/ppermute | solution.py:16
  28.3 13.7 %collective-permute-start.2 = (bf16[64,3584]{1,0:T(8,128)(2,1)S(1)}, bf16[64,3584]{1,0:T(8,128)(2,1)S(1)}, u32[]{:S(2)}, u32[]{:S(2)}) collective-permute-start(bf16[64,3584]{1,0:T(8,128)(2,1)S(1)} %collective-permute-done.refs_1_), channel_id=1, source_target_pairs={{0,4},{4,8},{8,12},{12,0},{1,5},{5,9},{9,13},{13,1},{2,6},{6,10},{... | collective-permute-start | bytes 1376264 | tf_op jit(solution)/shard_map/ppermute | solution.py:212
  30.8 11.2 %collective-permute-start.3 = (bf16[64,3584]{1,0:T(8,128)(2,1)S(1)}, bf16[64,3584]{1,0:T(8,128)(2,1)S(1)}, u32[]{:S(2)}, u32[]{:S(2)}) collective-permute-start(bf16[64,3584]{1,0:T(8,128)(2,1)S(1)} %collective-permute-done.refs_1_), channel_id=1, source_target_pairs={{0,2},{1,3},{2,0},{3,1},{4,6},{5,7},{6,4},{7,5},{8,10},{9,11},{10,... | collective-permute-start | bytes 1376264 | tf_op jit(solution)/shard_map/ppermute | solution.py:16
  42.0 14.3 %collective-permute-start.4 = (bf16[64,3584]{1,0:T(8,128)(2,1)S(1)}, bf16[64,3584]{1,0:T(8,128)(2,1)S(1)}, u32[]{:S(2)}, u32[]{:S(2)}) collective-permute-start(bf16[64,3584]{1,0:T(8,128)(2,1)S(1)} %collective-permute-done.2.refs_3_), channel_id=1, source_target_pairs={{0,4},{4,8},{8,12},{12,0},{1,5},{5,9},{9,13},{13,1},{2,6},{6,10},{... | collective-permute-start | bytes 1376264 | tf_op jit(solution)/shard_map/ppermute | solution.py:212
  43.0 13.3 %collective-permute-start.5 = (bf16[64,3584]{1,0:T(8,128)(2,1)S(1)}, bf16[64,3584]{1,0:T(8,128)(2,1)S(1)}, u32[]{:S(2)}, u32[]{:S(2)}) collective-permute-start(bf16[64,3584]{1,0:T(8,128)(2,1)S(1)} %collective-permute-done.2.refs_3_), channel_id=1, source_target_pairs={{0,2},{1,3},{2,0},{3,1},{4,6},{5,7},{6,4},{7,5},{8,10},{9,11},{10,... | collective-permute-start | bytes 1376264 | tf_op jit(solution)/shard_map/ppermute | solution.py:16
  44.1 1.0 copy-start.2
  45.1 14.9 %copy-start = (bf16[1,3584,512]{2,1,0:T(8,128)(2,1)S(1)}, bf16[1,3584,512]{2,1,0:T(8,128)(2,1)}, u32[]{:S(2)}) copy-start(bf16[1,3584,512]{2,1,0:T(8,128)(2,1)} %refs_3_.3) | copy-start | bytes 11010052
  56.3 10.7 %copy-start.3 = (bf16[64,3584]{1,0:T(8,128)(2,1)}, bf16[64,3584]{1,0:T(8,128)(2,1)S(1)}, u32[]{:S(2)}) copy-start(bf16[64,3584]{1,0:T(8,128)(2,1)S(1)} %get-tuple-element.44) | copy-start | bytes 1376260
  56.3 10.7 %collective-permute-start.13 = (bf16[32,3584]{1,0:T(8,128)(2,1)S(1)}, bf16[32,3584]{1,0:T(8,128)(2,1)S(1)}, u32[]{:S(2)}, u32[]{:S(2)}) collective-permute-start(bf16[32,3584]{1,0:T(8,128)(2,1)S(1)} %slice.24), channel_id=1, source_target_pairs={{0,2},{1,3},{2,0},{3,1},{4,6},{5,7},{6,4},{7,5},{8,10},{9,11},{10,... | collective-permute-start | bytes 688136 | tf_op jit(solution)/shard_map/ppermute | solution.py:16
  57.4 9.6 %collective-permute-start.14 = (bf16[32,3584]{1,0:T(8,128)(2,1)S(1)}, bf16[32,3584]{1,0:T(8,128)(2,1)S(1)}, u32[]{:S(2)}, u32[]{:S(2)}) collective-permute-start(bf16[32,3584]{1,0:T(8,128)(2,1)S(1)} %slice.25), channel_id=1, source_target_pairs={{0,4},{4,8},{8,12},{12,0},{1,5},{5,9},{9,13},{13,1},{2,6},{6,10},{... | collective-permute-start | bytes 688136 | tf_op jit(solution)/shard_map/ppermute | solution.py:212
  59.1 7.9 %collective-permute-start.15 = (bf16[32,3584]{1,0:T(8,128)(2,1)S(1)}, bf16[32,3584]{1,0:T(8,128)(2,1)S(1)}, u32[]{:S(2)}, u32[]{:S(2)}) collective-permute-start(bf16[32,3584]{1,0:T(8,128)(2,1)S(1)} %get-tuple-element.64), channel_id=1, source_target_pairs={{0,2},{1,3},{2,0},{3,1},{4,6},{5,7},{6,4},{7,5},{8,10},{9,11},{10,... | collective-permute-start | bytes 688136 | tf_op jit(solution)/shard_map/ppermute | solution.py:16
  59.7 8.5 %collective-permute-start.16 = (bf16[32,3584]{1,0:T(8,128)(2,1)S(1)}, bf16[32,3584]{1,0:T(8,128)(2,1)S(1)}, u32[]{:S(2)}, u32[]{:S(2)}) collective-permute-start(bf16[32,3584]{1,0:T(8,128)(2,1)S(1)} %get-tuple-element.63), channel_id=1, source_target_pairs={{0,4},{4,8},{8,12},{12,0},{1,5},{5,9},{9,13},{13,1},{2,6},{6,10},{... | collective-permute-start | bytes 688136 | tf_op jit(solution)/shard_map/ppermute | solution.py:212
  68.3 12.8 %collective-permute-start.18 = (bf16[64,3584]{1,0:T(8,128)(2,1)S(1)}, bf16[64,3584]{1,0:T(8,128)(2,1)S(1)}, u32[]{:S(2)}, u32[]{:S(2)}) collective-permute-start(bf16[64,3584]{1,0:T(8,128)(2,1)S(1)} %pad_maximum_fusion.1), channel_id=1, source_target_pairs={{0,4},{4,8},{8,12},{12,0},{1,5},{5,9},{9,13},{13,1},{2,6},{6,10},{... | collective-permute-start | bytes 1376264 | tf_op jit(solution)/shard_map/ppermute | solution.py:212
  70.3 10.8 %collective-permute-start.17 = (bf16[64,3584]{1,0:T(8,128)(2,1)}, bf16[64,3584]{1,0:T(8,128)(2,1)S(1)}, u32[]{:S(2)}, u32[]{:S(2)}) collective-permute-start(bf16[64,3584]{1,0:T(8,128)(2,1)} %pad_maximum_fusion), channel_id=1, source_target_pairs={{0,2},{1,3},{2,0},{3,1},{4,6},{5,7},{6,4},{7,5},{8,10},{9,11},{10,... | collective-permute-start | bytes 1376264 | tf_op jit(solution)/shard_map/ppermute | solution.py:16
  71.9 2.0 %copy-start.1 = (bf16[1,3584,512]{2,1,0:T(8,128)(2,1)S(1)}, bf16[1,3584,512]{2,1,0:T(8,128)(2,1)}, u32[]{:S(2)}) copy-start(bf16[1,3584,512]{2,1,0:T(8,128)(2,1)} %refs_3_.3) | copy-start | bytes 11010052
  73.9 9.4 %copy-start.4 = (bf16[64,3584]{1,0:T(8,128)(2,1)S(1)}, bf16[64,3584]{1,0:T(8,128)(2,1)}, u32[]{:S(2)}) copy-start(bf16[64,3584]{1,0:T(8,128)(2,1)} %copy-done.3) | copy-start | bytes 1376260
  81.3 11.2 %collective-permute-start.20 = (bf16[64,3584]{1,0:T(8,128)(2,1)S(1)}, bf16[64,3584]{1,0:T(8,128)(2,1)S(1)}, u32[]{:S(2)}, u32[]{:S(2)}) collective-permute-start(bf16[64,3584]{1,0:T(8,128)(2,1)S(1)} %add_convert_fusion.2), channel_id=1, source_target_pairs={{0,4},{4,8},{8,12},{12,0},{1,5},{5,9},{9,13},{13,1},{2,6},{6,10},{... | collective-permute-start | bytes 1376264 | tf_op jit(solution)/shard_map/ppermute | solution.py:212
  82.3 12.2 %collective-permute-start.19 = (bf16[64,3584]{1,0:T(8,128)(2,1)S(1)}, bf16[64,3584]{1,0:T(8,128)(2,1)S(1)}, u32[]{:S(2)}, u32[]{:S(2)}) collective-permute-start(bf16[64,3584]{1,0:T(8,128)(2,1)S(1)} %shard_map.66), channel_id=1, source_target_pairs={{0,2},{1,3},{2,0},{3,1},{4,6},{5,7},{6,4},{7,5},{8,10},{9,11},{10,... | collective-permute-start | bytes 1376264 | tf_op jit(solution)/shard_map/ppermute | solution.py:16
  83.4 16.0 %collective-permute-start.12 = (bf16[64,3584]{1,0:T(8,128)(2,1)S(1)}, bf16[64,3584]{1,0:T(8,128)(2,1)S(1)}, u32[]{:S(2)}, u32[]{:S(2)}) collective-permute-start(bf16[64,3584]{1,0:T(8,128)(2,1)S(1)} %copy-done.4), channel_id=1, source_target_pairs={{0,2},{1,3},{2,0},{3,1},{4,6},{5,7},{6,4},{7,5},{8,10},{9,11},{10,... | collective-permute-start | bytes 1376264 | tf_op jit(solution)/shard_map/ppermute | solution.py:16
  94.7 10.3 %collective-permute-start.21 = (bf16[64,3584]{1,0:T(8,128)(2,1)S(1)}, bf16[64,3584]{1,0:T(8,128)(2,1)S(1)}, u32[]{:S(2)}, u32[]{:S(2)}) collective-permute-start(bf16[64,3584]{1,0:T(8,128)(2,1)S(1)} %add_convert_fusion.1), channel_id=1, source_target_pairs={{0,4},{4,8},{8,12},{12,0},{1,5},{5,9},{9,13},{13,1},{2,6},{6,10},{... | collective-permute-start | bytes 1376264 | tf_op jit(solution)/shard_map/ppermute | solution.py:212

commit v3 on v2

--- a/solution.py
+++ b/solution.py
@@ -106,13 +106,42 @@
     combined = jnp.einsum("gsb,gsd->bd", one_hot, gathered_back, preferred_element_type=jnp.float32)
     return combined.astype(jnp.bfloat16)
 
-def expert_kernel(counts, down_tiles, hidden_tile, *refs):
-    taken, given = counts
-    blocks, scores, weights = refs[:taken], refs[taken], refs[taken + 1 : taken + 7]
-    outs = refs[taken + 7 : taken + 7 + given]
-    rows_all, gate, up, down, hidden, sems = refs[taken + 7 + given :]
-    width = rows_all.shape[1]
-    half = gate.shape[-1]
+LANES = 128
+
+
+def pack_kernel(tokens, expert_ids, gate_scores, *packed):
+    rows, width = tokens.shape
+    lane = lax.broadcasted_iota(jnp.int32, (LANES, rows), 0)
+    found = jnp.zeros((LANES, rows), jnp.float32)
+    for k in range(expert_ids.shape[0]):
+        score = gate_scores[k : k + 1, :].astype(jnp.float32)
+        found += jnp.where(lane == expert_ids[k : k + 1, :], score, 0.0)
+    factors = found.T.astype(jnp.bfloat16)
+    at = 0
+    for out in packed:
+        piece = out.shape[0]
+        out[:, :width] = tokens[at : at + piece, :]
+        out[:, width:] = factors[at : at + piece]
+        at += piece
+
+
+def pack(tokens, expert_ids, gate_scores, pieces):
+    rows, width = tokens.shape
+    vmem = pl.BlockSpec(memory_space=pltpu.VMEM)
+    shape = jax.ShapeDtypeStruct((rows // pieces, width + LANES), tokens.dtype)
+    return pl.pallas_call(
+        pack_kernel,
+        out_shape=[shape] * pieces,
+        in_specs=[vmem] * 3,
+        out_specs=[vmem] * pieces,
+    )(tokens, expert_ids.T, gate_scores.T)
+
+
+def expert_kernel(taken, down_tiles, hidden_tile, mine, *refs):
+    blocks, weights, outs = refs[:taken], refs[taken : taken + 6], refs[taken + 6 : -6]
+    rows_all, gate, up, down, hidden, sems = refs[-6:]
+    width = down.shape[2]
+    half = gate.shape[2]
     started = []
 
     def fetch(source, target):
@@ -142,40 +171,42 @@
     for block in blocks:
         rows_all[pl.ds(at, block.shape[0]), :] = block[...]
         at += block.shape[0]
+    lane = lax.broadcasted_iota(jnp.int32, (at, LANES), 1)
+    factors = rows_all[:, width:].astype(jnp.float32)
+    factor = jnp.sum(jnp.where(lane == mine[0], factors, 0.0), axis=1, keepdims=True)
     for side, cols, pair in first:
         for copy in pair:
             copy.wait()
-        gate_act = jnp.dot(rows_all[...], gate[side, :, cols], preferred_element_type=jnp.float32)
-        up_act = jnp.dot(rows_all[...], up[side, :, cols], preferred_element_type=jnp.float32)
+        rows = rows_all[:, :width]
+        gate_act = jnp.dot(rows, gate[side, :, cols], preferred_element_type=jnp.float32)
+        up_act = jnp.dot(rows, up[side, :, cols], preferred_element_type=jnp.float32)
         hidden[side, :, cols] = (jax.nn.silu(gate_act) * up_act).astype(jnp.bfloat16)
     for cols, pair in second:
         for copy in pair:
             copy.wait()
         result = jnp.dot(hidden[0], down[0, :, cols], preferred_element_type=jnp.float32)
         result += jnp.dot(hidden[1], down[1, :, cols], preferred_element_type=jnp.float32)
-        result = (result * scores[...]).astype(jnp.bfloat16)
+        result = (result * factor).astype(jnp.bfloat16)
         at = 0
         for out in outs:
             out[:, cols] = result[at : at + out.shape[0]]
             at += out.shape[0]
 
 
-def expert_rows(blocks, scores, own, other, out_rows):
-    width = blocks[0].shape[1]
-    half = own[0].shape[-1]
+def expert_rows(blocks, mine, own, other, out_rows):
+    half, width = own[2].shape[1:]
     total = sum(block.shape[0] for block in blocks)
-    given = total // out_rows
     down_tiles = 4
     hidden_tile = half // 2
     vmem = pl.BlockSpec(memory_space=pltpu.VMEM)
     anywhere = pl.BlockSpec(memory_space=pl.ANY)
     return pl.pallas_call(
-        functools.partial(expert_kernel, (len(blocks), given), down_tiles, hidden_tile),
-        out_shape=[jax.ShapeDtypeStruct((out_rows, width), jnp.bfloat16)] * given,
-        in_specs=[vmem] * (len(blocks) + 1) + [anywhere] * 6,
-        out_specs=[vmem] * given,
+        functools.partial(expert_kernel, len(blocks), down_tiles, hidden_tile),
+        out_shape=[jax.ShapeDtypeStruct((rows, width), jnp.bfloat16) for rows in out_rows],
+        in_specs=[pl.BlockSpec(memory_space=pltpu.SMEM)] + [vmem] * len(blocks) + [anywhere] * 6,
+        out_specs=[vmem] * len(out_rows),
         scratch_shapes=[
-            pltpu.VMEM((total, width), jnp.bfloat16),
+            pltpu.VMEM((total, width + LANES), jnp.bfloat16),
             pltpu.VMEM((2, width, half), jnp.bfloat16),
             pltpu.VMEM((2, width, half), jnp.bfloat16),
             pltpu.VMEM((2, half, width), jnp.bfloat16),
@@ -188,7 +219,7 @@
             bytes_accessed=12 * width * half + 4 * total * width,
             transcendentals=2 * total * half,
         ),
-    )(*blocks, scores, *own, *other)
+    )(mine, *blocks, *own, *other)
 
 
 def added(*terms):
@@ -197,12 +228,18 @@
 
 def together(*values):
     return lax.optimization_barrier(values)
+
+
+def after(value, *others):
+    for other in others:
+        same = other if other.shape == value.shape else other[:, :1]
+        value = jnp.where(same == same, value, same)
+    return value
 
 
 def dense(tokens, expert_ids, gate_scores, gate_weight, up_weight, down_weight):
     node_count = lax.axis_size("node")
     local_count = lax.axis_size("local")
-    node, local = lax.axis_index("node"), lax.axis_index("local")
     rows = tokens.shape[0]
     split = rows // 2
     last = node_count - 1
@@ -214,72 +251,40 @@
     def other_x(value):
         return partner(value, "local", 1)
 
+    mine = lax.axis_index("node") * (local_count // 2) + lax.axis_index("local") // 2
+    mine = jnp.full((1,), mine, jnp.int32)
     own = (gate_weight, up_weight, down_weight)
     other = tuple(partner(weight, "local", 0) for weight in own)
 
-    experts = jnp.arange(node_count * (local_count // 2))
-    named = expert_ids[:, :, None] == experts[None, None, :]
-    factors = jnp.sum(jnp.where(named, gate_scores[:, :, None], 0), axis=1).astype(jnp.bfloat16)
-    factors = jnp.stack([factors, other_x(factors)])
-    bit = 0
-    while 2**bit < node_count:
-        factors = jnp.concatenate([factors, partner(factors, "node", bit)])
-        bit += 1
-    mine = node * (local_count // 2) + local // 2
-    factors = lax.dynamic_index_in_dim(factors, mine, 2, keepdims=True).astype(jnp.float32)
-
-    def factor_of(kind, slot):
-        source = lax.rem(node - slot + node_count, node_count)
-        at = 2 * (source ^ node) + (0 if kind == "a" else 1)
-        return lax.dynamic_index_in_dim(factors, at, 0, keepdims=False)
-
-    done = {}
-
-    def work(keys, parts=None):
-        blocks = parts or [(along if kind == "a" else across)[slot] for kind, slot in keys]
-        scores = jnp.concatenate([factor_of(*key) for key in keys])
-        results = expert_rows(blocks, scores, own, other, rows)
-        done.update(zip(keys, results))
-        return results
-
-    def hold(keys, *values):
-        held = together(*values, *[done[key] for key in keys])
-        done.update(zip(keys, held[len(values) :]))
-        return held[: len(values)]
-
-    along, across = [tokens], []
-    early = [("a", 0)] + [(kind, slot) for slot in range(1, last) for kind in "ax"]
-    early = [("a", 0)]
-    for slot in range(1, last):
-        early += [("a", slot), ("x", slot - 1)]
+    along, across = list(pack(tokens, expert_ids, gate_scores, 1)), []
     for slot in range(last):
-        moved, crossed = next_node(along[slot]), other_x(along[slot])
+        crossed, moved = other_x(along[slot]), next_node(along[slot])
         if slot < last - 1:
-            moved, crossed = together(moved, crossed)
-        else:
-            work(early)
-            moved, crossed = hold(early, moved, crossed)
+            moved = after(moved, crossed)
         along.append(moved)
         across.append(crossed)
-    upper, lower = other_x(along[last][:split]), next_node(across[last - 1][split:])
-    middle = [("a", last), ("x", last - 1)]
-    work(middle)
-    upper, lower = hold(middle, upper, lower)
-
-    crossed, passed = together(other_x(done["x", 1][:split]), next_node(done["x", 1][split:]))
-    second = done["x", 2]
-    done["x", 2] = jnp.concatenate([second[:split], added(second[split:], passed)])
-    first = done["a", 1]
+    early = along[:last] + across[: last - 1]
+    sizes = [rows] * last + [rows, split, split] + [rows] * (last - 3)
+    results = list(expert_rows(early, mine, own, other, sizes))
+    at_home, away = results[:last], [results[last], None] + results[last + 3 :]
+    first_upper, first_lower = results[last + 1 : last + 3]
+    upper = other_x(after(along[last][:split], first_upper))
+    lower = next_node(after(across[last - 1][split:], first_lower))
+    middle = expert_rows([along[last], across[last - 1]], mine, own, other, [rows, rows])
+    at_home.append(middle[0])
+
+    crossed, passed = other_x(first_upper), next_node(first_lower)
+    second = [after(middle[1][:split], upper, lower), added(middle[1][split:], passed)]
+    away.append(jnp.concatenate(second))
+    away += expert_rows([upper, lower], mine, own, other, [rows])
+    first = at_home[1]
     running = jnp.concatenate([added(first[:split], crossed), first[split:]])
     for slot in list(range(2, node_count)) + [0]:
-        crossed, moved = other_x(done["x", slot]), next_node(running)
-        if slot == 2:
-            late = [("x", last)]
-            work(late, [upper, lower])
-            crossed, moved = hold(late, crossed, moved)
-        elif slot:
-            crossed, moved = together(crossed, moved)
-        running = added(done["a", slot], crossed, moved)
+        crossed, moved = other_x(away[slot]), next_node(running)
+        running = added(at_home[slot], crossed, moved)
+        if slot:
+            following = (slot + 1) % node_count
+            away[following] = after(away[following], crossed)
     return running
 
 

time: 106 us -> 97.1 us (0.916)
  starting transfers between devices: 24.9 us -> 20 us
  waiting for transfers between devices: 48.9 us -> 45.6 us
  local copies, waits for them, and re-layouts: 3.63 us -> 1.48 us
  Pallas kernels: 25.3 us -> 27.2 us
    ppermute x8, waiting for transfers between devices: 27.1 us -> 11.2 us  [next_node(): return lax.ppermute(value, 'node', pairs)]
    ppermute x14 -> x11, waiting for transfers between devices: 21.8 us -> 34.4 us  [partner(): return lax.ppermute(value, axis, pairs)]
    ppermute x14 -> x11, starting transfers between devices: 14.1 us -> 10.8 us  [partner(): return lax.ppermute(value, axis, pairs)]
    unnamed x10 -> x4, local copies, waits for them, and re-layouts: 3.06 us -> 1.02 us
    pallas_call x3 -> x4, Pallas kernels: 25.3 us -> 27.2 us  [the longest x3 25.3 us: expert_rows(): pl.pallas_call(functools.partial(expert_kernel, len(blocks), down_tiles,...]
    ppermute x8, starting transfers between devices: 10.8 us -> 9.22 us  [next_node(): return lax.ppermute(value, 'node', pairs)]
  transfers between devices with their start and end apart: 22 -> 19, of which waited for: 9 -> 10; matrix products, arithmetic and copies ran while one was open for 2% -> 2% of each run, Pallas kernels for 24% -> 28%
where the time goes in v3:
time: 97.1 us; the launch traced here: 96.9 us
  waiting for transfers between devices  45.6 us (47%)
  Pallas kernels  27.2 us (28%)
  starting transfers between devices  20 us (21%)
  other arithmetic  2.43 us (3%)
  local copies, waits for them, and re-layouts  1.48 us (2%)
    ppermute x11, waiting for transfers between devices, partner(): return lax.ppermute(value, axis, pairs)  34.4 us
    pallas_call x3, Pallas kernels, expert_rows(): pl.pallas_call(functools.partial(expert_kernel, len(blocks), down_tiles,...  25.3 us
    ppermute x8, waiting for transfers between devices, next_node(): return lax.ppermute(value, 'node', pairs)  11.2 us
    ppermute x11, starting transfers between devices, partner(): return lax.ppermute(value, axis, pairs)  10.8 us
    ppermute x8, starting transfers between devices, next_node(): return lax.ppermute(value, 'node', pairs)  9.22 us
  transfers between devices with their start and end apart: 19, of which 10 were waited for; matrix products, arithmetic and copies ran while one was open for 2% of the time, Pallas kernels for 28%

profile of v3, /device:TPU:0, one launch (start us, length us, event | category | flops | bytes accessed | tf_op | source)
XLA Modules:
  0.0 96.9 jit_solution(15206853480819105573)
XLA Ops:
  0.0 0.5 collective-permute-start.4
  0.5 0.5 collective-permute-start.6
  1.0 1.9 %shard_map.64.refs_0_ = bf16[64,3712]{1,0:T(8,128)(2,1)} custom-call(bf16[64,3584]{1,0:T(8,128)(2,1)} %tokens.1, s32[8,64]{1,0:T(8,128)} %bitcast.3, bf16[8,64]{1,0:T(8,128)(2,1)} %bitcast.4), custom_call_target="tpu_custom_call" | custom-call | tf_op jit(solution)/shard_map/pallas_call | solution.py:132
  2.9 2.5 %collective-permute-start = (bf16[64,3712]{1,0:T(8,128)(2,1)}, bf16[64,3712]{1,0:T(8,128)(2,1)S(1)}, u32[]{:S(2)}, u32[]{:S(2)}) collective-permute-start(bf16[64,3712]{1,0:T(8,128)(2,1)} %shard_map.64.refs_0_), channel_id=1, source_target_pairs={{0,2},{1,3},{2,0},{3,1},{4,6},{5,7},{6,4},{7,5},{8,10},{9,11},{10,... | collective-permute-start | bytes 1425416 | tf_op jit(solution)/shard_map/ppermute | solution.py:16
  5.4 1.6 %collective-permute-start.1 = (bf16[64,3712]{1,0:T(8,128)(2,1)}, bf16[64,3712]{1,0:T(8,128)(2,1)S(1)}, u32[]{:S(2)}, u32[]{:S(2)}) collective-permute-start(bf16[64,3712]{1,0:T(8,128)(2,1)} %shard_map.64.refs_0_), channel_id=1, source_target_pairs={{0,4},{4,8},{8,12},{12,0},{1,5},{5,9},{9,13},{13,1},{2,6},{6,10},{... | collective-permute-start | bytes 1425416 | tf_op jit(solution)/shard_map/ppermute | solution.py:249
  7.0 10.2 %collective-permute-done.refs_3_ = bf16[64,3712]{1,0:T(8,128)(2,1)S(1)} collective-permute-done((bf16[64,3712]{1,0:T(8,128)(2,1)}, bf16[64,3712]{1,0:T(8,128)(2,1)S(1)}, u32[]{:S(2)}, u32[]{:S(2)}) %collective-permute-start) | collective-permute-done | bytes 475168 | tf_op jit(solution)/shard_map/ppermute | solution.py:16
  17.1 3.4 %collective-permute-done.1 = bf16[64,3712]{1,0:T(8,128)(2,1)S(1)} collective-permute-done((bf16[64,3712]{1,0:T(8,128)(2,1)}, bf16[64,3712]{1,0:T(8,128)(2,1)S(1)}, u32[]{:S(2)}, u32[]{:S(2)}) %collective-permute-start.1) | collective-permute-done | bytes 475168 | tf_op jit(solution)/shard_map/ppermute | solution.py:249
  20.5 0.1 compare_select_fusion.1.refs_1_
  20.6 0.6 collective-permute-start.2
  21.2 11.7 %collective-permute-done.2.refs_4_ = bf16[64,3712]{1,0:T(8,128)(2,1)S(1)} collective-permute-done((bf16[64,3712]{1,0:T(8,128)(2,1)S(1)}, bf16[64,3712]{1,0:T(8,128)(2,1)S(1)}, u32[]{:S(2)}, u32[]{:S(2)}) %collective-permute-start.2) | collective-permute-done | bytes 475168 | tf_op jit(solution)/shard_map/ppermute | solution.py:16
  32.9 2.3 %collective-permute-done.3 = bf16[64,3712]{1,0:T(8,128)(2,1)S(1)} collective-permute-done((bf16[64,3712]{1,0:T(8,128)(2,1)S(1)}, bf16[64,3712]{1,0:T(8,128)(2,1)S(1)}, u32[]{:S(2)}, u32[]{:S(2)}) %collective-permute-start.3) | collective-permute-done | bytes 475168 | tf_op jit(solution)/shard_map/ppermute | solution.py:249
  35.2 0.1 compare_select_fusion.refs_2_
  35.2 1.3 %collective-permute-start.7 = (bf16[64,3712]{1,0:T(8,128)(2,1)S(1)}, bf16[64,3712]{1,0:T(8,128)(2,1)S(1)}, u32[]{:S(2)}, u32[]{:S(2)}) collective-permute-start(bf16[64,3712]{1,0:T(8,128)(2,1)S(1)} %compare_select_fusion.refs_2_), channel_id=1, source_target_pairs={{0,2},{1,3},{2,0},{3,1},{4,6},{5,7},{6,4},{7,5},{8,10},{9,11},{10,... | collective-permute-start | bytes 1425416 | tf_op jit(solution)/shard_map/ppermute | solution.py:16
  36.6 1.0 %copy-done.1 = bf16[64,3712]{1,0:T(8,128)(2,1)S(1)} copy-done((bf16[64,3712]{1,0:T(8,128)(2,1)S(1)}, bf16[64,3712]{1,0:T(8,128)(2,1)}, u32[]{:S(2)}) %copy-start.1) | copy-done | bytes 475160
  37.6 11.2 %shard_map.65 = (bf16[64,3584]{1,0:T(8,128)(2,1)S(1)}, bf16[64,3584]{1,0:T(8,128)(2,1)S(1)}, bf16[64,3584]{1,0:T(8,128)(2,1)S(1)}, bf16[64,3584]{1,0:T(8,128)(2,...) custom-call(s32[1]{0:T(128)} %bitcast.mine, bf16[64,3712]{1,0:T(8,128)(2,1)S(1)} %copy-done.1, ...), custom_call_target="tpu_custom_call" | custom-call | flops 7046430720 | bytes 26607616 | tf_op jit(solution)/shard_map/pallas_call | solution.py:203
  48.8 0.1 collective-permute-start.11
  48.9 0.1 slice_reduce_fusion.3
  49.0 0.1 compare_reduce_fusion.3
  49.1 0.1 slice_select_fusion.1
  49.2 1.0 collective-permute-start.8
  50.2 0.6 collective-permute-start.15
  50.8 0.1 slice_reduce_fusion.2
  50.9 0.1 compare_reduce_fusion.1
  51.0 0.1 slice_select_fusion
  51.1 1.5 %collective-permute-start.10 = (bf16[32,3712]{1,0:T(8,128)(2,1)S(1)}, bf16[32,3712]{1,0:T(8,128)(2,1)S(1)}, u32[]{:S(2)}, u32[]{:S(2)}) collective-permute-start(bf16[32,3712]{1,0:T(8,128)(2,1)S(1)} %slice_select_fusion), channel_id=1, source_target_pairs={{0,2},{1,3},{2,0},{3,1},{4,6},{5,7},{6,4},{7,5},{8,10},{9,11},{10,... | collective-permute-start | bytes 712712 | tf_op jit(solution)/shard_map/ppermute | solution.py:16
  52.6 7.0 %shard_map.66 = (bf16[64,3584]{1,0:T(8,128)(2,1)S(1)}, bf16[64,3584]{1,0:T(8,128)(2,1)S(1)}) custom-call(s32[1]{0:T(128)} %bitcast.mine, bf16[64,3712]{1,0:T(8,128)(2,1)S(1)} %collective-permute-done.9.refs_0_, bf16[64,3712]{1,0:T(8,128)(2,1)S(1)} %collective-permute-done.7.refs_1_, bf16[1,3584,512]{2,1,0:T(8,128)(2,1)S(1)} %copy-done, ...), custom_call_target="tpu_custom_call" | custom-call | flops 2818572288 | bytes 23855104 | tf_op jit(solution)/shard_map/pallas_call | solution.py:203
  59.7 0.1 add_convert_fusion.4
  59.8 1.5 %collective-permute-done.8.refs_1_ = bf16[32,3712]{1,0:T(8,128)(2,1)S(1)} collective-permute-done((bf16[32,3712]{1,0:T(8,128)(2,1)S(1)}, bf16[32,3712]{1,0:T(8,128)(2,1)S(1)}, u32[]{:S(2)}, u32[]{:S(2)}) %collective-permute-start.8) | collective-permute-done | bytes 237600 | tf_op jit(solution)/shard_map/ppermute | solution.py:249
  61.3 0.1 slice_reduce_fusion.1
  61.4 0.1 compare_reduce_fusion.2
  61.5 0.1 compare_reduce_fusion
  61.6 0.1 slice_reduce_fusion
  61.8 0.1 select_select_fusion
  61.9 1.0 %collective-permute-start.12 = (bf16[64,3584]{1,0:T(8,128)(2,1)S(1)}, bf16[64,3584]{1,0:T(8,128)(2,1)S(1)}, u32[]{:S(2)}, u32[]{:S(2)}) collective-permute-start(bf16[64,3584]{1,0:T(8,128)(2,1)S(1)} %pad_maximum_fusion), channel_id=1, source_target_pairs={{0,2},{1,3},{2,0},{3,1},{4,6},{5,7},{6,4},{7,5},{8,10},{9,11},{10,... | collective-permute-start | bytes 1376264 | tf_op jit(solution)/shard_map/ppermute | solution.py:16
  63.0 2.9 %collective-permute-start.16 = (bf16[64,3584]{1,0:T(8,128)(2,1)S(1)}, bf16[64,3584]{1,0:T(8,128)(2,1)S(1)}, u32[]{:S(2)}, u32[]{:S(2)}) collective-permute-start(bf16[64,3584]{1,0:T(8,128)(2,1)S(1)} %pad_maximum_fusion.1), channel_id=1, source_target_pairs={{0,4},{4,8},{8,12},{12,0},{1,5},{5,9},{9,13},{13,1},{2,6},{6,10},{... | collective-permute-start | bytes 1376264 | tf_op jit(solution)/shard_map/ppermute | solution.py:249
  65.9 7.1 %shard_map.67 = bf16[64,3584]{1,0:T(8,128)(2,1)S(1)} custom-call(s32[1]{0:T(128)} %bitcast.mine, bf16[32,3712]{1,0:T(8,128)(2,1)S(1)} %collective-permute-done.10.refs_0_, bf16[32,3712]{1,0:T(8,128)(2,1)S(1)} %collective-permute-done.8.refs_1_, bf16[1,3584,512]{2,1,0:T(8,128)(2,1)S(1)} %copy-done, bf16[1,3584,512]{2,1,0:T(8,128)(2,1)} %refs_3_.3, ...), custom_call_target="tpu_custom_call" | custom-call | flops 1409286144 | bytes 22937600 | tf_op jit(solution)/shard_map/pallas_call | solution.py:203
  73.0 1.1 %collective-permute-start.13 = (bf16[64,3584]{1,0:T(8,128)(2,1)S(1)}, bf16[64,3584]{1,0:T(8,128)(2,1)S(1)}, u32[]{:S(2)}, u32[]{:S(2)}) collective-permute-start(bf16[64,3584]{1,0:T(8,128)(2,1)S(1)} %compare_select_fusion.3), channel_id=1, source_target_pairs={{0,2},{1,3},{2,0},{3,1},{4,6},{5,7},{6,4},{7,5},{8,10},{9,11},{10,... | collective-permute-start | bytes 1376264 | tf_op jit(solution)/shard_map/ppermute | solution.py:16
  74.2 0.3 collective-permute-done.16
  74.5 0.2 add_convert_fusion.2
  74.7 1.8 %collective-permute-start.17 = (bf16[64,3584]{1,0:T(8,128)(2,1)S(1)}, bf16[64,3584]{1,0:T(8,128)(2,1)S(1)}, u32[]{:S(2)}, u32[]{:S(2)}) collective-permute-start(bf16[64,3584]{1,0:T(8,128)(2,1)S(1)} %add_convert_fusion.2), channel_id=1, source_target_pairs={{0,4},{4,8},{8,12},{12,0},{1,5},{5,9},{9,13},{13,1},{2,6},{6,10},{... | collective-permute-start | bytes 1376264 | tf_op jit(solution)/shard_map/ppermute | solution.py:249
  76.5 7.5 %collective-permute-done.13 = bf16[64,3584]{1,0:T(8,128)(2,1)S(1)} collective-permute-done((bf16[64,3584]{1,0:T(8,128)(2,1)S(1)}, bf16[64,3584]{1,0:T(8,128)(2,1)S(1)}, u32[]{:S(2)}, u32[]{:S(2)}) %collective-permute-start.13) | collective-permute-done | bytes 458784 | tf_op jit(solution)/shard_map/ppermute | solution.py:16
  84.0 1.1 %collective-permute-start.14 = (bf16[64,3584]{1,0:T(8,128)(2,1)S(1)}, bf16[64,3584]{1,0:T(8,128)(2,1)S(1)}, u32[]{:S(2)}, u32[]{:S(2)}) collective-permute-start(bf16[64,3584]{1,0:T(8,128)(2,1)S(1)} %compare_select_fusion.2), channel_id=1, source_target_pairs={{0,2},{1,3},{2,0},{3,1},{4,6},{5,7},{6,4},{7,5},{8,10},{9,11},{10,... | collective-permute-start | bytes 1376264 | tf_op jit(solution)/shard_map/ppermute | solution.py:16
  85.1 0.3 collective-permute-done.17
  85.5 0.2 add_convert_fusion.1
  85.6 1.9 %collective-permute-start.18 = (bf16[64,3584]{1,0:T(8,128)(2,1)S(1)}, bf16[64,3584]{1,0:T(8,128)(2,1)S(1)}, u32[]{:S(2)}, u32[]{:S(2)}) collective-permute-start(bf16[64,3584]{1,0:T(8,128)(2,1)S(1)} %add_convert_fusion.1), channel_id=1, source_target_pairs={{0,4},{4,8},{8,12},{12,0},{1,5},{5,9},{9,13},{13,1},{2,6},{6,10},{... | collective-permute-start | bytes 1376264 | tf_op jit(solution)/shard_map/ppermute | solution.py:249
  87.5 5.0 %collective-permute-done.14 = bf16[64,3584]{1,0:T(8,128)(2,1)S(1)} collective-permute-done((bf16[64,3584]{1,0:T(8,128)(2,1)S(1)}, bf16[64,3584]{1,0:T(8,128)(2,1)S(1)}, u32[]{:S(2)}, u32[]{:S(2)}) %collective-permute-start.14) | collective-permute-done | bytes 458784 | tf_op jit(solution)/shard_map/ppermute | solution.py:16
  92.6 3.4 %collective-permute-done.18 = bf16[64,3584]{1,0:T(8,128)(2,1)S(1)} collective-permute-done((bf16[64,3584]{1,0:T(8,128)(2,1)S(1)}, bf16[64,3584]{1,0:T(8,128)(2,1)S(1)}, u32[]{:S(2)}, u32[]{:S(2)}) %collective-permute-start.18) | collective-permute-done | bytes 458784 | tf_op jit(solution)/shard_map/ppermute | solution.py:249
  96.0 0.9 add_convert_fusion
  (21 shorter events, 0.3 us)
Async XLA Ops:
  0.0 36.6 %collective-permute-start.4 = (bf16[1,3584,512]{2,1,0:T(8,128)(2,1)}, bf16[1,3584,512]{2,1,0:T(8,128)(2,1)}, u32[]{:S(2)}, u32[]{:S(2)}) collective-permute-start(bf16[1,3584,512]{2,1,0:T(8,128)(2,1)} %refs_2_.3), channel_id=1, source_target_pairs={{0,1},{1,0},{2,3},{3,2},{4,5},{5,4},{6,7},{7,6},{8,9},{9,8},{10,11... | collective-permute-start | bytes 11010056 | tf_op jit(solution)/shard_map/ppermute | solution.py:16
  0.5 36.1 %collective-permute-start.5 = (bf16[1,3584,512]{2,1,0:T(8,128)(2,1)}, bf16[1,3584,512]{2,1,0:T(8,128)(2,1)}, u32[]{:S(2)}, u32[]{:S(2)}) collective-permute-start(bf16[1,3584,512]{2,1,0:T(8,128)(2,1)} %refs_3_.3), channel_id=1, source_target_pairs={{0,1},{1,0},{2,3},{3,2},{4,5},{5,4},{6,7},{7,6},{8,9},{9,8},{10,11... | collective-permute-start | bytes 11010056 | tf_op jit(solution)/shard_map/ppermute | solution.py:16
  0.5 36.1 %collective-permute-start.6 = (bf16[1,512,3584]{2,1,0:T(8,128)(2,1)}, bf16[1,512,3584]{2,1,0:T(8,128)(2,1)}, u32[]{:S(2)}, u32[]{:S(2)}) collective-permute-start(bf16[1,512,3584]{2,1,0:T(8,128)(2,1)} %refs_4_.3), channel_id=1, source_target_pairs={{0,1},{1,0},{2,3},{3,2},{4,5},{5,4},{6,7},{7,6},{8,9},{9,8},{10,11... | collective-permute-start | bytes 11010056 | tf_op jit(solution)/shard_map/ppermute | solution.py:16
  2.9 14.2 %collective-permute-start = (bf16[64,3712]{1,0:T(8,128)(2,1)}, bf16[64,3712]{1,0:T(8,128)(2,1)S(1)}, u32[]{:S(2)}, u32[]{:S(2)}) collective-permute-start(bf16[64,3712]{1,0:T(8,128)(2,1)} %shard_map.64.refs_0_), channel_id=1, source_target_pairs={{0,2},{1,3},{2,0},{3,1},{4,6},{5,7},{6,4},{7,5},{8,10},{9,11},{10,... | collective-permute-start | bytes 1425416 | tf_op jit(solution)/shard_map/ppermute | solution.py:16
  5.4 15.1 %collective-permute-start.1 = (bf16[64,3712]{1,0:T(8,128)(2,1)}, bf16[64,3712]{1,0:T(8,128)(2,1)S(1)}, u32[]{:S(2)}, u32[]{:S(2)}) collective-permute-start(bf16[64,3712]{1,0:T(8,128)(2,1)} %shard_map.64.refs_0_), channel_id=1, source_target_pairs={{0,4},{4,8},{8,12},{12,0},{1,5},{5,9},{9,13},{13,1},{2,6},{6,10},{... | collective-permute-start | bytes 1425416 | tf_op jit(solution)/shard_map/ppermute | solution.py:249
  20.6 12.4 %collective-permute-start.2 = (bf16[64,3712]{1,0:T(8,128)(2,1)S(1)}, bf16[64,3712]{1,0:T(8,128)(2,1)S(1)}, u32[]{:S(2)}, u32[]{:S(2)}) collective-permute-start(bf16[64,3712]{1,0:T(8,128)(2,1)S(1)} %compare_select_fusion.1.refs_1_), channel_id=1, source_target_pairs={{0,2},{1,3},{2,0},{3,1},{4,6},{5,7},{6,4},{7,5},{8,10},{9,11},{10,... | collective-permute-start | bytes 1425416 | tf_op jit(solution)/shard_map/ppermute | solution.py:16
  21.2 14.0 %collective-permute-start.3 = (bf16[64,3712]{1,0:T(8,128)(2,1)S(1)}, bf16[64,3712]{1,0:T(8,128)(2,1)S(1)}, u32[]{:S(2)}, u32[]{:S(2)}) collective-permute-start(bf16[64,3712]{1,0:T(8,128)(2,1)S(1)} %compare_select_fusion.1.refs_1_), channel_id=1, source_target_pairs={{0,4},{4,8},{8,12},{12,0},{1,5},{5,9},{9,13},{13,1},{2,6},{6,10},{... | collective-permute-start | bytes 1425416 | tf_op jit(solution)/shard_map/ppermute | solution.py:249
  35.2 13.9 %collective-permute-start.7 = (bf16[64,3712]{1,0:T(8,128)(2,1)S(1)}, bf16[64,3712]{1,0:T(8,128)(2,1)S(1)}, u32[]{:S(2)}, u32[]{:S(2)}) collective-permute-start(bf16[64,3712]{1,0:T(8,128)(2,1)S(1)} %compare_select_fusion.refs_2_), channel_id=1, source_target_pairs={{0,2},{1,3},{2,0},{3,1},{4,6},{5,7},{6,4},{7,5},{8,10},{9,11},{10,... | collective-permute-start | bytes 1425416 | tf_op jit(solution)/shard_map/ppermute | solution.py:16
  36.6 14.4 %collective-permute-start.9 = (bf16[64,3712]{1,0:T(8,128)(2,1)S(1)}, bf16[64,3712]{1,0:T(8,128)(2,1)S(1)}, u32[]{:S(2)}, u32[]{:S(2)}) collective-permute-start(bf16[64,3712]{1,0:T(8,128)(2,1)S(1)} %compare_select_fusion.refs_2_), channel_id=1, source_target_pairs={{0,4},{4,8},{8,12},{12,0},{1,5},{5,9},{9,13},{13,1},{2,6},{6,10},{... | collective-permute-start | bytes 1425416 | tf_op jit(solution)/shard_map/ppermute | solution.py:249
  36.6 1.0 %copy-start.1 = (bf16[64,3712]{1,0:T(8,128)(2,1)S(1)}, bf16[64,3712]{1,0:T(8,128)(2,1)}, u32[]{:S(2)}) copy-start(bf16[64,3712]{1,0:T(8,128)(2,1)} %shard_map.64.refs_0_) | copy-start | bytes 1425412
  37.6 15.0 %copy-start = (bf16[1,3584,512]{2,1,0:T(8,128)(2,1)S(1)}, bf16[1,3584,512]{2,1,0:T(8,128)(2,1)}, u32[]{:S(2)}) copy-start(bf16[1,3584,512]{2,1,0:T(8,128)(2,1)} %refs_2_.3) | copy-start | bytes 11010052
  48.8 10.9 %collective-permute-start.11 = (bf16[32,3584]{1,0:T(8,128)(2,1)S(1)}, bf16[32,3584]{1,0:T(8,128)(2,1)S(1)}, u32[]{:S(2)}, u32[]{:S(2)}) collective-permute-start(bf16[32,3584]{1,0:T(8,128)(2,1)S(1)} %get-tuple-element.14), channel_id=1, source_target_pairs={{0,4},{4,8},{8,12},{12,0},{1,5},{5,9},{9,13},{13,1},{2,6},{6,10},{... | collective-permute-start | bytes 688136 | tf_op jit(solution)/shard_map/ppermute | solution.py:249
  49.2 12.1 %collective-permute-start.8 = (bf16[32,3712]{1,0:T(8,128)(2,1)S(1)}, bf16[32,3712]{1,0:T(8,128)(2,1)S(1)}, u32[]{:S(2)}, u32[]{:S(2)}) collective-permute-start(bf16[32,3712]{1,0:T(8,128)(2,1)S(1)} %slice_select_fusion.1), channel_id=1, source_target_pairs={{0,4},{4,8},{8,12},{12,0},{1,5},{5,9},{9,13},{13,1},{2,6},{6,10},{... | collective-permute-start | bytes 712712 | tf_op jit(solution)/shard_map/ppermute | solution.py:249
  50.2 9.5 %collective-permute-start.15 = (bf16[32,3584]{1,0:T(8,128)(2,1)S(1)}, bf16[32,3584]{1,0:T(8,128)(2,1)S(1)}, u32[]{:S(2)}, u32[]{:S(2)}) collective-permute-start(bf16[32,3584]{1,0:T(8,128)(2,1)S(1)} %get-tuple-element.15), channel_id=1, source_target_pairs={{0,2},{1,3},{2,0},{3,1},{4,6},{5,7},{6,4},{7,5},{8,10},{9,11},{10,... | collective-permute-start | bytes 688136 | tf_op jit(solution)/shard_map/ppermute | solution.py:16
  51.1 10.4 %collective-permute-start.10 = (bf16[32,3712]{1,0:T(8,128)(2,1)S(1)}, bf16[32,3712]{1,0:T(8,128)(2,1)S(1)}, u32[]{:S(2)}, u32[]{:S(2)}) collective-permute-start(bf16[32,3712]{1,0:T(8,128)(2,1)S(1)} %slice_select_fusion), channel_id=1, source_target_pairs={{0,2},{1,3},{2,0},{3,1},{4,6},{5,7},{6,4},{7,5},{8,10},{9,11},{10,... | collective-permute-start | bytes 712712 | tf_op jit(solution)/shard_map/ppermute | solution.py:16
  61.9 11.0 %collective-permute-start.12 = (bf16[64,3584]{1,0:T(8,128)(2,1)S(1)}, bf16[64,3584]{1,0:T(8,128)(2,1)S(1)}, u32[]{:S(2)}, u32[]{:S(2)}) collective-permute-start(bf16[64,3584]{1,0:T(8,128)(2,1)S(1)} %pad_maximum_fusion), channel_id=1, source_target_pairs={{0,2},{1,3},{2,0},{3,1},{4,6},{5,7},{6,4},{7,5},{8,10},{9,11},{10,... | collective-permute-start | bytes 1376264 | tf_op jit(solution)/shard_map/ppermute | solution.py:16
  63.0 11.5 %collective-permute-start.16 = (bf16[64,3584]{1,0:T(8,128)(2,1)S(1)}, bf16[64,3584]{1,0:T(8,128)(2,1)S(1)}, u32[]{:S(2)}, u32[]{:S(2)}) collective-permute-start(bf16[64,3584]{1,0:T(8,128)(2,1)S(1)} %pad_maximum_fusion.1), channel_id=1, source_target_pairs={{0,4},{4,8},{8,12},{12,0},{1,5},{5,9},{9,13},{13,1},{2,6},{6,10},{... | collective-permute-start | bytes 1376264 | tf_op jit(solution)/shard_map/ppermute | solution.py:249
  73.0 10.9 %collective-permute-start.13 = (bf16[64,3584]{1,0:T(8,128)(2,1)S(1)}, bf16[64,3584]{1,0:T(8,128)(2,1)S(1)}, u32[]{:S(2)}, u32[]{:S(2)}) collective-permute-start(bf16[64,3584]{1,0:T(8,128)(2,1)S(1)} %compare_select_fusion.3), channel_id=1, source_target_pairs={{0,2},{1,3},{2,0},{3,1},{4,6},{5,7},{6,4},{7,5},{8,10},{9,11},{10,... | collective-permute-start | bytes 1376264 | tf_op jit(solution)/shard_map/ppermute | solution.py:16
  74.7 10.8 %collective-permute-start.17 = (bf16[64,3584]{1,0:T(8,128)(2,1)S(1)}, bf16[64,3584]{1,0:T(8,128)(2,1)S(1)}, u32[]{:S(2)}, u32[]{:S(2)}) collective-permute-start(bf16[64,3584]{1,0:T(8,128)(2,1)S(1)} %add_convert_fusion.2), channel_id=1, source_target_pairs={{0,4},{4,8},{8,12},{12,0},{1,5},{5,9},{9,13},{13,1},{2,6},{6,10},{... | collective-permute-start | bytes 1376264 | tf_op jit(solution)/shard_map/ppermute | solution.py:249
  84.0 8.5 %collective-permute-start.14 = (bf16[64,3584]{1,0:T(8,128)(2,1)S(1)}, bf16[64,3584]{1,0:T(8,128)(2,1)S(1)}, u32[]{:S(2)}, u32[]{:S(2)}) collective-permute-start(bf16[64,3584]{1,0:T(8,128)(2,1)S(1)} %compare_select_fusion.2), channel_id=1, source_target_pairs={{0,2},{1,3},{2,0},{3,1},{4,6},{5,7},{6,4},{7,5},{8,10},{9,11},{10,... | collective-permute-start | bytes 1376264 | tf_op jit(solution)/shard_map/ppermute | solution.py:16
  85.6 10.3 %collective-permute-start.18 = (bf16[64,3584]{1,0:T(8,128)(2,1)S(1)}, bf16[64,3584]{1,0:T(8,128)(2,1)S(1)}, u32[]{:S(2)}, u32[]{:S(2)}) collective-permute-start(bf16[64,3584]{1,0:T(8,128)(2,1)S(1)} %add_convert_fusion.1), channel_id=1, source_target_pairs={{0,4},{4,8},{8,12},{12,0},{1,5},{5,9},{9,13},{13,1},{2,6},{6,10},{... | collective-permute-start | bytes 1376264 | tf_op jit(solution)/shard_map/ppermute | solution.py:249

commit v4 on v3

--- a/solution.py
+++ b/solution.py
@@ -244,9 +244,10 @@
     split = rows // 2
     last = node_count - 1
 
+    ring = list(range(0, node_count, 2)) + list(range(1, node_count, 2))[::-1]
+
     def next_node(value):
-        pairs = [(source, (source + 1) % node_count) for source in range(node_count)]
-        return lax.ppermute(value, "node", pairs)
+        return lax.ppermute(value, "node", list(zip(ring, ring[1:] + ring[:1])))
 
     def other_x(value):
         return partner(value, "local", 1)
@@ -261,19 +262,24 @@
         crossed, moved = other_x(along[slot]), next_node(along[slot])
         if slot < last - 1:
             moved = after(moved, crossed)
+        if slot == last - 2:
+            begun = [along[0], along[1], across[0]]
+            begun = list(expert_rows(begun, mine, own, other, [rows] * 3))
+            moved = after(moved, begun[0])
         along.append(moved)
         across.append(crossed)
-    early = along[:last] + across[: last - 1]
-    sizes = [rows] * last + [rows, split, split] + [rows] * (last - 3)
-    results = list(expert_rows(early, mine, own, other, sizes))
-    at_home, away = results[:last], [results[last], None] + results[last + 3 :]
-    first_upper, first_lower = results[last + 1 : last + 3]
+    sizes = [rows, split, split]
+    home, first_upper, first_lower = expert_rows(
+        [along[2], across[1]], mine, own, other, sizes
+    )
+    at_home, away = [begun[0], begun[1], home], [begun[2], None]
     upper = other_x(after(along[last][:split], first_upper))
     lower = next_node(after(across[last - 1][split:], first_lower))
     middle = expert_rows([along[last], across[last - 1]], mine, own, other, [rows, rows])
     at_home.append(middle[0])
 
-    crossed, passed = other_x(first_upper), next_node(first_lower)
+    crossed = other_x(after(first_upper, along[last][:split]))
+    passed = next_node(after(first_lower, across[last - 1][split:]))
     second = [after(middle[1][:split], upper, lower), added(middle[1][split:], passed)]
     away.append(jnp.concatenate(second))
     away += expert_rows([upper, lower], mine, own, other, [rows])

time: 97.1 us -> 92.9 us (0.957)
  waiting for transfers between devices: 45.6 us -> 27.7 us
  starting transfers between devices: 20 us -> 28.1 us
  Pallas kernels: 27.2 us -> 31.9 us
    ppermute x11, waiting for transfers between devices: 34.4 us -> 13.5 us  [partner(): return lax.ppermute(value, axis, pairs)]
    ppermute x8, starting transfers between devices: 9.22 us -> 18.2 us  [next_node(): return lax.ppermute(value, 'node', list(zip(ring, ring[1:] + ring[:1])))]
    pallas_call x3 -> x4, Pallas kernels: 25.3 us -> 29.9 us  [expert_rows(): pl.pallas_call(functools.partial(expert_kernel, len(blocks), down_tiles,...]
    ppermute x8, waiting for transfers between devices: 11.2 us -> 14.2 us  [next_node(): return lax.ppermute(value, 'node', list(zip(ring, ring[1:] + ring[:1])))]
  transfers between devices with their start and end apart: 19 -> 19, of which waited for: 10 -> 8; matrix products, arithmetic and copies ran while one was open for 2% -> 3% of each run, Pallas kernels for 28% -> 34%
where the time goes in v4:
time: 92.9 us; the launch traced here: 92.7 us
  Pallas kernels  31.9 us (34%)
  starting transfers between devices  28.1 us (30%)
  waiting for transfers between devices  27.7 us (30%)
  other arithmetic  3.05 us (3%)
  local copies, waits for them, and re-layouts  1.81 us (2%)
    pallas_call x4, Pallas kernels, expert_rows(): pl.pallas_call(functools.partial(expert_kernel, len(blocks), down_tiles,...  29.9 us
    ppermute x8, starting transfers between devices, next_node(): return lax.ppermute(value, 'node', list(zip(ring, ring[1:] + ring[:1])))  18.2 us
    ppermute x8, waiting for transfers between devices, next_node(): return lax.ppermute(value, 'node', list(zip(ring, ring[1:] + ring[:1])))  14.2 us
    ppermute x11, waiting for transfers between devices, partner(): return lax.ppermute(value, axis, pairs)  13.5 us
    ppermute x11, starting transfers between devices, partner(): return lax.ppermute(value, axis, pairs)  9.91 us
    pallas_call x1, Pallas kernels, pack(): pl.pallas_call(pack_kernel, out_shape=[shape] * pieces, in_specs=[vmem] *...  1.93 us
  transfers between devices with their start and end apart: 19, of which 8 were waited for; matrix products, arithmetic and copies ran while one was open for 3% of the time, Pallas kernels for 34%

profile of v4, /device:TPU:0, one launch (start us, length us, event | category | flops | bytes accessed | tf_op | source)
XLA Modules:
  0.0 92.7 jit_solution(161291792158646215)
XLA Ops:
  0.0 0.5 collective-permute-start.2
  0.5 0.5 collective-permute-start.4
  1.0 1.9 %shard_map.64.refs_0_ = bf16[64,3712]{1,0:T(8,128)(2,1)} custom-call(bf16[64,3584]{1,0:T(8,128)(2,1)} %tokens.1, s32[8,64]{1,0:T(8,128)} %bitcast.3, bf16[8,64]{1,0:T(8,128)(2,1)} %bitcast.4), custom_call_target="tpu_custom_call" | custom-call | tf_op jit(solution)/shard_map/pallas_call | solution.py:132
  2.9 3.6 %collective-permute-start.1 = (bf16[64,3712]{1,0:T(8,128)(2,1)}, bf16[64,3712]{1,0:T(8,128)(2,1)S(1)}, u32[]{:S(2)}, u32[]{:S(2)}) collective-permute-start(bf16[64,3712]{1,0:T(8,128)(2,1)} %shard_map.64.refs_0_), channel_id=1, source_target_pairs={{0,8},{8,12},{12,4},{4,0},{1,9},{9,13},{13,5},{5,1},{2,10},{10,14}... | collective-permute-start | bytes 1425416 | tf_op jit(solution)/shard_map/ppermute | solution.py:250
  6.5 1.5 %collective-permute-start = (bf16[64,3712]{1,0:T(8,128)(2,1)}, bf16[64,3712]{1,0:T(8,128)(2,1)S(1)}, u32[]{:S(2)}, u32[]{:S(2)}) collective-permute-start(bf16[64,3712]{1,0:T(8,128)(2,1)} %shard_map.64.refs_0_), channel_id=1, source_target_pairs={{0,2},{1,3},{2,0},{3,1},{4,6},{5,7},{6,4},{7,5},{8,10},{9,11},{10,... | collective-permute-start | bytes 1425416 | tf_op jit(solution)/shard_map/ppermute | solution.py:16
  8.0 9.6 %collective-permute-done.1 = bf16[64,3712]{1,0:T(8,128)(2,1)S(1)} collective-permute-done((bf16[64,3712]{1,0:T(8,128)(2,1)}, bf16[64,3712]{1,0:T(8,128)(2,1)S(1)}, u32[]{:S(2)}, u32[]{:S(2)}) %collective-permute-start.1) | collective-permute-done | bytes 475168 | tf_op jit(solution)/shard_map/ppermute | solution.py:250
  17.6 2.1 %collective-permute-done.refs_2_ = bf16[64,3712]{1,0:T(8,128)(2,1)S(1)} collective-permute-done((bf16[64,3712]{1,0:T(8,128)(2,1)}, bf16[64,3712]{1,0:T(8,128)(2,1)S(1)}, u32[]{:S(2)}, u32[]{:S(2)}) %collective-permute-start) | collective-permute-done | bytes 475168 | tf_op jit(solution)/shard_map/ppermute | solution.py:16
  19.8 1.6 %collective-permute-start.6 = (bf16[64,3712]{1,0:T(8,128)(2,1)S(1)}, bf16[64,3712]{1,0:T(8,128)(2,1)S(1)}, u32[]{:S(2)}, u32[]{:S(2)}) collective-permute-start(bf16[64,3712]{1,0:T(8,128)(2,1)S(1)} %compare_select_fusion.1.refs_1_), channel_id=1, source_target_pairs={{0,8},{8,12},{12,4},{4,0},{1,9},{9,13},{13,5},{5,1},{2,10},{10,14}... | collective-permute-start | bytes 1425416 | tf_op jit(solution)/shard_map/ppermute | solution.py:250
  21.4 1.5 %collective-permute-start.5 = (bf16[64,3712]{1,0:T(8,128)(2,1)S(1)}, bf16[64,3712]{1,0:T(8,128)(2,1)S(1)}, u32[]{:S(2)}, u32[]{:S(2)}) collective-permute-start(bf16[64,3712]{1,0:T(8,128)(2,1)S(1)} %compare_select_fusion.1.refs_1_), channel_id=1, source_target_pairs={{0,2},{1,3},{2,0},{3,1},{4,6},{5,7},{6,4},{7,5},{8,10},{9,11},{10,... | collective-permute-start | bytes 1425416 | tf_op jit(solution)/shard_map/ppermute | solution.py:16
  22.9 1.0 %copy-done.1 = bf16[64,3712]{1,0:T(8,128)(2,1)S(1)} copy-done((bf16[64,3712]{1,0:T(8,128)(2,1)S(1)}, bf16[64,3712]{1,0:T(8,128)(2,1)}, u32[]{:S(2)}) %copy-start.1) | copy-done | bytes 475160
  23.9 8.9 %shard_map.65 = (bf16[64,3584]{1,0:T(8,128)(2,1)S(1)}, bf16[64,3584]{1,0:T(8,128)(2,1)S(1)}, bf16[64,3584]{1,0:T(8,128)(2,1)S(1)}) custom-call(s32[1]{0:T(128)} %bitcast.mine, bf16[64,3712]{1,0:T(8,128)(2,1)S(1)} %copy-done.1, bf16[64,3712]{1,0:T(8,128)(2,1)S(1)} %compare_select_fusion.1.refs_1_, bf16[64,3712]{1,0:T(8,128)(2,1)S(1)} %collective-permute-done.refs_2_, ...), custom_call_target="tpu_custom_call" | custom-call | flops 4227858432 | bytes 24772608 | tf_op jit(solution)/shard_map/pallas_call | solution.py:203
  32.9 0.1 compare_reduce_fusion
  33.0 0.3 collective-permute-done.5.refs_1_
  33.3 0.1 fusion.refs_0_
  33.4 1.2 %collective-permute-start.9 = (bf16[64,3712]{1,0:T(8,128)(2,1)S(1)}, bf16[64,3712]{1,0:T(8,128)(2,1)S(1)}, u32[]{:S(2)}, u32[]{:S(2)}) collective-permute-start(bf16[64,3712]{1,0:T(8,128)(2,1)S(1)} %fusion.refs_0_), channel_id=1, source_target_pairs={{0,8},{8,12},{12,4},{4,0},{1,9},{9,13},{13,5},{5,1},{2,10},{10,14}... | collective-permute-start | bytes 1425416 | tf_op jit(solution)/shard_map/ppermute | solution.py:250
  34.7 1.5 %collective-permute-start.7 = (bf16[64,3712]{1,0:T(8,128)(2,1)S(1)}, bf16[64,3712]{1,0:T(8,128)(2,1)S(1)}, u32[]{:S(2)}, u32[]{:S(2)}) collective-permute-start(bf16[64,3712]{1,0:T(8,128)(2,1)S(1)} %fusion.refs_0_), channel_id=1, source_target_pairs={{0,2},{1,3},{2,0},{3,1},{4,6},{5,7},{6,4},{7,5},{8,10},{9,11},{10,... | collective-permute-start | bytes 1425416 | tf_op jit(solution)/shard_map/ppermute | solution.py:16
  36.2 7.0 %shard_map.66 = (bf16[64,3584]{1,0:T(8,128)(2,1)S(1)}, bf16[32,3584]{1,0:T(8,128)(2,1)S(1)}, bf16[32,3584]{1,0:T(8,128)(2,1)S(1)}) custom-call(s32[1]{0:T(128)} %bitcast.mine, bf16[64,3712]{1,0:T(8,128)(2,1)S(1)} %fusion.refs_0_, bf16[64,3712]{1,0:T(8,128)(2,1)S(1)} %collective-permute-done.5.refs_1_, bf16[1,3584,512]{2,1,0:T(8,128)(2,1)S(1)} %copy-done, ...), custom_call_target="tpu_custom_call" | custom-call | flops 2818572288 | bytes 23855104 | tf_op jit(solution)/shard_map/pallas_call | solution.py:203
  43.2 0.1 slice_reduce_fusion.6
  43.3 0.1 slice_reduce_fusion.5
  43.4 0.1 compare_reduce_fusion.6
  43.5 0.1 compare_reduce_fusion.4
  43.6 1.2 %collective-permute-done.9.refs_0_ = bf16[64,3712]{1,0:T(8,128)(2,1)S(1)} collective-permute-done((bf16[64,3712]{1,0:T(8,128)(2,1)S(1)}, bf16[64,3712]{1,0:T(8,128)(2,1)S(1)}, u32[]{:S(2)}, u32[]{:S(2)}) %collective-permute-start.9) | collective-permute-done | bytes 475168 | tf_op jit(solution)/shard_map/ppermute | solution.py:250
  44.9 0.1 slice_reduce_fusion.1
  45.0 0.1 compare_reduce_fusion.1
  45.2 1.1 %collective-permute-start.15 = (bf16[32,3584]{1,0:T(8,128)(2,1)S(1)}, bf16[32,3584]{1,0:T(8,128)(2,1)S(1)}, u32[]{:S(2)}, u32[]{:S(2)}) collective-permute-start(bf16[32,3584]{1,0:T(8,128)(2,1)S(1)} %broadcast_select_fusion), channel_id=1, source_target_pairs={{0,2},{1,3},{2,0},{3,1},{4,6},{5,7},{6,4},{7,5},{8,10},{9,11},{10,... | collective-permute-start | bytes 688136 | tf_op jit(solution)/shard_map/ppermute | solution.py:16
  46.5 1.0 %collective-permute-start.10 = (bf16[32,3712]{1,0:T(8,128)(2,1)S(1)}, bf16[32,3712]{1,0:T(8,128)(2,1)S(1)}, u32[]{:S(2)}, u32[]{:S(2)}) collective-permute-start(bf16[32,3712]{1,0:T(8,128)(2,1)S(1)} %slice_select_fusion), channel_id=1, source_target_pairs={{0,2},{1,3},{2,0},{3,1},{4,6},{5,7},{6,4},{7,5},{8,10},{9,11},{10,... | collective-permute-start | bytes 712712 | tf_op jit(solution)/shard_map/ppermute | solution.py:16
  47.6 0.1 compare_reduce_fusion.2
  47.8 2.0 %collective-permute-start.11 = (bf16[32,3584]{1,0:T(8,128)(2,1)S(1)}, bf16[32,3584]{1,0:T(8,128)(2,1)S(1)}, u32[]{:S(2)}, u32[]{:S(2)}) collective-permute-start(bf16[32,3584]{1,0:T(8,128)(2,1)S(1)} %broadcast_select_fusion.1), channel_id=1, source_target_pairs={{0,8},{8,12},{12,4},{4,0},{1,9},{9,13},{13,5},{5,1},{2,10},{10,14}... | collective-permute-start | bytes 688136 | tf_op jit(solution)/shard_map/ppermute | solution.py:250
  49.9 0.2 collective-permute-start.8
  50.2 7.0 %shard_map.67 = (bf16[64,3584]{1,0:T(8,128)(2,1)S(1)}, bf16[64,3584]{1,0:T(8,128)(2,1)S(1)}) custom-call(s32[1]{0:T(128)} %bitcast.mine, bf16[64,3712]{1,0:T(8,128)(2,1)S(1)} %collective-permute-done.9.refs_0_, bf16[64,3712]{1,0:T(8,128)(2,1)S(1)} %collective-permute-done.7.refs_1_, bf16[1,3584,512]{2,1,0:T(8,128)(2,1)S(1)} %copy-done, ...), custom_call_target="tpu_custom_call" | custom-call | flops 2818572288 | bytes 23855104 | tf_op jit(solution)/shard_map/pallas_call | solution.py:203
  57.3 0.1 slice_reduce_fusion.3
  57.4 0.1 compare_reduce_fusion.3
  57.7 0.1 compare_reduce_fusion.5
  57.8 0.1 select_select_fusion
  58.0 1.5 %collective-permute-start.12 = (bf16[64,3584]{1,0:T(8,128)(2,1)S(1)}, bf16[64,3584]{1,0:T(8,128)(2,1)S(1)}, u32[]{:S(2)}, u32[]{:S(2)}) collective-permute-start(bf16[64,3584]{1,0:T(8,128)(2,1)S(1)} %pad_maximum_fusion), channel_id=1, source_target_pairs={{0,2},{1,3},{2,0},{3,1},{4,6},{5,7},{6,4},{7,5},{8,10},{9,11},{10,... | collective-permute-start | bytes 1376264 | tf_op jit(solution)/shard_map/ppermute | solution.py:16
  59.6 2.8 %collective-permute-start.16 = (bf16[64,3584]{1,0:T(8,128)(2,1)S(1)}, bf16[64,3584]{1,0:T(8,128)(2,1)S(1)}, u32[]{:S(2)}, u32[]{:S(2)}) collective-permute-start(bf16[64,3584]{1,0:T(8,128)(2,1)S(1)} %pad_maximum_fusion.1), channel_id=1, source_target_pairs={{0,8},{8,12},{12,4},{4,0},{1,9},{9,13},{13,5},{5,1},{2,10},{10,14}... | collective-permute-start | bytes 1376264 | tf_op jit(solution)/shard_map/ppermute | solution.py:250
  62.4 7.1 %shard_map.68 = bf16[64,3584]{1,0:T(8,128)(2,1)S(1)} custom-call(s32[1]{0:T(128)} %bitcast.mine, bf16[32,3712]{1,0:T(8,128)(2,1)S(1)} %collective-permute-done.10.refs_0_, bf16[32,3712]{1,0:T(8,128)(2,1)S(1)} %collective-permute-done.8.refs_1_, bf16[1,3584,512]{2,1,0:T(8,128)(2,1)S(1)} %copy-done, bf16[1,3584,512]{2,1,0:T(8,128)(2,1)} %refs_3_.7, ...), custom_call_target="tpu_custom_call" | custom-call | flops 1409286144 | bytes 22937600 | tf_op jit(solution)/shard_map/pallas_call | solution.py:203
  69.5 0.6 collective-permute-start.13
  70.1 0.2 add_convert_fusion.2
  70.3 3.2 %collective-permute-start.17 = (bf16[64,3584]{1,0:T(8,128)(2,1)S(1)}, bf16[64,3584]{1,0:T(8,128)(2,1)S(1)}, u32[]{:S(2)}, u32[]{:S(2)}) collective-permute-start(bf16[64,3584]{1,0:T(8,128)(2,1)S(1)} %add_convert_fusion.2), channel_id=1, source_target_pairs={{0,8},{8,12},{12,4},{4,0},{1,9},{9,13},{13,5},{5,1},{2,10},{10,14}... | collective-permute-start | bytes 1376264 | tf_op jit(solution)/shard_map/ppermute | solution.py:250
  73.5 7.4 %collective-permute-done.13 = bf16[64,3584]{1,0:T(8,128)(2,1)S(1)} collective-permute-done((bf16[64,3584]{1,0:T(8,128)(2,1)S(1)}, bf16[64,3584]{1,0:T(8,128)(2,1)S(1)}, u32[]{:S(2)}, u32[]{:S(2)}) %collective-permute-start.13) | collective-permute-done | bytes 458784 | tf_op jit(solution)/shard_map/ppermute | solution.py:16
  81.0 0.2 collective-permute-start.14
  81.2 1.0 %collective-permute-done.17 = bf16[64,3584]{1,0:T(8,128)(2,1)S(1)} collective-permute-done((bf16[64,3584]{1,0:T(8,128)(2,1)S(1)}, bf16[64,3584]{1,0:T(8,128)(2,1)S(1)}, u32[]{:S(2)}, u32[]{:S(2)}) %collective-permute-start.17) | collective-permute-done | bytes 458784 | tf_op jit(solution)/shard_map/ppermute | solution.py:250
  82.2 0.2 add_convert_fusion.1
  82.3 3.4 %collective-permute-start.18 = (bf16[64,3584]{1,0:T(8,128)(2,1)S(1)}, bf16[64,3584]{1,0:T(8,128)(2,1)S(1)}, u32[]{:S(2)}, u32[]{:S(2)}) collective-permute-start(bf16[64,3584]{1,0:T(8,128)(2,1)S(1)} %add_convert_fusion.1), channel_id=1, source_target_pairs={{0,8},{8,12},{12,4},{4,0},{1,9},{9,13},{13,5},{5,1},{2,10},{10,14}... | collective-permute-start | bytes 1376264 | tf_op jit(solution)/shard_map/ppermute | solution.py:250
  85.8 3.7 %collective-permute-done.14 = bf16[64,3584]{1,0:T(8,128)(2,1)S(1)} collective-permute-done((bf16[64,3584]{1,0:T(8,128)(2,1)S(1)}, bf16[64,3584]{1,0:T(8,128)(2,1)S(1)}, u32[]{:S(2)}, u32[]{:S(2)}) %collective-permute-start.14) | collective-permute-done | bytes 458784 | tf_op jit(solution)/shard_map/ppermute | solution.py:16
  89.5 2.3 %collective-permute-done.18 = bf16[64,3584]{1,0:T(8,128)(2,1)S(1)} collective-permute-done((bf16[64,3584]{1,0:T(8,128)(2,1)S(1)}, bf16[64,3584]{1,0:T(8,128)(2,1)S(1)}, u32[]{:S(2)}, u32[]{:S(2)}) %collective-permute-start.18) | collective-permute-done | bytes 458784 | tf_op jit(solution)/shard_map/ppermute | solution.py:250
  91.8 0.9 %add_convert_fusion = bf16[64,3584]{1,0:T(8,128)(2,1)} fusion(bf16[64,3584]{1,0:T(8,128)(2,1)S(1)} %collective-permute-done.18, bf16[64,3584]{1,0:T(8,128)(2,1)S(1)} %collective-permute-done.14, bf16[64,3584]{1,0:T(8,128)(2,1)S(1)} %get-tuple-element.13), kind=kLoop, calls=%fused_computation.4 | loop fusion | flops 1376256 | bytes 1835008 | tf_op jit(solution)/shard_map/convert_element_type | solution.py:226
  (30 shorter events, 1.2 us)
Async XLA Ops:
  0.0 22.9 %collective-permute-start.2 = (bf16[1,3584,512]{2,1,0:T(8,128)(2,1)}, bf16[1,3584,512]{2,1,0:T(8,128)(2,1)}, u32[]{:S(2)}, u32[]{:S(2)}) collective-permute-start(bf16[1,3584,512]{2,1,0:T(8,128)(2,1)} %refs_2_.5), channel_id=1, source_target_pairs={{0,1},{1,0},{2,3},{3,2},{4,5},{5,4},{6,7},{7,6},{8,9},{9,8},{10,11... | collective-permute-start | bytes 11010056 | tf_op jit(solution)/shard_map/ppermute | solution.py:16
  0.5 22.4 %collective-permute-start.3 = (bf16[1,3584,512]{2,1,0:T(8,128)(2,1)}, bf16[1,3584,512]{2,1,0:T(8,128)(2,1)}, u32[]{:S(2)}, u32[]{:S(2)}) collective-permute-start(bf16[1,3584,512]{2,1,0:T(8,128)(2,1)} %refs_3_.7), channel_id=1, source_target_pairs={{0,1},{1,0},{2,3},{3,2},{4,5},{5,4},{6,7},{7,6},{8,9},{9,8},{10,11... | collective-permute-start | bytes 11010056 | tf_op jit(solution)/shard_map/ppermute | solution.py:16
  0.5 22.4 %collective-permute-start.4 = (bf16[1,512,3584]{2,1,0:T(8,128)(2,1)}, bf16[1,512,3584]{2,1,0:T(8,128)(2,1)}, u32[]{:S(2)}, u32[]{:S(2)}) collective-permute-start(bf16[1,512,3584]{2,1,0:T(8,128)(2,1)} %refs_4_.7), channel_id=1, source_target_pairs={{0,1},{1,0},{2,3},{3,2},{4,5},{5,4},{6,7},{7,6},{8,9},{9,8},{10,11... | collective-permute-start | bytes 11010056 | tf_op jit(solution)/shard_map/ppermute | solution.py:16
  2.9 14.7 %collective-permute-start.1 = (bf16[64,3712]{1,0:T(8,128)(2,1)}, bf16[64,3712]{1,0:T(8,128)(2,1)S(1)}, u32[]{:S(2)}, u32[]{:S(2)}) collective-permute-start(bf16[64,3712]{1,0:T(8,128)(2,1)} %shard_map.64.refs_0_), channel_id=1, source_target_pairs={{0,8},{8,12},{12,4},{4,0},{1,9},{9,13},{13,5},{5,1},{2,10},{10,14}... | collective-permute-start | bytes 1425416 | tf_op jit(solution)/shard_map/ppermute | solution.py:250
  6.5 13.2 %collective-permute-start = (bf16[64,3712]{1,0:T(8,128)(2,1)}, bf16[64,3712]{1,0:T(8,128)(2,1)S(1)}, u32[]{:S(2)}, u32[]{:S(2)}) collective-permute-start(bf16[64,3712]{1,0:T(8,128)(2,1)} %shard_map.64.refs_0_), channel_id=1, source_target_pairs={{0,2},{1,3},{2,0},{3,1},{4,6},{5,7},{6,4},{7,5},{8,10},{9,11},{10,... | collective-permute-start | bytes 1425416 | tf_op jit(solution)/shard_map/ppermute | solution.py:16
  19.8 13.3 %collective-permute-start.6 = (bf16[64,3712]{1,0:T(8,128)(2,1)S(1)}, bf16[64,3712]{1,0:T(8,128)(2,1)S(1)}, u32[]{:S(2)}, u32[]{:S(2)}) collective-permute-start(bf16[64,3712]{1,0:T(8,128)(2,1)S(1)} %compare_select_fusion.1.refs_1_), channel_id=1, source_target_pairs={{0,8},{8,12},{12,4},{4,0},{1,9},{9,13},{13,5},{5,1},{2,10},{10,14}... | collective-permute-start | bytes 1425416 | tf_op jit(solution)/shard_map/ppermute | solution.py:250
  21.4 11.9 %collective-permute-start.5 = (bf16[64,3712]{1,0:T(8,128)(2,1)S(1)}, bf16[64,3712]{1,0:T(8,128)(2,1)S(1)}, u32[]{:S(2)}, u32[]{:S(2)}) collective-permute-start(bf16[64,3712]{1,0:T(8,128)(2,1)S(1)} %compare_select_fusion.1.refs_1_), channel_id=1, source_target_pairs={{0,2},{1,3},{2,0},{3,1},{4,6},{5,7},{6,4},{7,5},{8,10},{9,11},{10,... | collective-permute-start | bytes 1425416 | tf_op jit(solution)/shard_map/ppermute | solution.py:16
  22.9 1.0 %copy-start.1 = (bf16[64,3712]{1,0:T(8,128)(2,1)S(1)}, bf16[64,3712]{1,0:T(8,128)(2,1)}, u32[]{:S(2)}) copy-start(bf16[64,3712]{1,0:T(8,128)(2,1)} %shard_map.64.refs_0_) | copy-start | bytes 1425412
  23.9 12.2 %copy-start = (bf16[1,3584,512]{2,1,0:T(8,128)(2,1)S(1)}, bf16[1,3584,512]{2,1,0:T(8,128)(2,1)}, u32[]{:S(2)}) copy-start(bf16[1,3584,512]{2,1,0:T(8,128)(2,1)} %refs_2_.5) | copy-start | bytes 11010052
  33.4 11.4 %collective-permute-start.9 = (bf16[64,3712]{1,0:T(8,128)(2,1)S(1)}, bf16[64,3712]{1,0:T(8,128)(2,1)S(1)}, u32[]{:S(2)}, u32[]{:S(2)}) collective-permute-start(bf16[64,3712]{1,0:T(8,128)(2,1)S(1)} %fusion.refs_0_), channel_id=1, source_target_pairs={{0,8},{8,12},{12,4},{4,0},{1,9},{9,13},{13,5},{5,1},{2,10},{10,14}... | collective-permute-start | bytes 1425416 | tf_op jit(solution)/shard_map/ppermute | solution.py:250
  34.7 12.8 %collective-permute-start.7 = (bf16[64,3712]{1,0:T(8,128)(2,1)S(1)}, bf16[64,3712]{1,0:T(8,128)(2,1)S(1)}, u32[]{:S(2)}, u32[]{:S(2)}) collective-permute-start(bf16[64,3712]{1,0:T(8,128)(2,1)S(1)} %fusion.refs_0_), channel_id=1, source_target_pairs={{0,2},{1,3},{2,0},{3,1},{4,6},{5,7},{6,4},{7,5},{8,10},{9,11},{10,... | collective-permute-start | bytes 1425416 | tf_op jit(solution)/shard_map/ppermute | solution.py:16
  45.2 12.0 %collective-permute-start.15 = (bf16[32,3584]{1,0:T(8,128)(2,1)S(1)}, bf16[32,3584]{1,0:T(8,128)(2,1)S(1)}, u32[]{:S(2)}, u32[]{:S(2)}) collective-permute-start(bf16[32,3584]{1,0:T(8,128)(2,1)S(1)} %broadcast_select_fusion), channel_id=1, source_target_pairs={{0,2},{1,3},{2,0},{3,1},{4,6},{5,7},{6,4},{7,5},{8,10},{9,11},{10,... | collective-permute-start | bytes 688136 | tf_op jit(solution)/shard_map/ppermute | solution.py:16
  46.5 10.9 %collective-permute-start.10 = (bf16[32,3712]{1,0:T(8,128)(2,1)S(1)}, bf16[32,3712]{1,0:T(8,128)(2,1)S(1)}, u32[]{:S(2)}, u32[]{:S(2)}) collective-permute-start(bf16[32,3712]{1,0:T(8,128)(2,1)S(1)} %slice_select_fusion), channel_id=1, source_target_pairs={{0,2},{1,3},{2,0},{3,1},{4,6},{5,7},{6,4},{7,5},{8,10},{9,11},{10,... | collective-permute-start | bytes 712712 | tf_op jit(solution)/shard_map/ppermute | solution.py:16
  47.8 9.4 %collective-permute-start.11 = (bf16[32,3584]{1,0:T(8,128)(2,1)S(1)}, bf16[32,3584]{1,0:T(8,128)(2,1)S(1)}, u32[]{:S(2)}, u32[]{:S(2)}) collective-permute-start(bf16[32,3584]{1,0:T(8,128)(2,1)S(1)} %broadcast_select_fusion.1), channel_id=1, source_target_pairs={{0,8},{8,12},{12,4},{4,0},{1,9},{9,13},{13,5},{5,1},{2,10},{10,14}... | collective-permute-start | bytes 688136 | tf_op jit(solution)/shard_map/ppermute | solution.py:250
  49.9 7.7 %collective-permute-start.8 = (bf16[32,3712]{1,0:T(8,128)(2,1)S(1)}, bf16[32,3712]{1,0:T(8,128)(2,1)S(1)}, u32[]{:S(2)}, u32[]{:S(2)}) collective-permute-start(bf16[32,3712]{1,0:T(8,128)(2,1)S(1)} %slice_select_fusion.1), channel_id=1, source_target_pairs={{0,8},{8,12},{12,4},{4,0},{1,9},{9,13},{13,5},{5,1},{2,10},{10,14}... | collective-permute-start | bytes 712712 | tf_op jit(solution)/shard_map/ppermute | solution.py:250
  58.0 11.5 %collective-permute-start.12 = (bf16[64,3584]{1,0:T(8,128)(2,1)S(1)}, bf16[64,3584]{1,0:T(8,128)(2,1)S(1)}, u32[]{:S(2)}, u32[]{:S(2)}) collective-permute-start(bf16[64,3584]{1,0:T(8,128)(2,1)S(1)} %pad_maximum_fusion), channel_id=1, source_target_pairs={{0,2},{1,3},{2,0},{3,1},{4,6},{5,7},{6,4},{7,5},{8,10},{9,11},{10,... | collective-permute-start | bytes 1376264 | tf_op jit(solution)/shard_map/ppermute | solution.py:16
  59.6 10.6 %collective-permute-start.16 = (bf16[64,3584]{1,0:T(8,128)(2,1)S(1)}, bf16[64,3584]{1,0:T(8,128)(2,1)S(1)}, u32[]{:S(2)}, u32[]{:S(2)}) collective-permute-start(bf16[64,3584]{1,0:T(8,128)(2,1)S(1)} %pad_maximum_fusion.1), channel_id=1, source_target_pairs={{0,8},{8,12},{12,4},{4,0},{1,9},{9,13},{13,5},{5,1},{2,10},{10,14}... | collective-permute-start | bytes 1376264 | tf_op jit(solution)/shard_map/ppermute | solution.py:250
  69.5 11.4 %collective-permute-start.13 = (bf16[64,3584]{1,0:T(8,128)(2,1)S(1)}, bf16[64,3584]{1,0:T(8,128)(2,1)S(1)}, u32[]{:S(2)}, u32[]{:S(2)}) collective-permute-start(bf16[64,3584]{1,0:T(8,128)(2,1)S(1)} %compare_select_fusion.3), channel_id=1, source_target_pairs={{0,2},{1,3},{2,0},{3,1},{4,6},{5,7},{6,4},{7,5},{8,10},{9,11},{10,... | collective-permute-start | bytes 1376264 | tf_op jit(solution)/shard_map/ppermute | solution.py:16
  70.3 11.9 %collective-permute-start.17 = (bf16[64,3584]{1,0:T(8,128)(2,1)S(1)}, bf16[64,3584]{1,0:T(8,128)(2,1)S(1)}, u32[]{:S(2)}, u32[]{:S(2)}) collective-permute-start(bf16[64,3584]{1,0:T(8,128)(2,1)S(1)} %add_convert_fusion.2), channel_id=1, source_target_pairs={{0,8},{8,12},{12,4},{4,0},{1,9},{9,13},{13,5},{5,1},{2,10},{10,14}... | collective-permute-start | bytes 1376264 | tf_op jit(solution)/shard_map/ppermute | solution.py:250
  81.0 8.5 %collective-permute-start.14 = (bf16[64,3584]{1,0:T(8,128)(2,1)S(1)}, bf16[64,3584]{1,0:T(8,128)(2,1)S(1)}, u32[]{:S(2)}, u32[]{:S(2)}) collective-permute-start(bf16[64,3584]{1,0:T(8,128)(2,1)S(1)} %compare_select_fusion.2), channel_id=1, source_target_pairs={{0,2},{1,3},{2,0},{3,1},{4,6},{5,7},{6,4},{7,5},{8,10},{9,11},{10,... | collective-permute-start | bytes 1376264 | tf_op jit(solution)/shard_map/ppermute | solution.py:16
  82.3 9.4 %collective-permute-start.18 = (bf16[64,3584]{1,0:T(8,128)(2,1)S(1)}, bf16[64,3584]{1,0:T(8,128)(2,1)S(1)}, u32[]{:S(2)}, u32[]{:S(2)}) collective-permute-start(bf16[64,3584]{1,0:T(8,128)(2,1)S(1)} %add_convert_fusion.1), channel_id=1, source_target_pairs={{0,8},{8,12},{12,4},{4,0},{1,9},{9,13},{13,5},{5,1},{2,10},{10,14}... | collective-permute-start | bytes 1376264 | tf_op jit(solution)/shard_map/ppermute | solution.py:250

commit v5 on v4

--- a/solution.py
+++ b/solution.py
@@ -137,7 +137,8 @@
     )(tokens, expert_ids.T, gate_scores.T)
 
 
-def expert_kernel(taken, down_tiles, hidden_tile, mine, *refs):
+def expert_kernel(ranges, down_tiles, hidden_tile, mine, *refs):
+    taken = len(ranges)
     blocks, weights, outs = refs[:taken], refs[taken : taken + 6], refs[taken + 6 : -6]
     rows_all, gate, up, down, hidden, sems = refs[-6:]
     width = down.shape[2]
@@ -168,9 +169,9 @@
         )
         second.append((cols, pair))
     at = 0
-    for block in blocks:
-        rows_all[pl.ds(at, block.shape[0]), :] = block[...]
-        at += block.shape[0]
+    for block, (start, rows) in zip(blocks, ranges):
+        rows_all[pl.ds(at, rows), :] = block[pl.ds(start, rows), :]
+        at += rows
     lane = lax.broadcasted_iota(jnp.int32, (at, LANES), 1)
     factors = rows_all[:, width:].astype(jnp.float32)
     factor = jnp.sum(jnp.where(lane == mine[0], factors, 0.0), axis=1, keepdims=True)
@@ -191,20 +192,25 @@
         for out in outs:
             out[:, cols] = result[at : at + out.shape[0]]
             at += out.shape[0]
-
-
-def expert_rows(blocks, mine, own, other, out_rows):
+    for out in outs:
+        if out.shape[1] > width:
+            out[:, width:] = jnp.zeros((out.shape[0], out.shape[1] - width), out.dtype)
+
+
+def expert_rows(pieces, mine, own, other, outs):
     half, width = own[2].shape[1:]
-    total = sum(block.shape[0] for block in blocks)
+    blocks = [piece[0] for piece in pieces]
+    ranges = [piece[1:] for piece in pieces]
+    total = sum(count for _, count in ranges)
     down_tiles = 4
     hidden_tile = half // 2
     vmem = pl.BlockSpec(memory_space=pltpu.VMEM)
     anywhere = pl.BlockSpec(memory_space=pl.ANY)
     return pl.pallas_call(
-        functools.partial(expert_kernel, len(blocks), down_tiles, hidden_tile),
-        out_shape=[jax.ShapeDtypeStruct((rows, width), jnp.bfloat16) for rows in out_rows],
+        functools.partial(expert_kernel, ranges, down_tiles, hidden_tile),
+        out_shape=[jax.ShapeDtypeStruct(out, jnp.bfloat16) for out in outs],
         in_specs=[pl.BlockSpec(memory_space=pltpu.SMEM)] + [vmem] * len(blocks) + [anywhere] * 6,
-        out_specs=[vmem] * len(out_rows),
+        out_specs=[vmem] * len(outs),
         scratch_shapes=[
             pltpu.VMEM((total, width + LANES), jnp.bfloat16),
             pltpu.VMEM((2, width, half), jnp.bfloat16),
@@ -213,7 +219,7 @@
             pltpu.VMEM((2, total, half), jnp.bfloat16),
             pltpu.SemaphoreType.DMA((4 * (half // hidden_tile) + 2 * down_tiles,)),
         ],
-        compiler_params=pltpu.CompilerParams(vmem_limit_bytes=48 * 2**20),
+        compiler_params=pltpu.CompilerParams(vmem_limit_bytes=52 * 2**20),
         cost_estimate=pl.CostEstimate(
             flops=12 * total * width * half,
             bytes_accessed=12 * width * half + 4 * total * width,
@@ -226,10 +232,6 @@
     return sum(term.astype(jnp.float32) for term in terms).astype(jnp.bfloat16)
 
 
-def together(*values):
-    return lax.optimization_barrier(values)
-
-
 def after(value, *others):
     for other in others:
         same = other if other.shape == value.shape else other[:, :1]
@@ -240,7 +242,7 @@
 def dense(tokens, expert_ids, gate_scores, gate_weight, up_weight, down_weight):
     node_count = lax.axis_size("node")
     local_count = lax.axis_size("local")
-    rows = tokens.shape[0]
+    rows, width = tokens.shape
     split = rows // 2
     last = node_count - 1
 
@@ -256,6 +258,8 @@
     mine = jnp.full((1,), mine, jnp.int32)
     own = (gate_weight, up_weight, down_weight)
     other = tuple(partner(weight, "local", 0) for weight in own)
+
+    whole, wide = (rows, width), (split, width + LANES)
 
     along, across = list(pack(tokens, expert_ids, gate_scores, 1)), []
     for slot in range(last):
@@ -263,34 +267,34 @@
         if slot < last - 1:
             moved = after(moved, crossed)
         if slot == last - 2:
-            begun = [along[0], along[1], across[0]]
-            begun = list(expert_rows(begun, mine, own, other, [rows] * 3))
-            moved = after(moved, begun[0])
+            pieces = [(along[0], 0, rows), (across[0], 0, rows)]
+            home_own, away_own = expert_rows(pieces, mine, own, other, [whole] * 2)
+            moved = after(moved, home_own)
         along.append(moved)
         across.append(crossed)
-    sizes = [rows, split, split]
-    home, first_upper, first_lower = expert_rows(
-        [along[2], across[1]], mine, own, other, sizes
-    )
-    at_home, away = [begun[0], begun[1], home], [begun[2], None]
-    upper = other_x(after(along[last][:split], first_upper))
-    lower = next_node(after(across[last - 1][split:], first_lower))
-    middle = expert_rows([along[last], across[last - 1]], mine, own, other, [rows, rows])
-    at_home.append(middle[0])
-
-    crossed = other_x(after(first_upper, along[last][:split]))
-    passed = next_node(after(first_lower, across[last - 1][split:]))
-    second = [after(middle[1][:split], upper, lower), added(middle[1][split:], passed)]
-    away.append(jnp.concatenate(second))
-    away += expert_rows([upper, lower], mine, own, other, [rows])
-    first = at_home[1]
-    running = jnp.concatenate([added(first[:split], crossed), first[split:]])
-    for slot in list(range(2, node_count)) + [0]:
-        crossed, moved = other_x(away[slot]), next_node(running)
-        running = added(at_home[slot], crossed, moved)
-        if slot:
-            following = (slot + 1) % node_count
-            away[following] = after(away[following], crossed)
+    pieces = [(along[1], 0, rows), (along[2], 0, rows), (across[1], 0, rows)]
+    home_one, home_two, away_upper, away_lower = expert_rows(
+        pieces, mine, own, other, [whole, whole, wide, wide]
+    )
+
+    by_x = other_x(jnp.concatenate([along[last][:split], away_upper]))
+    by_node = next_node(jnp.concatenate([across[last - 1][split:], away_lower]))
+    crossed, passed = by_x[split:, :width], by_node[split:, :width]
+    pieces = [(along[last], 0, rows), (across[last - 1], 0, rows)]
+    home_last, away_two = expert_rows(pieces, mine, own, other, [whole] * 2)
+
+    running = jnp.concatenate([added(home_one[:split], crossed), home_one[split:]])
+    away_two = jnp.concatenate(
+        [after(away_two[:split], crossed), added(away_two[split:], passed)]
+    )
+    pieces = [(by_x, 0, split), (by_node, 0, split)]
+    (away_last,) = expert_rows(pieces, mine, own, other, [whole])
+    homes, aways = [home_two, home_last, home_own], [away_two, away_last, away_own]
+    for i, home in enumerate(homes):
+        crossed, moved = other_x(aways[i]), next_node(running)
+        running = added(home, crossed, moved)
+        if i < 2:
+            aways[i + 1] = after(aways[i + 1], crossed)
     return running
 
 

time: 92.9 us -> 90.6 us (0.975)
  starting transfers between devices: 28.1 us -> 22.8 us
  Pallas kernels: 31.9 us -> 35.7 us
  other arithmetic: 3.05 us -> 2 us
    ppermute x8 -> x7, waiting for transfers between devices: 14.2 us -> 21.8 us  [next_node(): return lax.ppermute(value, 'node', list(zip(ring, ring[1:] + ring[:1])))]
    ppermute x8 -> x7, starting transfers between devices: 18.2 us -> 11.2 us  [next_node(): return lax.ppermute(value, 'node', list(zip(ring, ring[1:] + ring[:1])))]
    ppermute x11 -> x10, waiting for transfers between devices: 13.5 us -> 6.74 us  [partner(): return lax.ppermute(value, axis, pairs)]
    pallas_call x4, Pallas kernels: 29.9 us -> 33.8 us  [expert_rows(): pl.pallas_call(functools.partial(expert_kernel, ranges, down_tiles, hidde...]
    ppermute x11 -> x10, starting transfers between devices: 9.91 us -> 11.6 us  [partner(): return lax.ppermute(value, axis, pairs)]
  transfers between devices with their start and end apart: 19 -> 17, of which waited for: 8 -> 9; matrix products, arithmetic and copies ran while one was open for 3% -> 1% of each run, Pallas kernels for 34% -> 40%
where the time goes in v5:
time: 90.6 us; the launch traced here: 90.4 us
  Pallas kernels  35.7 us (39%)
  waiting for transfers between devices  28.5 us (31%)
  starting transfers between devices  22.8 us (25%)
  other arithmetic  2 us (2%)
  local copies, waits for them, and re-layouts  1.18 us (1%)
    pallas_call x4, Pallas kernels, expert_rows(): pl.pallas_call(functools.partial(expert_kernel, ranges, down_tiles, hidde...  33.8 us
    ppermute x7, waiting for transfers between devices, next_node(): return lax.ppermute(value, 'node', list(zip(ring, ring[1:] + ring[:1])))  21.8 us
    ppermute x10, starting transfers between devices, partner(): return lax.ppermute(value, axis, pairs)  11.6 us
    ppermute x7, starting transfers between devices, next_node(): return lax.ppermute(value, 'node', list(zip(ring, ring[1:] + ring[:1])))  11.2 us
    ppermute x10, waiting for transfers between devices, partner(): return lax.ppermute(value, axis, pairs)  6.74 us
    pallas_call x1, Pallas kernels, pack(): pl.pallas_call(pack_kernel, out_shape=[shape] * pieces, in_specs=[vmem] *...  1.92 us
  transfers between devices with their start and end apart: 17, of which 9 were waited for; matrix products, arithmetic and copies ran while one was open for 1% of the time, Pallas kernels for 40%

profile of v5, /device:TPU:0, one launch (start us, length us, event | category | flops | bytes accessed | tf_op | source)
XLA Modules:
  0.0 90.4 jit_solution(12102446117092263034)
XLA Ops:
  0.0 0.5 collective-permute-start.1
  0.5 0.1 collective-permute-start.2
  0.5 0.5 collective-permute-start.3
  1.0 1.9 %shard_map.64.refs_0_ = bf16[64,3712]{1,0:T(8,128)(2,1)} custom-call(bf16[64,3584]{1,0:T(8,128)(2,1)} %tokens.1, s32[8,64]{1,0:T(8,128)} %bitcast.3, bf16[8,64]{1,0:T(8,128)(2,1)} %bitcast.4), custom_call_target="tpu_custom_call" | custom-call | tf_op jit(solution)/shard_map/pallas_call | solution.py:132
  2.9 3.6 %collective-permute-start.4 = (bf16[64,3712]{1,0:T(8,128)(2,1)}, bf16[64,3712]{1,0:T(8,128)(2,1)S(1)}, u32[]{:S(2)}, u32[]{:S(2)}) collective-permute-start(bf16[64,3712]{1,0:T(8,128)(2,1)} %shard_map.64.refs_0_), channel_id=1, source_target_pairs={{0,8},{8,12},{12,4},{4,0},{1,9},{9,13},{13,5},{5,1},{2,10},{10,14}... | collective-permute-start | bytes 1425416 | tf_op jit(solution)/shard_map/ppermute | solution.py:252
  6.5 1.5 %collective-permute-start = (bf16[64,3712]{1,0:T(8,128)(2,1)}, bf16[64,3712]{1,0:T(8,128)(2,1)S(1)}, u32[]{:S(2)}, u32[]{:S(2)}) collective-permute-start(bf16[64,3712]{1,0:T(8,128)(2,1)} %shard_map.64.refs_0_), channel_id=1, source_target_pairs={{0,2},{1,3},{2,0},{3,1},{4,6},{5,7},{6,4},{7,5},{8,10},{9,11},{10,... | collective-permute-start | bytes 1425416 | tf_op jit(solution)/shard_map/ppermute | solution.py:16
  8.0 9.6 %collective-permute-done.4 = bf16[64,3712]{1,0:T(8,128)(2,1)S(1)} collective-permute-done((bf16[64,3712]{1,0:T(8,128)(2,1)}, bf16[64,3712]{1,0:T(8,128)(2,1)S(1)}, u32[]{:S(2)}, u32[]{:S(2)}) %collective-permute-start.4) | collective-permute-done | bytes 475168 | tf_op jit(solution)/shard_map/ppermute | solution.py:252
  17.6 2.1 %collective-permute-done.refs_1_ = bf16[64,3712]{1,0:T(8,128)(2,1)S(1)} collective-permute-done((bf16[64,3712]{1,0:T(8,128)(2,1)}, bf16[64,3712]{1,0:T(8,128)(2,1)S(1)}, u32[]{:S(2)}, u32[]{:S(2)}) %collective-permute-start) | collective-permute-done | bytes 475168 | tf_op jit(solution)/shard_map/ppermute | solution.py:16
  19.7 0.1 compare_select_fusion.1.refs_0_
  19.8 1.6 %collective-permute-start.6 = (bf16[64,3712]{1,0:T(8,128)(2,1)S(1)}, bf16[64,3712]{1,0:T(8,128)(2,1)S(1)}, u32[]{:S(2)}, u32[]{:S(2)}) collective-permute-start(bf16[64,3712]{1,0:T(8,128)(2,1)S(1)} %compare_select_fusion.1.refs_0_), channel_id=1, source_target_pairs={{0,8},{8,12},{12,4},{4,0},{1,9},{9,13},{13,5},{5,1},{2,10},{10,14}... | collective-permute-start | bytes 1425416 | tf_op jit(solution)/shard_map/ppermute | solution.py:252
  21.4 1.5 %collective-permute-start.5 = (bf16[64,3712]{1,0:T(8,128)(2,1)S(1)}, bf16[64,3712]{1,0:T(8,128)(2,1)S(1)}, u32[]{:S(2)}, u32[]{:S(2)}) collective-permute-start(bf16[64,3712]{1,0:T(8,128)(2,1)S(1)} %compare_select_fusion.1.refs_0_), channel_id=1, source_target_pairs={{0,2},{1,3},{2,0},{3,1},{4,6},{5,7},{6,4},{7,5},{8,10},{9,11},{10,... | collective-permute-start | bytes 1425416 | tf_op jit(solution)/shard_map/ppermute | solution.py:16
  22.9 0.0 collective-permute-done.1.refs_5_.refs_6_
  22.9 0.0 collective-permute-done.2.refs_6_.refs_7_
  22.9 0.0 collective-permute-done.3.refs_7_.refs_8_
  22.9 1.0 %copy-done = bf16[64,3712]{1,0:T(8,128)(2,1)S(1)} copy-done((bf16[64,3712]{1,0:T(8,128)(2,1)S(1)}, bf16[64,3712]{1,0:T(8,128)(2,1)}, u32[]{:S(2)}) %copy-start) | copy-done | bytes 475160
  23.9 7.9 %shard_map.65 = (bf16[64,3584]{1,0:T(8,128)(2,1)S(1)}, bf16[64,3584]{1,0:T(8,128)(2,1)S(1)}) custom-call(s32[1]{0:T(128)} %bitcast.mine, bf16[64,3712]{1,0:T(8,128)(2,1)S(1)} %copy-done, bf16[64,3712]{1,0:T(8,128)(2,1)S(1)} %collective-permute-done.refs_1_, bf16[1,3584,512]{2,1,0:T(8,128)(2,1)} %refs_2_.5, bf16[1,3584,512]{2,1,0:T(8,128)(2,1)} %refs_3_.7, ...), custom_call_target="tpu_custom_call" | custom-call | flops 2818572288 | bytes 23855104 | tf_op jit(solution)/shard_map/pallas_call | solution.py:209
  31.9 0.1 slice_reduce_fusion
  32.0 0.1 compare_reduce_fusion
  32.1 0.0 collective-permute-done.6
  32.1 1.2 %collective-permute-done.5.refs_2_ = bf16[64,3712]{1,0:T(8,128)(2,1)S(1)} collective-permute-done((bf16[64,3712]{1,0:T(8,128)(2,1)S(1)}, bf16[64,3712]{1,0:T(8,128)(2,1)S(1)}, u32[]{:S(2)}, u32[]{:S(2)}) %collective-permute-start.5) | collective-permute-done | bytes 475168 | tf_op jit(solution)/shard_map/ppermute | solution.py:16
  33.3 0.1 fusion.refs_1_
  33.4 1.2 %collective-permute-start.7 = (bf16[64,3712]{1,0:T(8,128)(2,1)S(1)}, bf16[64,3712]{1,0:T(8,128)(2,1)S(1)}, u32[]{:S(2)}, u32[]{:S(2)}) collective-permute-start(bf16[64,3712]{1,0:T(8,128)(2,1)S(1)} %fusion.refs_1_), channel_id=1, source_target_pairs={{0,8},{8,12},{12,4},{4,0},{1,9},{9,13},{13,5},{5,1},{2,10},{10,14}... | collective-permute-start | bytes 1425416 | tf_op jit(solution)/shard_map/ppermute | solution.py:252
  34.7 1.5 %collective-permute-start.9 = (bf16[64,3712]{1,0:T(8,128)(2,1)S(1)}, bf16[64,3712]{1,0:T(8,128)(2,1)S(1)}, u32[]{:S(2)}, u32[]{:S(2)}) collective-permute-start(bf16[64,3712]{1,0:T(8,128)(2,1)S(1)} %fusion.refs_1_), channel_id=1, source_target_pairs={{0,2},{1,3},{2,0},{3,1},{4,6},{5,7},{6,4},{7,5},{8,10},{9,11},{10,... | collective-permute-start | bytes 1425416 | tf_op jit(solution)/shard_map/ppermute | solution.py:16
  36.2 9.9 %shard_map.66 = (bf16[64,3584]{1,0:T(8,128)(2,1)S(1)}, bf16[64,3584]{1,0:T(8,128)(2,1)S(1)}, bf16[32,3712]{1,0:T(8,128)(2,1)S(1)}, bf16[32,3712]{1,0:T(8,128)(2,1)S(1)}) custom-call(s32[1]{0:T(128)} %bitcast.mine, bf16[64,3712]{1,0:T(8,128)(2,1)S(1)} %compare_select_fusion.1.refs_0_, bf16[64,3712]{1,0:T(8,128)(2,1)} %copy-done.2, ...), custom_call_target="tpu_custom_call" | custom-call | flops 4227858432 | bytes 24772608 | tf_op jit(solution)/shard_map/pallas_call | solution.py:209
  46.1 0.0 collective-permute-done.7.refs_0_
  46.2 0.6 collective-permute-start.8
  46.8 0.0 collective-permute-done.9.refs_1_
  46.9 1.9 %collective-permute-start.10 = (bf16[64,3712]{1,0:T(8,128)(2,1)S(1)}, bf16[64,3712]{1,0:T(8,128)(2,1)S(1)}, u32[]{:S(2)}, u32[]{:S(2)}) collective-permute-start(bf16[64,3712]{1,0:T(8,128)(2,1)S(1)} %pad_maximum_fusion.1), channel_id=1, source_target_pairs={{0,8},{8,12},{12,4},{4,0},{1,9},{9,13},{13,5},{5,1},{2,10},{10,14}... | collective-permute-start | bytes 1425416 | tf_op jit(solution)/shard_map/ppermute | solution.py:252
  48.8 7.9 %shard_map.67 = (bf16[64,3584]{1,0:T(8,128)(2,1)S(1)}, bf16[64,3584]{1,0:T(8,128)(2,1)S(1)}) custom-call(s32[1]{0:T(128)} %bitcast.mine, bf16[64,3712]{1,0:T(8,128)(2,1)S(1)} %collective-permute-done.7.refs_0_, bf16[64,3712]{1,0:T(8,128)(2,1)S(1)} %collective-permute-done.9.refs_1_, bf16[1,3584,512]{2,1,0:T(8,128)(2,1)} %refs_2_.5, ...), custom_call_target="tpu_custom_call" | custom-call | flops 2818572288 | bytes 23855104 | tf_op jit(solution)/shard_map/pallas_call | solution.py:209
  56.7 0.2 collective-permute-done.8.refs_0_
  57.0 0.1 add_convert_fusion.3
  57.1 0.7 collective-permute-start.14
  57.9 0.4 collective-permute-done.10.refs_1_
  58.2 0.1 add_convert_fusion.4
  58.4 2.4 %collective-permute-start.11 = (bf16[64,3584]{1,0:T(8,128)(2,1)S(1)}, bf16[64,3584]{1,0:T(8,128)(2,1)S(1)}, u32[]{:S(2)}, u32[]{:S(2)}) collective-permute-start(bf16[64,3584]{1,0:T(8,128)(2,1)S(1)} %pad_maximum_fusion.2), channel_id=1, source_target_pairs={{0,2},{1,3},{2,0},{3,1},{4,6},{5,7},{6,4},{7,5},{8,10},{9,11},{10,... | collective-permute-start | bytes 1376264 | tf_op jit(solution)/shard_map/ppermute | solution.py:16
  60.8 8.0 %shard_map.68 = bf16[64,3584]{1,0:T(8,128)(2,1)S(1)} custom-call(s32[1]{0:T(128)} %bitcast.mine, bf16[64,3712]{1,0:T(8,128)(2,1)S(1)} %collective-permute-done.8.refs_0_, bf16[64,3712]{1,0:T(8,128)(2,1)S(1)} %collective-permute-done.10.refs_1_, bf16[1,3584,512]{2,1,0:T(8,128)(2,1)} %refs_2_.5, bf16[1,3584,512]{2,1,0:T(8,128)(2,1)} %refs_3_.7, ...), custom_call_target="tpu_custom_call" | custom-call | flops 1409286144 | bytes 22937600 | tf_op jit(solution)/shard_map/pallas_call | solution.py:209
  68.8 0.0 collective-permute-done.11
  68.8 0.2 add_convert_fusion.2
  69.0 1.0 %collective-permute-start.15 = (bf16[64,3584]{1,0:T(8,128)(2,1)S(1)}, bf16[64,3584]{1,0:T(8,128)(2,1)S(1)}, u32[]{:S(2)}, u32[]{:S(2)}) collective-permute-start(bf16[64,3584]{1,0:T(8,128)(2,1)S(1)} %add_convert_fusion.2), channel_id=1, source_target_pairs={{0,8},{8,12},{12,4},{4,0},{1,9},{9,13},{13,5},{5,1},{2,10},{10,14}... | collective-permute-start | bytes 1376264 | tf_op jit(solution)/shard_map/ppermute | solution.py:252
  70.0 1.7 %collective-permute-start.12 = (bf16[64,3584]{1,0:T(8,128)(2,1)S(1)}, bf16[64,3584]{1,0:T(8,128)(2,1)S(1)}, u32[]{:S(2)}, u32[]{:S(2)}) collective-permute-start(bf16[64,3584]{1,0:T(8,128)(2,1)S(1)} %compare_select_fusion.3), channel_id=1, source_target_pairs={{0,2},{1,3},{2,0},{3,1},{4,6},{5,7},{6,4},{7,5},{8,10},{9,11},{10,... | collective-permute-start | bytes 1376264 | tf_op jit(solution)/shard_map/ppermute | solution.py:16
  71.7 5.8 %collective-permute-done.15 = bf16[64,3584]{1,0:T(8,128)(2,1)S(1)} collective-permute-done((bf16[64,3584]{1,0:T(8,128)(2,1)S(1)}, bf16[64,3584]{1,0:T(8,128)(2,1)S(1)}, u32[]{:S(2)}, u32[]{:S(2)}) %collective-permute-start.15) | collective-permute-done | bytes 458784 | tf_op jit(solution)/shard_map/ppermute | solution.py:252
  77.5 2.0 %collective-permute-done.12 = bf16[64,3584]{1,0:T(8,128)(2,1)S(1)} collective-permute-done((bf16[64,3584]{1,0:T(8,128)(2,1)S(1)}, bf16[64,3584]{1,0:T(8,128)(2,1)S(1)}, u32[]{:S(2)}, u32[]{:S(2)}) %collective-permute-start.12) | collective-permute-done | bytes 458784 | tf_op jit(solution)/shard_map/ppermute | solution.py:16
  79.5 0.2 add_convert_fusion.1
  79.7 1.1 %collective-permute-start.16 = (bf16[64,3584]{1,0:T(8,128)(2,1)S(1)}, bf16[64,3584]{1,0:T(8,128)(2,1)S(1)}, u32[]{:S(2)}, u32[]{:S(2)}) collective-permute-start(bf16[64,3584]{1,0:T(8,128)(2,1)S(1)} %add_convert_fusion.1), channel_id=1, source_target_pairs={{0,8},{8,12},{12,4},{4,0},{1,9},{9,13},{13,5},{5,1},{2,10},{10,14}... | collective-permute-start | bytes 1376264 | tf_op jit(solution)/shard_map/ppermute | solution.py:252
  80.9 1.5 %collective-permute-start.13 = (bf16[64,3584]{1,0:T(8,128)(2,1)S(1)}, bf16[64,3584]{1,0:T(8,128)(2,1)S(1)}, u32[]{:S(2)}, u32[]{:S(2)}) collective-permute-start(bf16[64,3584]{1,0:T(8,128)(2,1)S(1)} %compare_select_fusion.2), channel_id=1, source_target_pairs={{0,2},{1,3},{2,0},{3,1},{4,6},{5,7},{6,4},{7,5},{8,10},{9,11},{10,... | collective-permute-start | bytes 1376264 | tf_op jit(solution)/shard_map/ppermute | solution.py:16
  82.3 5.9 %collective-permute-done.16 = bf16[64,3584]{1,0:T(8,128)(2,1)S(1)} collective-permute-done((bf16[64,3584]{1,0:T(8,128)(2,1)S(1)}, bf16[64,3584]{1,0:T(8,128)(2,1)S(1)}, u32[]{:S(2)}, u32[]{:S(2)}) %collective-permute-start.16) | collective-permute-done | bytes 458784 | tf_op jit(solution)/shard_map/ppermute | solution.py:252
  88.3 1.2 %collective-permute-done.13 = bf16[64,3584]{1,0:T(8,128)(2,1)S(1)} collective-permute-done((bf16[64,3584]{1,0:T(8,128)(2,1)S(1)}, bf16[64,3584]{1,0:T(8,128)(2,1)S(1)}, u32[]{:S(2)}, u32[]{:S(2)}) %collective-permute-start.13) | collective-permute-done | bytes 458784 | tf_op jit(solution)/shard_map/ppermute | solution.py:16
  89.5 0.9 %add_convert_fusion = bf16[64,3584]{1,0:T(8,128)(2,1)} fusion(bf16[64,3584]{1,0:T(8,128)(2,1)S(1)} %collective-permute-done.16, bf16[64,3584]{1,0:T(8,128)(2,1)S(1)} %collective-permute-done.13, bf16[64,3584]{1,0:T(8,128)(2,1)S(1)} %get-tuple-element.13), kind=kLoop, calls=%fused_computation.4 | loop fusion | flops 1376256 | bytes 1835008 | tf_op jit(solution)/shard_map/convert_element_type | solution.py:232
  (16 shorter events, 0.3 us)
Async XLA Ops:
  0.0 22.9 %collective-permute-start.1 = (bf16[1,3584,512]{2,1,0:T(8,128)(2,1)}, bf16[1,3584,512]{2,1,0:T(8,128)(2,1)}, u32[]{:S(2)}, u32[]{:S(2)}) collective-permute-start(bf16[1,3584,512]{2,1,0:T(8,128)(2,1)} %refs_2_.5), channel_id=1, source_target_pairs={{0,1},{1,0},{2,3},{3,2},{4,5},{5,4},{6,7},{7,6},{8,9},{9,8},{10,11... | collective-permute-start | bytes 11010056 | tf_op jit(solution)/shard_map/ppermute | solution.py:16
  0.5 22.4 %collective-permute-start.2 = (bf16[1,3584,512]{2,1,0:T(8,128)(2,1)}, bf16[1,3584,512]{2,1,0:T(8,128)(2,1)}, u32[]{:S(2)}, u32[]{:S(2)}) collective-permute-start(bf16[1,3584,512]{2,1,0:T(8,128)(2,1)} %refs_3_.7), channel_id=1, source_target_pairs={{0,1},{1,0},{2,3},{3,2},{4,5},{5,4},{6,7},{7,6},{8,9},{9,8},{10,11... | collective-permute-start | bytes 11010056 | tf_op jit(solution)/shard_map/ppermute | solution.py:16
  0.5 22.4 %collective-permute-start.3 = (bf16[1,512,3584]{2,1,0:T(8,128)(2,1)}, bf16[1,512,3584]{2,1,0:T(8,128)(2,1)}, u32[]{:S(2)}, u32[]{:S(2)}) collective-permute-start(bf16[1,512,3584]{2,1,0:T(8,128)(2,1)} %refs_4_.7), channel_id=1, source_target_pairs={{0,1},{1,0},{2,3},{3,2},{4,5},{5,4},{6,7},{7,6},{8,9},{9,8},{10,11... | collective-permute-start | bytes 11010056 | tf_op jit(solution)/shard_map/ppermute | solution.py:16
  2.9 14.7 %collective-permute-start.4 = (bf16[64,3712]{1,0:T(8,128)(2,1)}, bf16[64,3712]{1,0:T(8,128)(2,1)S(1)}, u32[]{:S(2)}, u32[]{:S(2)}) collective-permute-start(bf16[64,3712]{1,0:T(8,128)(2,1)} %shard_map.64.refs_0_), channel_id=1, source_target_pairs={{0,8},{8,12},{12,4},{4,0},{1,9},{9,13},{13,5},{5,1},{2,10},{10,14}... | collective-permute-start | bytes 1425416 | tf_op jit(solution)/shard_map/ppermute | solution.py:252
  6.5 13.2 %collective-permute-start = (bf16[64,3712]{1,0:T(8,128)(2,1)}, bf16[64,3712]{1,0:T(8,128)(2,1)S(1)}, u32[]{:S(2)}, u32[]{:S(2)}) collective-permute-start(bf16[64,3712]{1,0:T(8,128)(2,1)} %shard_map.64.refs_0_), channel_id=1, source_target_pairs={{0,2},{1,3},{2,0},{3,1},{4,6},{5,7},{6,4},{7,5},{8,10},{9,11},{10,... | collective-permute-start | bytes 1425416 | tf_op jit(solution)/shard_map/ppermute | solution.py:16
  19.8 12.3 %collective-permute-start.6 = (bf16[64,3712]{1,0:T(8,128)(2,1)S(1)}, bf16[64,3712]{1,0:T(8,128)(2,1)S(1)}, u32[]{:S(2)}, u32[]{:S(2)}) collective-permute-start(bf16[64,3712]{1,0:T(8,128)(2,1)S(1)} %compare_select_fusion.1.refs_0_), channel_id=1, source_target_pairs={{0,8},{8,12},{12,4},{4,0},{1,9},{9,13},{13,5},{5,1},{2,10},{10,14}... | collective-permute-start | bytes 1425416 | tf_op jit(solution)/shard_map/ppermute | solution.py:252
  21.4 11.9 %collective-permute-start.5 = (bf16[64,3712]{1,0:T(8,128)(2,1)S(1)}, bf16[64,3712]{1,0:T(8,128)(2,1)S(1)}, u32[]{:S(2)}, u32[]{:S(2)}) collective-permute-start(bf16[64,3712]{1,0:T(8,128)(2,1)S(1)} %compare_select_fusion.1.refs_0_), channel_id=1, source_target_pairs={{0,2},{1,3},{2,0},{3,1},{4,6},{5,7},{6,4},{7,5},{8,10},{9,11},{10,... | collective-permute-start | bytes 1425416 | tf_op jit(solution)/shard_map/ppermute | solution.py:16
  22.9 1.0 %copy-start = (bf16[64,3712]{1,0:T(8,128)(2,1)S(1)}, bf16[64,3712]{1,0:T(8,128)(2,1)}, u32[]{:S(2)}) copy-start(bf16[64,3712]{1,0:T(8,128)(2,1)} %shard_map.64.refs_0_) | copy-start | bytes 1425412
  33.3 2.9 %copy-start.1 = (bf16[64,3712]{1,0:T(8,128)(2,1)}, bf16[64,3712]{1,0:T(8,128)(2,1)S(1)}, u32[]{:S(2)}) copy-start(bf16[64,3712]{1,0:T(8,128)(2,1)S(1)} %collective-permute-done.5.refs_2_) | copy-start | bytes 1425412
  33.4 2.7 %copy-start.2 = (bf16[64,3712]{1,0:T(8,128)(2,1)}, bf16[64,3712]{1,0:T(8,128)(2,1)S(1)}, u32[]{:S(2)}) copy-start(bf16[64,3712]{1,0:T(8,128)(2,1)S(1)} %fusion.refs_1_) | copy-start | bytes 1425412
  33.4 12.7 %collective-permute-start.7 = (bf16[64,3712]{1,0:T(8,128)(2,1)S(1)}, bf16[64,3712]{1,0:T(8,128)(2,1)S(1)}, u32[]{:S(2)}, u32[]{:S(2)}) collective-permute-start(bf16[64,3712]{1,0:T(8,128)(2,1)S(1)} %fusion.refs_1_), channel_id=1, source_target_pairs={{0,8},{8,12},{12,4},{4,0},{1,9},{9,13},{13,5},{5,1},{2,10},{10,14}... | collective-permute-start | bytes 1425416 | tf_op jit(solution)/shard_map/ppermute | solution.py:252
  34.7 12.1 %collective-permute-start.9 = (bf16[64,3712]{1,0:T(8,128)(2,1)S(1)}, bf16[64,3712]{1,0:T(8,128)(2,1)S(1)}, u32[]{:S(2)}, u32[]{:S(2)}) collective-permute-start(bf16[64,3712]{1,0:T(8,128)(2,1)S(1)} %fusion.refs_1_), channel_id=1, source_target_pairs={{0,2},{1,3},{2,0},{3,1},{4,6},{5,7},{6,4},{7,5},{8,10},{9,11},{10,... | collective-permute-start | bytes 1425416 | tf_op jit(solution)/shard_map/ppermute | solution.py:16
  46.2 10.8 %collective-permute-start.8 = (bf16[64,3712]{1,0:T(8,128)(2,1)S(1)}, bf16[64,3712]{1,0:T(8,128)(2,1)S(1)}, u32[]{:S(2)}, u32[]{:S(2)}) collective-permute-start(bf16[64,3712]{1,0:T(8,128)(2,1)S(1)} %pad_maximum_fusion), channel_id=1, source_target_pairs={{0,2},{1,3},{2,0},{3,1},{4,6},{5,7},{6,4},{7,5},{8,10},{9,11},{10,... | collective-permute-start | bytes 1425416 | tf_op jit(solution)/shard_map/ppermute | solution.py:16
  46.9 11.4 %collective-permute-start.10 = (bf16[64,3712]{1,0:T(8,128)(2,1)S(1)}, bf16[64,3712]{1,0:T(8,128)(2,1)S(1)}, u32[]{:S(2)}, u32[]{:S(2)}) collective-permute-start(bf16[64,3712]{1,0:T(8,128)(2,1)S(1)} %pad_maximum_fusion.1), channel_id=1, source_target_pairs={{0,8},{8,12},{12,4},{4,0},{1,9},{9,13},{13,5},{5,1},{2,10},{10,14}... | collective-permute-start | bytes 1425416 | tf_op jit(solution)/shard_map/ppermute | solution.py:252
  57.1 11.7 %collective-permute-start.14 = (bf16[64,3584]{1,0:T(8,128)(2,1)S(1)}, bf16[64,3584]{1,0:T(8,128)(2,1)S(1)}, u32[]{:S(2)}, u32[]{:S(2)}) collective-permute-start(bf16[64,3584]{1,0:T(8,128)(2,1)S(1)} %pad_maximum_fusion.3), channel_id=1, source_target_pairs={{0,8},{8,12},{12,4},{4,0},{1,9},{9,13},{13,5},{5,1},{2,10},{10,14}... | collective-permute-start | bytes 1376264 | tf_op jit(solution)/shard_map/ppermute | solution.py:252
  58.4 10.4 %collective-permute-start.11 = (bf16[64,3584]{1,0:T(8,128)(2,1)S(1)}, bf16[64,3584]{1,0:T(8,128)(2,1)S(1)}, u32[]{:S(2)}, u32[]{:S(2)}) collective-permute-start(bf16[64,3584]{1,0:T(8,128)(2,1)S(1)} %pad_maximum_fusion.2), channel_id=1, source_target_pairs={{0,2},{1,3},{2,0},{3,1},{4,6},{5,7},{6,4},{7,5},{8,10},{9,11},{10,... | collective-permute-start | bytes 1376264 | tf_op jit(solution)/shard_map/ppermute | solution.py:16
  69.0 8.5 %collective-permute-start.15 = (bf16[64,3584]{1,0:T(8,128)(2,1)S(1)}, bf16[64,3584]{1,0:T(8,128)(2,1)S(1)}, u32[]{:S(2)}, u32[]{:S(2)}) collective-permute-start(bf16[64,3584]{1,0:T(8,128)(2,1)S(1)} %add_convert_fusion.2), channel_id=1, source_target_pairs={{0,8},{8,12},{12,4},{4,0},{1,9},{9,13},{13,5},{5,1},{2,10},{10,14}... | collective-permute-start | bytes 1376264 | tf_op jit(solution)/shard_map/ppermute | solution.py:252
  70.0 9.5 %collective-permute-start.12 = (bf16[64,3584]{1,0:T(8,128)(2,1)S(1)}, bf16[64,3584]{1,0:T(8,128)(2,1)S(1)}, u32[]{:S(2)}, u32[]{:S(2)}) collective-permute-start(bf16[64,3584]{1,0:T(8,128)(2,1)S(1)} %compare_select_fusion.3), channel_id=1, source_target_pairs={{0,2},{1,3},{2,0},{3,1},{4,6},{5,7},{6,4},{7,5},{8,10},{9,11},{10,... | collective-permute-start | bytes 1376264 | tf_op jit(solution)/shard_map/ppermute | solution.py:16
  79.7 8.6 %collective-permute-start.16 = (bf16[64,3584]{1,0:T(8,128)(2,1)S(1)}, bf16[64,3584]{1,0:T(8,128)(2,1)S(1)}, u32[]{:S(2)}, u32[]{:S(2)}) collective-permute-start(bf16[64,3584]{1,0:T(8,128)(2,1)S(1)} %add_convert_fusion.1), channel_id=1, source_target_pairs={{0,8},{8,12},{12,4},{4,0},{1,9},{9,13},{13,5},{5,1},{2,10},{10,14}... | collective-permute-start | bytes 1376264 | tf_op jit(solution)/shard_map/ppermute | solution.py:252
  80.9 8.6 %collective-permute-start.13 = (bf16[64,3584]{1,0:T(8,128)(2,1)S(1)}, bf16[64,3584]{1,0:T(8,128)(2,1)S(1)}, u32[]{:S(2)}, u32[]{:S(2)}) collective-permute-start(bf16[64,3584]{1,0:T(8,128)(2,1)S(1)} %compare_select_fusion.2), channel_id=1, source_target_pairs={{0,2},{1,3},{2,0},{3,1},{4,6},{5,7},{6,4},{7,5},{8,10},{9,11},{10,... | collective-permute-start | bytes 1376264 | tf_op jit(solution)/shard_map/ppermute | solution.py:16

commit v6 on v5

--- a/solution.py
+++ b/solution.py
@@ -128,7 +128,7 @@
 def pack(tokens, expert_ids, gate_scores, pieces):
     rows, width = tokens.shape
     vmem = pl.BlockSpec(memory_space=pltpu.VMEM)
-    shape = jax.ShapeDtypeStruct((rows // pieces, width + LANES), tokens.dtype)
+    shape = pltpu.VMEM((rows // pieces, width + LANES), tokens.dtype)
     return pl.pallas_call(
         pack_kernel,
         out_shape=[shape] * pieces,

time: 90.6 us -> 89.7 us (0.990)
  local copies, waits for them, and re-layouts: 1.18 us -> 0.17 us
    unnamed x6 -> x4, local copies, waits for them, and re-layouts: 1.03 us -> 0.01 us
  transfers between devices with their start and end apart: 17 -> 17, of which waited for: 9 -> 10; matrix products, arithmetic and copies ran while one was open for 1% -> 1% of each run, Pallas kernels for 40% -> 39%
where the time goes in v6:
time: 89.7 us; the launch traced here: 89.5 us
  Pallas kernels  35 us (39%)
  waiting for transfers between devices  29.4 us (33%)
  starting transfers between devices  22.8 us (25%)
  other arithmetic  1.96 us (2%)
    pallas_call x4, Pallas kernels, expert_rows(): pl.pallas_call(functools.partial(expert_kernel, ranges, down_tiles, hidde...  33.8 us
    ppermute x7, waiting for transfers between devices, next_node(): return lax.ppermute(value, 'node', list(zip(ring, ring[1:] + ring[:1])))  22.4 us
    ppermute x10, starting transfers between devices, partner(): return lax.ppermute(value, axis, pairs)  11.6 us
    ppermute x7, starting transfers between devices, next_node(): return lax.ppermute(value, 'node', list(zip(ring, ring[1:] + ring[:1])))  11.3 us
    ppermute x10, waiting for transfers between devices, partner(): return lax.ppermute(value, axis, pairs)  6.97 us
  transfers between devices with their start and end apart: 17, of which 10 were waited for; matrix products, arithmetic and copies ran while one was open for 1% of the time, Pallas kernels for 39%

profile of v6, /device:TPU:0, one launch (start us, length us, event | category | flops | bytes accessed | tf_op | source)
XLA Modules:
  0.0 89.5 jit_solution(12768638591366837766)
XLA Ops:
  0.0 0.5 collective-permute-start.1
  0.5 0.1 collective-permute-start.2
  0.5 0.5 collective-permute-start.3
  1.0 1.2 %shard_map.64.refs_0_ = bf16[64,3712]{1,0:T(8,128)(2,1)S(1)} custom-call(bf16[64,3584]{1,0:T(8,128)(2,1)} %tokens.1, s32[8,64]{1,0:T(8,128)} %bitcast.3, bf16[8,64]{1,0:T(8,128)(2,1)} %bitcast.4), custom_call_target="tpu_custom_call" | custom-call | tf_op jit(solution)/shard_map/pallas_call | solution.py:132
  2.1 3.6 %collective-permute-start.4 = (bf16[64,3712]{1,0:T(8,128)(2,1)S(1)}, bf16[64,3712]{1,0:T(8,128)(2,1)S(1)}, u32[]{:S(2)}, u32[]{:S(2)}) collective-permute-start(bf16[64,3712]{1,0:T(8,128)(2,1)S(1)} %shard_map.64.refs_0_), channel_id=1, source_target_pairs={{0,8},{8,12},{12,4},{4,0},{1,9},{9,13},{13,5},{5,1},{2,10},{10,14}... | collective-permute-start | bytes 1425416 | tf_op jit(solution)/shard_map/ppermute | solution.py:252
  5.8 1.5 %collective-permute-start = (bf16[64,3712]{1,0:T(8,128)(2,1)S(1)}, bf16[64,3712]{1,0:T(8,128)(2,1)S(1)}, u32[]{:S(2)}, u32[]{:S(2)}) collective-permute-start(bf16[64,3712]{1,0:T(8,128)(2,1)S(1)} %shard_map.64.refs_0_), channel_id=1, source_target_pairs={{0,2},{1,3},{2,0},{3,1},{4,6},{5,7},{6,4},{7,5},{8,10},{9,11},{10,... | collective-permute-start | bytes 1425416 | tf_op jit(solution)/shard_map/ppermute | solution.py:16
  7.3 9.3 %collective-permute-done.4 = bf16[64,3712]{1,0:T(8,128)(2,1)S(1)} collective-permute-done((bf16[64,3712]{1,0:T(8,128)(2,1)S(1)}, bf16[64,3712]{1,0:T(8,128)(2,1)S(1)}, u32[]{:S(2)}, u32[]{:S(2)}) %collective-permute-start.4) | collective-permute-done | bytes 475168 | tf_op jit(solution)/shard_map/ppermute | solution.py:252
  16.6 2.2 %collective-permute-done.refs_1_ = bf16[64,3712]{1,0:T(8,128)(2,1)S(1)} collective-permute-done((bf16[64,3712]{1,0:T(8,128)(2,1)S(1)}, bf16[64,3712]{1,0:T(8,128)(2,1)S(1)}, u32[]{:S(2)}, u32[]{:S(2)}) %collective-permute-start) | collective-permute-done | bytes 475168 | tf_op jit(solution)/shard_map/ppermute | solution.py:16
  18.8 0.1 compare_select_fusion.1.refs_0_
  18.8 1.6 %collective-permute-start.6 = (bf16[64,3712]{1,0:T(8,128)(2,1)S(1)}, bf16[64,3712]{1,0:T(8,128)(2,1)S(1)}, u32[]{:S(2)}, u32[]{:S(2)}) collective-permute-start(bf16[64,3712]{1,0:T(8,128)(2,1)S(1)} %compare_select_fusion.1.refs_0_), channel_id=1, source_target_pairs={{0,8},{8,12},{12,4},{4,0},{1,9},{9,13},{13,5},{5,1},{2,10},{10,14}... | collective-permute-start | bytes 1425416 | tf_op jit(solution)/shard_map/ppermute | solution.py:252
  20.5 1.5 %collective-permute-start.5 = (bf16[64,3712]{1,0:T(8,128)(2,1)S(1)}, bf16[64,3712]{1,0:T(8,128)(2,1)S(1)}, u32[]{:S(2)}, u32[]{:S(2)}) collective-permute-start(bf16[64,3712]{1,0:T(8,128)(2,1)S(1)} %compare_select_fusion.1.refs_0_), channel_id=1, source_target_pairs={{0,2},{1,3},{2,0},{3,1},{4,6},{5,7},{6,4},{7,5},{8,10},{9,11},{10,... | collective-permute-start | bytes 1425416 | tf_op jit(solution)/shard_map/ppermute | solution.py:16
  22.0 0.0 collective-permute-done.1.refs_5_.refs_6_
  22.0 0.0 collective-permute-done.2.refs_6_.refs_7_
  22.0 0.0 collective-permute-done.3.refs_7_.refs_8_
  22.0 8.0 %shard_map.65 = (bf16[64,3584]{1,0:T(8,128)(2,1)S(1)}, bf16[64,3584]{1,0:T(8,128)(2,1)S(1)}) custom-call(s32[1]{0:T(128)} %bitcast.mine, bf16[64,3712]{1,0:T(8,128)(2,1)S(1)} %shard_map.64.refs_0_, bf16[64,3712]{1,0:T(8,128)(2,1)S(1)} %collective-permute-done.refs_1_, bf16[1,3584,512]{2,1,0:T(8,128)(2,1)} %refs_2_.5, bf16[1,3584,512]{2,1,0:T(8,128)(2,1)} %refs_3_.7, ...), custom_call_target="tpu_custom_call" | custom-call | flops 2818572288 | bytes 23855104 | tf_op jit(solution)/shard_map/pallas_call | solution.py:209
  29.9 0.1 slice_reduce_fusion
  30.0 0.1 compare_reduce_fusion
  30.2 0.9 %collective-permute-done.6 = bf16[64,3712]{1,0:T(8,128)(2,1)S(1)} collective-permute-done((bf16[64,3712]{1,0:T(8,128)(2,1)S(1)}, bf16[64,3712]{1,0:T(8,128)(2,1)S(1)}, u32[]{:S(2)}, u32[]{:S(2)}) %collective-permute-start.6) | collective-permute-done | bytes 475168 | tf_op jit(solution)/shard_map/ppermute | solution.py:252
  31.1 1.3 %collective-permute-done.5.refs_2_ = bf16[64,3712]{1,0:T(8,128)(2,1)S(1)} collective-permute-done((bf16[64,3712]{1,0:T(8,128)(2,1)S(1)}, bf16[64,3712]{1,0:T(8,128)(2,1)S(1)}, u32[]{:S(2)}, u32[]{:S(2)}) %collective-permute-start.5) | collective-permute-done | bytes 475168 | tf_op jit(solution)/shard_map/ppermute | solution.py:16
  32.4 0.1 fusion.refs_1_
  32.5 1.2 %collective-permute-start.7 = (bf16[64,3712]{1,0:T(8,128)(2,1)S(1)}, bf16[64,3712]{1,0:T(8,128)(2,1)S(1)}, u32[]{:S(2)}, u32[]{:S(2)}) collective-permute-start(bf16[64,3712]{1,0:T(8,128)(2,1)S(1)} %fusion.refs_1_), channel_id=1, source_target_pairs={{0,8},{8,12},{12,4},{4,0},{1,9},{9,13},{13,5},{5,1},{2,10},{10,14}... | collective-permute-start | bytes 1425416 | tf_op jit(solution)/shard_map/ppermute | solution.py:252
  33.8 1.5 %collective-permute-start.9 = (bf16[64,3712]{1,0:T(8,128)(2,1)S(1)}, bf16[64,3712]{1,0:T(8,128)(2,1)S(1)}, u32[]{:S(2)}, u32[]{:S(2)}) collective-permute-start(bf16[64,3712]{1,0:T(8,128)(2,1)S(1)} %fusion.refs_1_), channel_id=1, source_target_pairs={{0,2},{1,3},{2,0},{3,1},{4,6},{5,7},{6,4},{7,5},{8,10},{9,11},{10,... | collective-permute-start | bytes 1425416 | tf_op jit(solution)/shard_map/ppermute | solution.py:16
  35.3 9.9 %shard_map.66 = (bf16[64,3584]{1,0:T(8,128)(2,1)S(1)}, bf16[64,3584]{1,0:T(8,128)(2,1)S(1)}, bf16[32,3712]{1,0:T(8,128)(2,1)S(1)}, bf16[32,3712]{1,0:T(8,128)(2,1)S(1)}) custom-call(s32[1]{0:T(128)} %bitcast.mine, bf16[64,3712]{1,0:T(8,128)(2,1)S(1)} %compare_select_fusion.1.refs_0_, bf16[64,3712]{1,0:T(8,128)(2,1)} %copy-done.1, bf16[64,3712]{1,0:T(8,128)(2,1)} %copy-done, ...), custom_call_target="tpu_custom_call" | custom-call | flops 4227858432 | bytes 24772608 | tf_op jit(solution)/shard_map/pallas_call | solution.py:209
  45.2 0.0 collective-permute-done.7.refs_0_
  45.3 0.6 collective-permute-start.8
  45.9 0.0 collective-permute-done.9.refs_1_
  46.0 1.9 %collective-permute-start.10 = (bf16[64,3712]{1,0:T(8,128)(2,1)S(1)}, bf16[64,3712]{1,0:T(8,128)(2,1)S(1)}, u32[]{:S(2)}, u32[]{:S(2)}) collective-permute-start(bf16[64,3712]{1,0:T(8,128)(2,1)S(1)} %pad_maximum_fusion.1), channel_id=1, source_target_pairs={{0,8},{8,12},{12,4},{4,0},{1,9},{9,13},{13,5},{5,1},{2,10},{10,14}... | collective-permute-start | bytes 1425416 | tf_op jit(solution)/shard_map/ppermute | solution.py:252
  47.9 7.9 %shard_map.67 = (bf16[64,3584]{1,0:T(8,128)(2,1)S(1)}, bf16[64,3584]{1,0:T(8,128)(2,1)S(1)}) custom-call(s32[1]{0:T(128)} %bitcast.mine, bf16[64,3712]{1,0:T(8,128)(2,1)S(1)} %collective-permute-done.7.refs_0_, bf16[64,3712]{1,0:T(8,128)(2,1)S(1)} %collective-permute-done.9.refs_1_, bf16[1,3584,512]{2,1,0:T(8,128)(2,1)} %refs_2_.5, ...), custom_call_target="tpu_custom_call" | custom-call | flops 2818572288 | bytes 23855104 | tf_op jit(solution)/shard_map/pallas_call | solution.py:209
  55.8 0.2 collective-permute-done.8.refs_0_
  56.0 0.1 add_convert_fusion.3
  56.1 0.8 collective-permute-start.14
  56.9 0.4 collective-permute-done.10.refs_1_
  57.4 0.1 add_convert_fusion.4
  57.5 2.4 %collective-permute-start.11 = (bf16[64,3584]{1,0:T(8,128)(2,1)S(1)}, bf16[64,3584]{1,0:T(8,128)(2,1)S(1)}, u32[]{:S(2)}, u32[]{:S(2)}) collective-permute-start(bf16[64,3584]{1,0:T(8,128)(2,1)S(1)} %pad_maximum_fusion.2), channel_id=1, source_target_pairs={{0,2},{1,3},{2,0},{3,1},{4,6},{5,7},{6,4},{7,5},{8,10},{9,11},{10,... | collective-permute-start | bytes 1376264 | tf_op jit(solution)/shard_map/ppermute | solution.py:16
  59.8 8.0 %shard_map.68 = bf16[64,3584]{1,0:T(8,128)(2,1)S(1)} custom-call(s32[1]{0:T(128)} %bitcast.mine, bf16[64,3712]{1,0:T(8,128)(2,1)S(1)} %collective-permute-done.8.refs_0_, bf16[64,3712]{1,0:T(8,128)(2,1)S(1)} %collective-permute-done.10.refs_1_, bf16[1,3584,512]{2,1,0:T(8,128)(2,1)} %refs_2_.5, bf16[1,3584,512]{2,1,0:T(8,128)(2,1)} %refs_3_.7, ...), custom_call_target="tpu_custom_call" | custom-call | flops 1409286144 | bytes 22937600 | tf_op jit(solution)/shard_map/pallas_call | solution.py:209
  67.9 0.0 collective-permute-done.14
  67.9 0.0 collective-permute-done.11
  67.9 0.2 add_convert_fusion.2
  68.1 1.0 %collective-permute-start.15 = (bf16[64,3584]{1,0:T(8,128)(2,1)S(1)}, bf16[64,3584]{1,0:T(8,128)(2,1)S(1)}, u32[]{:S(2)}, u32[]{:S(2)}) collective-permute-start(bf16[64,3584]{1,0:T(8,128)(2,1)S(1)} %add_convert_fusion.2), channel_id=1, source_target_pairs={{0,8},{8,12},{12,4},{4,0},{1,9},{9,13},{13,5},{5,1},{2,10},{10,14}... | collective-permute-start | bytes 1376264 | tf_op jit(solution)/shard_map/ppermute | solution.py:252
  69.1 1.7 %collective-permute-start.12 = (bf16[64,3584]{1,0:T(8,128)(2,1)S(1)}, bf16[64,3584]{1,0:T(8,128)(2,1)S(1)}, u32[]{:S(2)}, u32[]{:S(2)}) collective-permute-start(bf16[64,3584]{1,0:T(8,128)(2,1)S(1)} %compare_select_fusion.3), channel_id=1, source_target_pairs={{0,2},{1,3},{2,0},{3,1},{4,6},{5,7},{6,4},{7,5},{8,10},{9,11},{10,... | collective-permute-start | bytes 1376264 | tf_op jit(solution)/shard_map/ppermute | solution.py:16
  70.8 5.8 %collective-permute-done.15 = bf16[64,3584]{1,0:T(8,128)(2,1)S(1)} collective-permute-done((bf16[64,3584]{1,0:T(8,128)(2,1)S(1)}, bf16[64,3584]{1,0:T(8,128)(2,1)S(1)}, u32[]{:S(2)}, u32[]{:S(2)}) %collective-permute-start.15) | collective-permute-done | bytes 458784 | tf_op jit(solution)/shard_map/ppermute | solution.py:252
  76.6 2.0 %collective-permute-done.12 = bf16[64,3584]{1,0:T(8,128)(2,1)S(1)} collective-permute-done((bf16[64,3584]{1,0:T(8,128)(2,1)S(1)}, bf16[64,3584]{1,0:T(8,128)(2,1)S(1)}, u32[]{:S(2)}, u32[]{:S(2)}) %collective-permute-start.12) | collective-permute-done | bytes 458784 | tf_op jit(solution)/shard_map/ppermute | solution.py:16
  78.6 0.2 add_convert_fusion.1
  78.8 1.1 %collective-permute-start.16 = (bf16[64,3584]{1,0:T(8,128)(2,1)S(1)}, bf16[64,3584]{1,0:T(8,128)(2,1)S(1)}, u32[]{:S(2)}, u32[]{:S(2)}) collective-permute-start(bf16[64,3584]{1,0:T(8,128)(2,1)S(1)} %add_convert_fusion.1), channel_id=1, source_target_pairs={{0,8},{8,12},{12,4},{4,0},{1,9},{9,13},{13,5},{5,1},{2,10},{10,14}... | collective-permute-start | bytes 1376264 | tf_op jit(solution)/shard_map/ppermute | solution.py:252
  80.0 1.5 %collective-permute-start.13 = (bf16[64,3584]{1,0:T(8,128)(2,1)S(1)}, bf16[64,3584]{1,0:T(8,128)(2,1)S(1)}, u32[]{:S(2)}, u32[]{:S(2)}) collective-permute-start(bf16[64,3584]{1,0:T(8,128)(2,1)S(1)} %compare_select_fusion.2), channel_id=1, source_target_pairs={{0,2},{1,3},{2,0},{3,1},{4,6},{5,7},{6,4},{7,5},{8,10},{9,11},{10,... | collective-permute-start | bytes 1376264 | tf_op jit(solution)/shard_map/ppermute | solution.py:16
  81.4 5.9 %collective-permute-done.16 = bf16[64,3584]{1,0:T(8,128)(2,1)S(1)} collective-permute-done((bf16[64,3584]{1,0:T(8,128)(2,1)S(1)}, bf16[64,3584]{1,0:T(8,128)(2,1)S(1)}, u32[]{:S(2)}, u32[]{:S(2)}) %collective-permute-start.16) | collective-permute-done | bytes 458784 | tf_op jit(solution)/shard_map/ppermute | solution.py:252
  87.4 1.2 %collective-permute-done.13 = bf16[64,3584]{1,0:T(8,128)(2,1)S(1)} collective-permute-done((bf16[64,3584]{1,0:T(8,128)(2,1)S(1)}, bf16[64,3584]{1,0:T(8,128)(2,1)S(1)}, u32[]{:S(2)}, u32[]{:S(2)}) %collective-permute-start.13) | collective-permute-done | bytes 458784 | tf_op jit(solution)/shard_map/ppermute | solution.py:16
  88.6 0.9 %add_convert_fusion = bf16[64,3584]{1,0:T(8,128)(2,1)} fusion(bf16[64,3584]{1,0:T(8,128)(2,1)S(1)} %collective-permute-done.16, bf16[64,3584]{1,0:T(8,128)(2,1)S(1)} %collective-permute-done.13, bf16[64,3584]{1,0:T(8,128)(2,1)S(1)} %get-tuple-element.13), kind=kLoop, calls=%fused_computation.4 | loop fusion | flops 1376256 | bytes 1835008 | tf_op jit(solution)/shard_map/convert_element_type | solution.py:232
  (14 shorter events, 0.3 us)
Async XLA Ops:
  0.0 22.0 %collective-permute-start.1 = (bf16[1,3584,512]{2,1,0:T(8,128)(2,1)}, bf16[1,3584,512]{2,1,0:T(8,128)(2,1)}, u32[]{:S(2)}, u32[]{:S(2)}) collective-permute-start(bf16[1,3584,512]{2,1,0:T(8,128)(2,1)} %refs_2_.5), channel_id=1, source_target_pairs={{0,1},{1,0},{2,3},{3,2},{4,5},{5,4},{6,7},{7,6},{8,9},{9,8},{10,11... | collective-permute-start | bytes 11010056 | tf_op jit(solution)/shard_map/ppermute | solution.py:16
  0.5 21.5 %collective-permute-start.2 = (bf16[1,3584,512]{2,1,0:T(8,128)(2,1)}, bf16[1,3584,512]{2,1,0:T(8,128)(2,1)}, u32[]{:S(2)}, u32[]{:S(2)}) collective-permute-start(bf16[1,3584,512]{2,1,0:T(8,128)(2,1)} %refs_3_.7), channel_id=1, source_target_pairs={{0,1},{1,0},{2,3},{3,2},{4,5},{5,4},{6,7},{7,6},{8,9},{9,8},{10,11... | collective-permute-start | bytes 11010056 | tf_op jit(solution)/shard_map/ppermute | solution.py:16
  0.5 21.5 %collective-permute-start.3 = (bf16[1,512,3584]{2,1,0:T(8,128)(2,1)}, bf16[1,512,3584]{2,1,0:T(8,128)(2,1)}, u32[]{:S(2)}, u32[]{:S(2)}) collective-permute-start(bf16[1,512,3584]{2,1,0:T(8,128)(2,1)} %refs_4_.7), channel_id=1, source_target_pairs={{0,1},{1,0},{2,3},{3,2},{4,5},{5,4},{6,7},{7,6},{8,9},{9,8},{10,11... | collective-permute-start | bytes 11010056 | tf_op jit(solution)/shard_map/ppermute | solution.py:16
  2.1 14.4 %collective-permute-start.4 = (bf16[64,3712]{1,0:T(8,128)(2,1)S(1)}, bf16[64,3712]{1,0:T(8,128)(2,1)S(1)}, u32[]{:S(2)}, u32[]{:S(2)}) collective-permute-start(bf16[64,3712]{1,0:T(8,128)(2,1)S(1)} %shard_map.64.refs_0_), channel_id=1, source_target_pairs={{0,8},{8,12},{12,4},{4,0},{1,9},{9,13},{13,5},{5,1},{2,10},{10,14}... | collective-permute-start | bytes 1425416 | tf_op jit(solution)/shard_map/ppermute | solution.py:252
  5.8 13.0 %collective-permute-start = (bf16[64,3712]{1,0:T(8,128)(2,1)S(1)}, bf16[64,3712]{1,0:T(8,128)(2,1)S(1)}, u32[]{:S(2)}, u32[]{:S(2)}) collective-permute-start(bf16[64,3712]{1,0:T(8,128)(2,1)S(1)} %shard_map.64.refs_0_), channel_id=1, source_target_pairs={{0,2},{1,3},{2,0},{3,1},{4,6},{5,7},{6,4},{7,5},{8,10},{9,11},{10,... | collective-permute-start | bytes 1425416 | tf_op jit(solution)/shard_map/ppermute | solution.py:16
  18.8 12.2 %collective-permute-start.6 = (bf16[64,3712]{1,0:T(8,128)(2,1)S(1)}, bf16[64,3712]{1,0:T(8,128)(2,1)S(1)}, u32[]{:S(2)}, u32[]{:S(2)}) collective-permute-start(bf16[64,3712]{1,0:T(8,128)(2,1)S(1)} %compare_select_fusion.1.refs_0_), channel_id=1, source_target_pairs={{0,8},{8,12},{12,4},{4,0},{1,9},{9,13},{13,5},{5,1},{2,10},{10,14}... | collective-permute-start | bytes 1425416 | tf_op jit(solution)/shard_map/ppermute | solution.py:252
  20.5 11.9 %collective-permute-start.5 = (bf16[64,3712]{1,0:T(8,128)(2,1)S(1)}, bf16[64,3712]{1,0:T(8,128)(2,1)S(1)}, u32[]{:S(2)}, u32[]{:S(2)}) collective-permute-start(bf16[64,3712]{1,0:T(8,128)(2,1)S(1)} %compare_select_fusion.1.refs_0_), channel_id=1, source_target_pairs={{0,2},{1,3},{2,0},{3,1},{4,6},{5,7},{6,4},{7,5},{8,10},{9,11},{10,... | collective-permute-start | bytes 1425416 | tf_op jit(solution)/shard_map/ppermute | solution.py:16
  32.4 2.9 %copy-start = (bf16[64,3712]{1,0:T(8,128)(2,1)}, bf16[64,3712]{1,0:T(8,128)(2,1)S(1)}, u32[]{:S(2)}) copy-start(bf16[64,3712]{1,0:T(8,128)(2,1)S(1)} %collective-permute-done.5.refs_2_) | copy-start | bytes 1425412
  32.5 2.7 %copy-start.1 = (bf16[64,3712]{1,0:T(8,128)(2,1)}, bf16[64,3712]{1,0:T(8,128)(2,1)S(1)}, u32[]{:S(2)}) copy-start(bf16[64,3712]{1,0:T(8,128)(2,1)S(1)} %fusion.refs_1_) | copy-start | bytes 1425412
  32.5 12.7 %collective-permute-start.7 = (bf16[64,3712]{1,0:T(8,128)(2,1)S(1)}, bf16[64,3712]{1,0:T(8,128)(2,1)S(1)}, u32[]{:S(2)}, u32[]{:S(2)}) collective-permute-start(bf16[64,3712]{1,0:T(8,128)(2,1)S(1)} %fusion.refs_1_), channel_id=1, source_target_pairs={{0,8},{8,12},{12,4},{4,0},{1,9},{9,13},{13,5},{5,1},{2,10},{10,14}... | collective-permute-start | bytes 1425416 | tf_op jit(solution)/shard_map/ppermute | solution.py:252
  33.8 12.1 %collective-permute-start.9 = (bf16[64,3712]{1,0:T(8,128)(2,1)S(1)}, bf16[64,3712]{1,0:T(8,128)(2,1)S(1)}, u32[]{:S(2)}, u32[]{:S(2)}) collective-permute-start(bf16[64,3712]{1,0:T(8,128)(2,1)S(1)} %fusion.refs_1_), channel_id=1, source_target_pairs={{0,2},{1,3},{2,0},{3,1},{4,6},{5,7},{6,4},{7,5},{8,10},{9,11},{10,... | collective-permute-start | bytes 1425416 | tf_op jit(solution)/shard_map/ppermute | solution.py:16
  45.3 10.8 %collective-permute-start.8 = (bf16[64,3712]{1,0:T(8,128)(2,1)S(1)}, bf16[64,3712]{1,0:T(8,128)(2,1)S(1)}, u32[]{:S(2)}, u32[]{:S(2)}) collective-permute-start(bf16[64,3712]{1,0:T(8,128)(2,1)S(1)} %pad_maximum_fusion), channel_id=1, source_target_pairs={{0,2},{1,3},{2,0},{3,1},{4,6},{5,7},{6,4},{7,5},{8,10},{9,11},{10,... | collective-permute-start | bytes 1425416 | tf_op jit(solution)/shard_map/ppermute | solution.py:16
  46.0 11.4 %collective-permute-start.10 = (bf16[64,3712]{1,0:T(8,128)(2,1)S(1)}, bf16[64,3712]{1,0:T(8,128)(2,1)S(1)}, u32[]{:S(2)}, u32[]{:S(2)}) collective-permute-start(bf16[64,3712]{1,0:T(8,128)(2,1)S(1)} %pad_maximum_fusion.1), channel_id=1, source_target_pairs={{0,8},{8,12},{12,4},{4,0},{1,9},{9,13},{13,5},{5,1},{2,10},{10,14}... | collective-permute-start | bytes 1425416 | tf_op jit(solution)/shard_map/ppermute | solution.py:252
  56.1 11.7 %collective-permute-start.14 = (bf16[64,3584]{1,0:T(8,128)(2,1)S(1)}, bf16[64,3584]{1,0:T(8,128)(2,1)S(1)}, u32[]{:S(2)}, u32[]{:S(2)}) collective-permute-start(bf16[64,3584]{1,0:T(8,128)(2,1)S(1)} %pad_maximum_fusion.3), channel_id=1, source_target_pairs={{0,8},{8,12},{12,4},{4,0},{1,9},{9,13},{13,5},{5,1},{2,10},{10,14}... | collective-permute-start | bytes 1376264 | tf_op jit(solution)/shard_map/ppermute | solution.py:252
  57.5 10.4 %collective-permute-start.11 = (bf16[64,3584]{1,0:T(8,128)(2,1)S(1)}, bf16[64,3584]{1,0:T(8,128)(2,1)S(1)}, u32[]{:S(2)}, u32[]{:S(2)}) collective-permute-start(bf16[64,3584]{1,0:T(8,128)(2,1)S(1)} %pad_maximum_fusion.2), channel_id=1, source_target_pairs={{0,2},{1,3},{2,0},{3,1},{4,6},{5,7},{6,4},{7,5},{8,10},{9,11},{10,... | collective-permute-start | bytes 1376264 | tf_op jit(solution)/shard_map/ppermute | solution.py:16
  68.1 8.5 %collective-permute-start.15 = (bf16[64,3584]{1,0:T(8,128)(2,1)S(1)}, bf16[64,3584]{1,0:T(8,128)(2,1)S(1)}, u32[]{:S(2)}, u32[]{:S(2)}) collective-permute-start(bf16[64,3584]{1,0:T(8,128)(2,1)S(1)} %add_convert_fusion.2), channel_id=1, source_target_pairs={{0,8},{8,12},{12,4},{4,0},{1,9},{9,13},{13,5},{5,1},{2,10},{10,14}... | collective-permute-start | bytes 1376264 | tf_op jit(solution)/shard_map/ppermute | solution.py:252
  69.1 9.5 %collective-permute-start.12 = (bf16[64,3584]{1,0:T(8,128)(2,1)S(1)}, bf16[64,3584]{1,0:T(8,128)(2,1)S(1)}, u32[]{:S(2)}, u32[]{:S(2)}) collective-permute-start(bf16[64,3584]{1,0:T(8,128)(2,1)S(1)} %compare_select_fusion.3), channel_id=1, source_target_pairs={{0,2},{1,3},{2,0},{3,1},{4,6},{5,7},{6,4},{7,5},{8,10},{9,11},{10,... | collective-permute-start | bytes 1376264 | tf_op jit(solution)/shard_map/ppermute | solution.py:16
  78.8 8.6 %collective-permute-start.16 = (bf16[64,3584]{1,0:T(8,128)(2,1)S(1)}, bf16[64,3584]{1,0:T(8,128)(2,1)S(1)}, u32[]{:S(2)}, u32[]{:S(2)}) collective-permute-start(bf16[64,3584]{1,0:T(8,128)(2,1)S(1)} %add_convert_fusion.1), channel_id=1, source_target_pairs={{0,8},{8,12},{12,4},{4,0},{1,9},{9,13},{13,5},{5,1},{2,10},{10,14}... | collective-permute-start | bytes 1376264 | tf_op jit(solution)/shard_map/ppermute | solution.py:252
  80.0 8.6 %collective-permute-start.13 = (bf16[64,3584]{1,0:T(8,128)(2,1)S(1)}, bf16[64,3584]{1,0:T(8,128)(2,1)S(1)}, u32[]{:S(2)}, u32[]{:S(2)}) collective-permute-start(bf16[64,3584]{1,0:T(8,128)(2,1)S(1)} %compare_select_fusion.2), channel_id=1, source_target_pairs={{0,2},{1,3},{2,0},{3,1},{4,6},{5,7},{6,4},{7,5},{8,10},{9,11},{10,... | collective-permute-start | bytes 1376264 | tf_op jit(solution)/shard_map/ppermute | solution.py:16
